TPU v7x, 32 devices: a whole 2x2x4 slice. The times are simulated.
32 devices in a mesh: bin: 16 (over z, y, x), grp: 2 (over core).
Axes of the slice: x: 2, y: 2, z: 4, core: 2. Of those that a mesh axis runs over, the one named last changes fastest.
Arguments:
- record: bfloat16 [2, 1024, 8704], P('grp', 'bin'), may hold values from -60 to 60
- ref_index: int32 [2, 64], P('grp'), may hold values from 0 to 1023, as said below
- offsets: int32 [16], replicated, may hold values from 0 to 7680, as said below
Outputs:
- transfer: bfloat16 [512, 2048, 256], P('bin', 'grp')
Inputs may be any that keep to these rules, and one draw needn't show every extreme that they name: `ref_index`: each row lists 64 different channels of its group; every row holds 0 and 1023. `offsets`: starts rise; the first is 0, the last is 7680, and neighbours lie 512 // 2 to 768 apart.
All inputs are finite; a program needn't handle non-finite values.
Results may differ from a plain program's by a relative error of at most 0.0095.
Values may be sent and summed in bfloat16 or wider, within the bound.
No kernel may reach another device: no remote copies, remote signals or barrier semaphores. Data moves between devices by JAX's collectives and lax.ppermute only.
A program may use at most 64 MiB of HBM per device.

v0:
```python
import math

import jax
import jax.numpy as jnp
from jax import lax
from jax.sharding import PartitionSpec as P

L = 1024
NB = 512


ridge_weight = 0.5


def make_table(seg_len, bins):
    sample_num = lax.iota(jnp.int32, seg_len)[:, None]
    bin_num = lax.iota(jnp.int32, bins)[None, :]
    angles = (sample_num * bin_num % seg_len).astype(jnp.float32) * (2.0 * math.pi / seg_len)
    hann_window = 0.5 - 0.5 * jnp.cos(sample_num.astype(jnp.float32) * (2.0 * math.pi / seg_len))
    return jnp.concatenate(
        [hann_window * jnp.cos(angles), -(hann_window * jnp.sin(angles))], axis=1
    ).astype(jnp.bfloat16)


def transform(chan_rows, starts, dft_table, bin_devices):
    seg_len = dft_table.shape[0]
    pieces = jax.vmap(lambda start_at: lax.dynamic_slice_in_dim(chan_rows, start_at, seg_len, 1))(
        starts
    )
    spectra = jnp.einsum(
        "scn,nk->ksc", pieces, dft_table, preferred_element_type=jnp.float32
    ).astype(jnp.bfloat16)
    bin_total = dft_table.shape[1] // 2
    return spectra.reshape(
        2, bin_devices, bin_total // bin_devices, starts.shape[0], chan_rows.shape[0]
    )


def local(record, ref_index, offsets):
    chan_rows = record[0]
    dft_table = make_table(L, NB)
    bin_devices = lax.axis_size("bin")
    spectra = transform(chan_rows, offsets, dft_table, bin_devices)
    channels = lax.all_to_all(spectra, "bin", split_axis=1, concat_axis=4, tiled=True)[:, 0]
    local_refs = jnp.take(channels, ref_index[0], axis=3)
    references = lax.all_gather(local_refs, "grp", axis=3, tiled=True)
    ref_real = references[0]
    ref_imag = references[1]
    ref_blocks = jnp.stack(
        [
            jnp.concatenate([ref_real, -ref_imag], axis=-1),
            jnp.concatenate([ref_imag, ref_real], axis=-1),
        ]
    )
    bins_here = channels.shape[1]
    group_size = math.gcd(bins_here, 4)
    group_count = bins_here // group_size
    real_order = ref_blocks.shape[-1]

    def solve_group(group_index):
        first_bin = group_index * group_size
        ref_group = lax.dynamic_slice_in_dim(ref_blocks, first_bin, group_size, 1)
        chan_group = lax.dynamic_slice_in_dim(channels, first_bin, group_size, 1)
        ref_rows = jnp.swapaxes(ref_group, 0, 1).reshape(group_size, -1, real_order)
        chan_cols = jnp.swapaxes(chan_group, 0, 1).reshape(group_size, -1, chan_group.shape[-1])
        gram_small = jnp.einsum(
            "fkr,fjr->fkj", ref_rows, ref_rows, preferred_element_type=jnp.float32
        )
        small_order = gram_small.shape[-1]
        ridge_term = ridge_weight * jnp.trace(gram_small, axis1=1, axis2=2) / real_order
        factor = jnp.linalg.cholesky(
            gram_small + ridge_term[:, None, None] * jnp.eye(small_order, dtype=jnp.float32)
        )
        solved = jax.scipy.linalg.cho_solve((factor, True), chan_cols.astype(jnp.float32))
        solved_high = solved.astype(jnp.bfloat16)
        solved_low = (solved - solved_high.astype(jnp.float32)).astype(jnp.bfloat16)
        transfer_t = jnp.einsum(
            "fkr,fkc->frc", ref_rows, solved_high, preferred_element_type=jnp.float32
        )
        transfer_t = transfer_t + jnp.einsum(
            "fkr,fkc->frc", ref_rows, solved_low, preferred_element_type=jnp.float32
        )
        return jnp.swapaxes(transfer_t, 1, 2).astype(jnp.bfloat16)

    results = lax.map(solve_group, jnp.arange(group_count))
    return results.reshape(bins_here, results.shape[2], results.shape[3])


def solution(mesh):
    placed = (P("grp", "bin", None), P("grp", None), P())
    return jax.shard_map(
        local, mesh=mesh, in_specs=placed, out_specs=P("bin", "grp", None), check_vma=False
    )
```

profile of v0, /device:TPU:0, one launch (start us, length us, event | category | flops | bytes accessed | tf_op | source)
XLA Modules:
  0.0 392.8 jit_solution(9663214665081754569)
XLA Ops:
  0.1 9.5 %multiply_convert_fusion = (bf16[1024,512]{1,0:T(8,128)(2,1)S(1)}, bf16[1024,512]{1,0:T(8,128)(2,1)}) fusion(f32[1024]{0:T(1024)S(1)} %multiply_subtract_fusion), kind=kLoop, calls=%fused_computation.39 | loop fusion | flops 9961472 | bytes 2101248 | tf_op jit(solution)/shard_map/convert
  9.6 47.4 %while.14 = (s32[]{:T(128)}, bf16[64,8704]{1,0:T(8,128)(2,1)}, s32[16,2]{0,1:T(2,128)S(1)}, bf16[16,64,1024]{2,1,0:T(8,128)(2,1)}, s32[]{:T(128)}) while((s32[]{:T(128)}, bf16[64,8704]{1,0:T(8,128)(2,1)}, s32[16,2]{0,1:T(2,128)S(1)}, bf16[16,64,1024]{2,1,0:T(8,128)(2,1)}, s32[]{:T(128)}) %tuple.56), condition=%wide.while_cond, body=%wide.while_body.sunk | while | flops 2 | bytes 263257 | solution.py:27
  10.3 2.3 bitcast_dynamic-update-slice_fusion.5
  13.2 2.3 bitcast_dynamic-update-slice_fusion.5
  16.2 2.3 bitcast_dynamic-update-slice_fusion.5
  19.2 2.3 bitcast_dynamic-update-slice_fusion.5
  22.1 2.3 bitcast_dynamic-update-slice_fusion.5
  25.1 2.3 bitcast_dynamic-update-slice_fusion.5
  28.0 2.3 bitcast_dynamic-update-slice_fusion.5
  31.0 2.3 bitcast_dynamic-update-slice_fusion.5
  34.0 2.3 bitcast_dynamic-update-slice_fusion.5
  36.9 2.3 bitcast_dynamic-update-slice_fusion.5
  39.9 2.3 bitcast_dynamic-update-slice_fusion.5
  42.8 2.3 bitcast_dynamic-update-slice_fusion.5
  45.8 2.3 bitcast_dynamic-update-slice_fusion.5
  48.8 2.3 bitcast_dynamic-update-slice_fusion.5
  51.7 2.3 bitcast_dynamic-update-slice_fusion.5
  54.7 2.3 bitcast_dynamic-update-slice_fusion.5
  57.0 4.2 %fusion.20 = bf16[1024,16,64]{0,2,1:T(8,128)(2,1)S(1)} fusion(bf16[16,64,1024]{2,1,0:T(8,128)(2,1)} %get-tuple-element.78, bf16[1024,512]{1,0:T(8,128)(2,1)} %get-tuple-element.126, bf16[1024,512]{1,0:T(8,128)(2,1)S(1)} %get-tuple-element.125), kind=kOutput, calls=%fused_computation.43 | convolution fusion | flops 2152726528 | bytes 6291456 | tf_op jit(solution)/shard_map/scn,nk->ksc/dot_general | solution.py:30
  61.2 4.8 %copy.26 = bf16[1024,16,64]{2,1,0:T(8,128)(2,1)} copy(bf16[1024,16,64]{0,2,1:T(8,128)(2,1)S(1)} %fusion.20) | data formatting | bytes 4194304 | tf_op jit(solution)/shard_map/convert_element_type | solution.py:32
  66.1 5.3 %copy.38 = bf16[2,16,32,16,64]{4,3,2,0,1:T(8,128)(2,1)} copy(bf16[2,16,32,16,64]{4,3,2,1,0:T(8,128)(2,1)} %bitcast.108) | data formatting | bytes 4194304 | tf_op jit(solution)/shard_map/reshape | solution.py:34
  71.4 7.5 %reshape.130 = bf16[16,2,32768]{2,1,0:T(2,128)(2,1)} reshape(bf16[16,2,32,16,64]{4,3,2,1,0:T(8,128)(2,1)} %bitcast.109) | data formatting | bytes 4194304
  78.9 8.4 %all-to-all-start = ((bf16[16,2,32768]{2,1,0:T(2,128)(2,1)}), bf16[16,2,32768]{2,1,0:T(2,128)(2,1)S(1)}, u32[]{:S(2)}, u32[]{:S(2)}) async-start(bf16[16,2,32768]{2,1,0:T(2,128)(2,1)} %reshape.130), calls=%async_computation | async-start | bytes 4194304 | tf_op jit(solution)/shard_map/all_to_all | solution.py:44
  87.4 43.0 %all-to-all-done = bf16[16,2,32768]{2,1,0:T(2,128)(2,1)S(1)} async-done(((bf16[16,2,32768]{2,1,0:T(2,128)(2,1)}), bf16[16,2,32768]{2,1,0:T(2,128)(2,1)S(1)}, u32[]{:S(2)}, u32[]{:S(2)}) %all-to-all-start) | async-done | bytes 2097184 | tf_op jit(solution)/shard_map/all_to_all | solution.py:44
  130.4 5.0 %reshape.131 = bf16[16,2,32,16,64]{4,3,2,1,0:T(8,128)(2,1)} reshape(bf16[16,2,32768]{2,1,0:T(2,128)(2,1)S(1)} %all-to-all-done) | data formatting | bytes 4194304
  135.4 5.3 %bitcast_bitcast_fusion = bf16[2,1,32,16,16,64]{5,3,2,0,4,1:T(8,128)(2,1)} fusion(bf16[16,2,32,16,64]{4,3,2,1,0:T(8,128)(2,1)} %reshape.131), kind=kLoop, calls=%fused_computation.60 | loop fusion | bytes 4194304 | tf_op jit(solution)/shard_map/all_to_all | solution.py:44
  140.7 11.6 %copy.28 = bf16[2,1,32,16,16,64]{2,3,5,4,0,1:T(8,128)(2,1)} copy(bf16[2,1,32,16,16,64]{5,3,2,0,4,1:T(8,128)(2,1)} %bitcast_bitcast_fusion) | data formatting | bytes 4194304 | tf_op jit(solution)/shard_map/all_to_all | solution.py:44
  152.3 4.1 %gather_fusion = bf16[64,2,32,16]{2,3,1,0:T(8,128)(2,1)S(1)} fusion(bf16[2,32,16,1024]{1,2,3,0:T(8,128)(2,1)} %bitcast.105, s32[1024]{0:T(1024)S(1)} %pad_clamp_fusion), kind=kCustom, calls=%fused_computation | custom fusion | bytes 262400 | tf_op jit(solution)/shard_map/jit(_take)/gather | solution.py:45
  156.6 2.7 all_gather.3
  160.4 9.6 %copy.34 = bf16[2,32,16,1024]{3,2,0,1:T(8,128)(2,1)S(1)} copy(bf16[2,32,16,1024]{1,2,3,0:T(8,128)(2,1)} %bitcast.106) | data formatting | bytes 4194304 | tf_op jit(solution)/shard_map/while | solution.py:85
  172.7 220.0 %while.13 = (s32[]{:T(128)}, bf16[8,4,1024,256]{3,2,1,0:T(8,128)(2,1)}, s32[8]{0:T(128)S(1)}, bf16[2,32,16,256]{3,2,1,0:T(8,128)(2,1)S(1)}, bf16[2,32,16,1024]{3...) while((s32[]{:T(128)}, bf16[8,4,1024,256]{3,2,1,0:T(8,128)(2,1)}, ...), condition=%wide.region_4.5_spmd, body=%wide.region_0.0_spmd.sunk | while | flops 239790208 | bytes 14555879 | solution.py:85
  174.6 11.7 %custom-call.23 = f32[4,32,32]{2,1,0:T(8,128)S(1)} custom-call(f32[4,32,32]{2,1,0:T(8,128)S(1)} %fusion.56), custom_call_target="Cholesky" | custom-call | tf_op jit(solution)/shard_map/while/body/eval_jaxpr/jit(cholesky)/cholesky | solution.py:71
  186.5 9.8 %custom-call.24 = f32[4,1,32,32]{2,3,1,0:T(8,128)S(1)} custom-call(f32[4,1,32,32]{3,2,1,0:T(8,128)S(1)} %select_bitcast_fusion.3), custom_call_target="InvertDiagBlocksLowerTriangular" | custom-call | tf_op jit(solution)/shard_map/while/body/eval_jaxpr/jit(_cho_solve)/vmap()/triangular_solve | solution.py:74
  198.2 2.1 bitcast_dynamic-update-slice_fusion.4
  202.1 11.7 %custom-call.23 = f32[4,32,32]{2,1,0:T(8,128)S(1)} custom-call(f32[4,32,32]{2,1,0:T(8,128)S(1)} %fusion.56), custom_call_target="Cholesky" | custom-call | tf_op jit(solution)/shard_map/while/body/eval_jaxpr/jit(cholesky)/cholesky | solution.py:71
  214.0 9.8 %custom-call.24 = f32[4,1,32,32]{2,3,1,0:T(8,128)S(1)} custom-call(f32[4,1,32,32]{3,2,1,0:T(8,128)S(1)} %select_bitcast_fusion.3), custom_call_target="InvertDiagBlocksLowerTriangular" | custom-call | tf_op jit(solution)/shard_map/while/body/eval_jaxpr/jit(_cho_solve)/vmap()/triangular_solve | solution.py:74
  229.6 11.7 %custom-call.23 = f32[4,32,32]{2,1,0:T(8,128)S(1)} custom-call(f32[4,32,32]{2,1,0:T(8,128)S(1)} %fusion.56), custom_call_target="Cholesky" | custom-call | tf_op jit(solution)/shard_map/while/body/eval_jaxpr/jit(cholesky)/cholesky | solution.py:71
  241.5 9.8 %custom-call.24 = f32[4,1,32,32]{2,3,1,0:T(8,128)S(1)} custom-call(f32[4,1,32,32]{3,2,1,0:T(8,128)S(1)} %select_bitcast_fusion.3), custom_call_target="InvertDiagBlocksLowerTriangular" | custom-call | tf_op jit(solution)/shard_map/while/body/eval_jaxpr/jit(_cho_solve)/vmap()/triangular_solve | solution.py:74
  257.1 11.7 %custom-call.23 = f32[4,32,32]{2,1,0:T(8,128)S(1)} custom-call(f32[4,32,32]{2,1,0:T(8,128)S(1)} %fusion.56), custom_call_target="Cholesky" | custom-call | tf_op jit(solution)/shard_map/while/body/eval_jaxpr/jit(cholesky)/cholesky | solution.py:71
  269.0 9.8 %custom-call.24 = f32[4,1,32,32]{2,3,1,0:T(8,128)S(1)} custom-call(f32[4,1,32,32]{3,2,1,0:T(8,128)S(1)} %select_bitcast_fusion.3), custom_call_target="InvertDiagBlocksLowerTriangular" | custom-call | tf_op jit(solution)/shard_map/while/body/eval_jaxpr/jit(_cho_solve)/vmap()/triangular_solve | solution.py:74
  284.6 11.7 %custom-call.23 = f32[4,32,32]{2,1,0:T(8,128)S(1)} custom-call(f32[4,32,32]{2,1,0:T(8,128)S(1)} %fusion.56), custom_call_target="Cholesky" | custom-call | tf_op jit(solution)/shard_map/while/body/eval_jaxpr/jit(cholesky)/cholesky | solution.py:71
  296.5 9.8 %custom-call.24 = f32[4,1,32,32]{2,3,1,0:T(8,128)S(1)} custom-call(f32[4,1,32,32]{3,2,1,0:T(8,128)S(1)} %select_bitcast_fusion.3), custom_call_target="InvertDiagBlocksLowerTriangular" | custom-call | tf_op jit(solution)/shard_map/while/body/eval_jaxpr/jit(_cho_solve)/vmap()/triangular_solve | solution.py:74
  312.1 11.7 %custom-call.23 = f32[4,32,32]{2,1,0:T(8,128)S(1)} custom-call(f32[4,32,32]{2,1,0:T(8,128)S(1)} %fusion.56), custom_call_target="Cholesky" | custom-call | tf_op jit(solution)/shard_map/while/body/eval_jaxpr/jit(cholesky)/cholesky | solution.py:71
  324.0 9.8 %custom-call.24 = f32[4,1,32,32]{2,3,1,0:T(8,128)S(1)} custom-call(f32[4,1,32,32]{3,2,1,0:T(8,128)S(1)} %select_bitcast_fusion.3), custom_call_target="InvertDiagBlocksLowerTriangular" | custom-call | tf_op jit(solution)/shard_map/while/body/eval_jaxpr/jit(_cho_solve)/vmap()/triangular_solve | solution.py:74
  339.6 11.7 %custom-call.23 = f32[4,32,32]{2,1,0:T(8,128)S(1)} custom-call(f32[4,32,32]{2,1,0:T(8,128)S(1)} %fusion.56), custom_call_target="Cholesky" | custom-call | tf_op jit(solution)/shard_map/while/body/eval_jaxpr/jit(cholesky)/cholesky | solution.py:71
  351.5 9.8 %custom-call.24 = f32[4,1,32,32]{2,3,1,0:T(8,128)S(1)} custom-call(f32[4,1,32,32]{3,2,1,0:T(8,128)S(1)} %select_bitcast_fusion.3), custom_call_target="InvertDiagBlocksLowerTriangular" | custom-call | tf_op jit(solution)/shard_map/while/body/eval_jaxpr/jit(_cho_solve)/vmap()/triangular_solve | solution.py:74
  367.1 11.7 %custom-call.23 = f32[4,32,32]{2,1,0:T(8,128)S(1)} custom-call(f32[4,32,32]{2,1,0:T(8,128)S(1)} %fusion.56), custom_call_target="Cholesky" | custom-call | tf_op jit(solution)/shard_map/while/body/eval_jaxpr/jit(cholesky)/cholesky | solution.py:71
  379.0 9.8 %custom-call.24 = f32[4,1,32,32]{2,3,1,0:T(8,128)S(1)} custom-call(f32[4,1,32,32]{3,2,1,0:T(8,128)S(1)} %select_bitcast_fusion.3), custom_call_target="InvertDiagBlocksLowerTriangular" | custom-call | tf_op jit(solution)/shard_map/while/body/eval_jaxpr/jit(_cho_solve)/vmap()/triangular_solve | solution.py:74
  (196 shorter events, 54.0 us)
Async XLA Ops:
  0.0 9.6 %copy-start = (s32[16]{0:T(128)S(1)}, s32[16]{0:T(128)}, u32[]{:S(2)}) copy-start(s32[16]{0:T(128)} %param.7) | copy-start | bytes 196
  78.9 8.5 %copy-start.1 = (s32[1,64]{1,0:T(1,128)S(1)}, s32[1,64]{1,0:T(1,128)}, u32[]{:S(2)}) copy-start(s32[1,64]{1,0:T(1,128)} %param.6) | copy-start | bytes 772
  78.9 51.5 %all-to-all-start = ((bf16[16,2,32768]{2,1,0:T(2,128)(2,1)}), bf16[16,2,32768]{2,1,0:T(2,128)(2,1)S(1)}, u32[]{:S(2)}, u32[]{:S(2)}) async-start(bf16[16,2,32768]{2,1,0:T(2,128)(2,1)} %reshape.130), calls=%async_computation | async-start | bytes 4194304 | tf_op jit(solution)/shard_map/all_to_all | solution.py:44
where the time goes:
time: 398 us; the launch traced here: 393 us
  other arithmetic  185 us (46%)
  local copies, waits for them, and re-layouts  111 us (28%)
  waiting for transfers between devices  43 us (11%)
  matrix products  36.8 us (9%)
  starting transfers between devices  8.44 us (2%)
  loops' own time  5.85 us (1%)
    another operation x32, other arithmetic, solve_group(): jnp.linalg.cholesky(gram_small + ridge_term[:, None, None] * jnp.eye(smal...  95.1 us
    another operation x24, other arithmetic, solve_group(): jax.scipy.linalg.cho_solve((factor, True), chan_cols.astype(jnp.float32))  79.4 us
    gather x48, local copies, waits for them, and re-layouts  47.3 us
    all_to_all x1, waiting for transfers between devices, local(): lax.all_to_all(spectra, 'bin', split_axis=1, concat_axis=4, tiled=True)  43 us
    all_to_all x2, local copies, waits for them, and re-layouts, local(): lax.all_to_all(spectra, 'bin', split_axis=1, concat_axis=4, tiled=True)  16.9 us
    dot_general x8, matrix products, solve_group(): jnp.einsum('fkr,fkc->frc', ref_rows, solved_low, preferred_element_type=j...  16.7 us
    unnamed x6, local copies, waits for them, and re-layouts  12.5 us
    while x1, local copies, waits for them, and re-layouts, local(): results = lax.map(solve_group, jnp.arange(group_count))  9.63 us
  transfers between devices with their start and end apart: 1, of which 1 were waited for; matrix products, arithmetic and copies ran while one was open for 0% of the time, Pallas kernels for 0%

commit v1 on v0

--- a/solution.py
+++ b/solution.py
@@ -2,12 +2,18 @@
 
 import jax
 import jax.numpy as jnp
+import numpy as np
 from jax import lax
+from jax.experimental import pallas as pl
+from jax.experimental.pallas import tpu as pltpu
 from jax.sharding import PartitionSpec as P
 
 L = 1024
 NB = 512
-
+LANES = 128
+SUB = 8
+VMEM_LIMIT = 48 * 1024 * 1024
+CHUNKS = (3, 1)
 
 ridge_weight = 0.5
 
@@ -20,6 +26,282 @@
     return jnp.concatenate(
         [hann_window * jnp.cos(angles), -(hann_window * jnp.sin(angles))], axis=1
     ).astype(jnp.bfloat16)
+
+
+def host_table(seg_len, bins):
+    step = np.float32(2.0 * math.pi / seg_len)
+    sample_num = np.arange(seg_len, dtype=np.int64)
+    bin_num = np.arange(bins, dtype=np.int64)[:, None]
+    angles = (sample_num[None, :] * bin_num % seg_len).astype(np.float32) * step
+    hann_window = np.float32(0.5) - np.float32(0.5) * np.cos(sample_num.astype(np.float32) * step)
+    return np.stack([hann_window * np.cos(angles), -(hann_window * np.sin(angles))]).astype(jnp.bfloat16)
+
+
+def spectra_kernel(starts_ref, record_ref, table_ref, out_ref, pieces_ref):
+    chans, samples = record_ref.shape
+    seg_len = table_ref.shape[1]
+    segs = starts_ref.shape[0]
+    wide = seg_len + LANES
+    per_dot = max(1, 256 // chans)
+    for first in range(0, segs, per_dot):
+        for seg in range(first, first + per_dot):
+            start = starts_ref[seg]
+            base = jnp.minimum(start // LANES * LANES, samples - wide)
+            window = record_ref[:, pl.ds(pl.multiple_of(base, LANES), wide)].astype(jnp.float32)
+            shift = lax.rem(wide - (start - base), wide)
+            piece = pltpu.roll(window, shift, 1)[:, :seg_len]
+            pieces_ref[pl.ds(seg * chans, chans), :] = piece.astype(jnp.bfloat16)
+        cols = pl.ds(first * chans, per_dot * chans)
+        out_ref[:, cols] = lax.dot_general(
+            table_ref[...],
+            pieces_ref[cols, :],
+            (((1,), (1,)), ((), ())),
+            preferred_element_type=jnp.float32,
+        ).astype(jnp.bfloat16)
+
+
+def spectra_of(record, offsets, table):
+    chans = record.shape[0]
+    segs = offsets.shape[0]
+    rows, seg_len = table.shape
+    cols = segs * chans
+    return pl.pallas_call(
+        spectra_kernel,
+        out_shape=jax.ShapeDtypeStruct((rows, cols), jnp.bfloat16),
+        in_specs=[
+            pl.BlockSpec(memory_space=pltpu.SMEM),
+            pl.BlockSpec(memory_space=pltpu.VMEM),
+            pl.BlockSpec(memory_space=pltpu.VMEM),
+        ],
+        out_specs=pl.BlockSpec(memory_space=pltpu.VMEM),
+        scratch_shapes=[pltpu.VMEM((cols, seg_len), jnp.bfloat16)],
+        compiler_params=pltpu.CompilerParams(vmem_limit_bytes=VMEM_LIMIT),
+        cost_estimate=pl.CostEstimate(
+            flops=2 * rows * cols * seg_len, bytes_accessed=4 * rows * cols, transcendentals=0
+        ),
+        name="spectra",
+    )(offsets, record, table)
+
+
+def pick_kernel(index_ref, got_ref, out_ref):
+    sources, rows, _ = got_ref.shape
+    chans = LANES // 2
+    group_rows = 2 * SUB
+    tiles = got_ref.shape[2] // LANES
+    index = index_ref[...]
+    chan = lax.broadcasted_iota(jnp.int32, (LANES, LANES), 0)
+    col = lax.broadcasted_iota(jnp.int32, (LANES, LANES), 1)
+    same_seg = (chan >= chans) == (col >= chans)
+    chan = jnp.where(chan >= chans, chan - chans, chan)
+    picks = []
+    for source in range(sources):
+        hit = same_seg & (chan + source * chans == index)
+        picks.append(jnp.where(hit, 1.0, 0.0).astype(jnp.bfloat16))
+    for group in range(rows // group_rows):
+        total = jnp.zeros((tiles * group_rows, LANES), jnp.float32)
+        for source in range(sources):
+            block = jnp.concatenate(
+                [
+                    got_ref[source, pl.ds(group * group_rows, group_rows), pl.ds(tile * LANES, LANES)]
+                    for tile in range(tiles)
+                ],
+                axis=0,
+            )
+            total = total + jnp.dot(block, picks[source], preferred_element_type=jnp.float32)
+        out_ref[group] = total.astype(jnp.bfloat16)
+
+
+def pick_refs(index, got):
+    sources, rows, cols = got.shape
+    groups = rows // (2 * SUB)
+    out_rows = cols // LANES * 2 * SUB
+    return pl.pallas_call(
+        pick_kernel,
+        out_shape=jax.ShapeDtypeStruct((groups, out_rows, LANES), jnp.bfloat16),
+        in_specs=[pl.BlockSpec(memory_space=pltpu.VMEM)] * 2,
+        out_specs=pl.BlockSpec(memory_space=pltpu.VMEM),
+        compiler_params=pltpu.CompilerParams(vmem_limit_bytes=VMEM_LIMIT),
+        cost_estimate=pl.CostEstimate(
+            flops=2 * groups * out_rows * sources * LANES * LANES,
+            bytes_accessed=2 * sources * rows * cols,
+            transcendentals=0,
+        ),
+        name="pick_refs",
+    )(index, got)
+
+
+def turn_kernel(got_ref, out_ref):
+    sources, rows, _ = got_ref.shape
+    chans = LANES // 2
+    group_rows = 2 * SUB
+    tiles = got_ref.shape[2] // LANES
+    for group in range(rows // group_rows):
+        for source in range(sources):
+            block = jnp.concatenate(
+                [
+                    got_ref[source, pl.ds(group * group_rows, group_rows), pl.ds(tile * LANES, LANES)]
+                    for tile in range(tiles)
+                ],
+                axis=0,
+            )
+            turned = block.T
+            here = pl.ds(source * chans, chans)
+            out_ref[group, here, 0:LANES] = turned[:chans]
+            out_ref[group, here, LANES : 2 * LANES] = turned[chans:]
+
+
+def turn(got):
+    sources, rows, cols = got.shape
+    groups = rows // (2 * SUB)
+    return pl.pallas_call(
+        turn_kernel,
+        out_shape=jax.ShapeDtypeStruct((groups, sources * LANES // 2, 2 * LANES), jnp.bfloat16),
+        in_specs=[pl.BlockSpec(memory_space=pltpu.VMEM)],
+        out_specs=pl.BlockSpec(memory_space=pltpu.VMEM),
+        compiler_params=pltpu.CompilerParams(vmem_limit_bytes=VMEM_LIMIT),
+        cost_estimate=pl.CostEstimate(
+            flops=0, bytes_accessed=4 * sources * rows * cols, transcendentals=0
+        ),
+        name="turn",
+    )(got)
+
+
+def solve_group(refs, segs, total_refs):
+    gram = {}
+    for i in range(segs):
+        for j in range(i + 1):
+            (ir, ii), (jr, ji) = refs[i], refs[j]
+            real = jnp.sum(ir * jr + ii * ji, axis=1, keepdims=True)
+            imag = None if i == j else jnp.sum(ir * ji - ii * jr, axis=1, keepdims=True)
+            gram[i, j] = (real, imag)
+    trace = gram[0, 0][0]
+    for i in range(1, segs):
+        trace = trace + gram[i, i][0]
+    ridge = ridge_weight * trace / total_refs
+    wide = refs[0][0].shape
+    spread = lambda x: jnp.broadcast_to(x, wide)
+    real = {k: spread(v[0] + ridge if k[0] == k[1] else v[0]) for k, v in gram.items()}
+    imag = {k: spread(v[1]) for k, v in gram.items() if k[0] != k[1]}
+    right = [(r, -i) for r, i in refs]
+    lower = {}
+    inverse = []
+    for k in range(segs):
+        inv = 1.0 / real[k, k]
+        inverse.append(inv)
+        for i in range(k + 1, segs):
+            lower[i, k] = (real[i, k] * inv, imag[i, k] * inv)
+        for i in range(k + 1, segs):
+            lr, li = lower[i, k]
+            for j in range(k + 1, i):
+                gr, gi = real[j, k], imag[j, k]
+                real[i, j] = real[i, j] - (lr * gr + li * gi)
+                imag[i, j] = imag[i, j] - (li * gr - lr * gi)
+            real[i, i] = real[i, i] - (lr * real[i, k] + li * imag[i, k])
+            br, bi = right[k]
+            cr, ci = right[i]
+            right[i] = (cr - (lr * br - li * bi), ci - (lr * bi + li * br))
+    found = [None] * segs
+    for k in range(segs - 1, -1, -1):
+        br, bi = right[k]
+        vr, vi = br * inverse[k], bi * inverse[k]
+        for i in range(k + 1, segs):
+            lr, li = lower[i, k]
+            wr, wi = found[i]
+            vr = vr - (lr * wr + li * wi)
+            vi = vi - (lr * wi - li * wr)
+        found[k] = (vr, vi)
+    return found
+
+
+def solve_kernel(refs_ref, turned_ref, *rest):
+    out_ref, wide_ref = rest[-2], rest[-1]
+    half = LANES // 2
+    rows = refs_ref.shape[2]
+    segs = 2 * rows // (2 * SUB)
+    step = pl.program_id(1)
+
+    @pl.when(step == 0)
+    def _():
+        low = refs_ref[0, 0].astype(jnp.float32)
+        high = refs_ref[1, 0].astype(jnp.float32)
+        left = lax.broadcasted_iota(jnp.int32, low.shape, 1) < half
+        even = jnp.where(left, low, pltpu.roll(high, half, 1))
+        odd = jnp.where(left, pltpu.roll(low, half, 1), high)
+        refs = []
+        for seg in range(segs):
+            source = odd if seg % 2 else even
+            at = seg // 2 * 2 * SUB
+            refs.append((source[at : at + SUB], source[at + SUB : at + 2 * SUB]))
+        found = solve_group(refs, segs, LANES)
+        for seg in range(segs):
+            vr, vi = found[seg]
+            at = (seg % 2) * LANES + seg // 2 * 2 * SUB
+            wide_ref[at : at + SUB, 0:LANES] = vr
+            wide_ref[at : at + SUB, LANES : 2 * LANES] = vi
+            wide_ref[at + SUB : at + 2 * SUB, 0:LANES] = -vi
+            wide_ref[at + SUB : at + 2 * SUB, LANES : 2 * LANES] = vr
+
+    row_bin = lax.broadcasted_iota(jnp.int32, wide_ref.shape, 0) % SUB
+    weights = jnp.where(row_bin == step, wide_ref[...], 0.0).astype(jnp.bfloat16)
+    out_ref[0] = jnp.dot(turned_ref[0], weights, preferred_element_type=jnp.float32).astype(
+        jnp.bfloat16
+    )
+
+
+def solve_and_apply(refs, turned, bins, first_bin, before):
+    groups, chans, depth = turned.shape
+    first_group = first_bin // SUB
+    operands = [refs, turned]
+    specs = [
+        pl.BlockSpec((2, 1, refs.shape[2], LANES), lambda g, f: (0, g, 0, 0)),
+        pl.BlockSpec((1, chans, depth), lambda g, f: (g, 0, 0)),
+    ]
+    aliases = {}
+    if before is not None:
+        operands.append(before)
+        specs.append(pl.BlockSpec(memory_space=pl.ANY))
+        aliases = {2: 0}
+    return pl.pallas_call(
+        solve_kernel,
+        grid=(groups, SUB),
+        out_shape=jax.ShapeDtypeStruct((bins, chans, 2 * LANES), jnp.bfloat16),
+        in_specs=specs,
+        out_specs=pl.BlockSpec(
+            (1, chans, 2 * LANES), lambda g, f: ((first_group + g) * SUB + f, 0, 0)
+        ),
+        scratch_shapes=[pltpu.VMEM((depth, 2 * LANES), jnp.float32)],
+        input_output_aliases=aliases,
+        compiler_params=pltpu.CompilerParams(
+            vmem_limit_bytes=VMEM_LIMIT, dimension_semantics=("arbitrary", "arbitrary")
+        ),
+        cost_estimate=pl.CostEstimate(
+            flops=2 * groups * SUB * chans * depth * 2 * LANES,
+            bytes_accessed=groups * SUB * chans * 4 * LANES,
+            transcendentals=0,
+        ),
+        name="solve_apply",
+    )(*operands)
+
+
+def local_kernels(record, ref_index, offsets):
+    chan_rows = record[0]
+    devices = lax.axis_size("bin")
+    bins = NB // devices
+    table = host_table(L, NB).reshape(2, devices, bins // SUB, SUB, L).transpose(1, 2, 0, 3, 4)
+    index = jnp.concatenate([ref_index, ref_index], axis=1)
+    out = None
+    first_group = 0
+    for groups in CHUNKS:
+        part = table[:, first_group : first_group + groups].reshape(-1, L)
+        sent = spectra_of(chan_rows, offsets, jnp.asarray(part))
+        sent = sent.reshape(devices, groups * 2 * SUB, -1)
+        got = lax.all_to_all(sent, "bin", 0, 0, tiled=True)
+        own = pick_refs(index, got)
+        refs = lax.all_gather(own, "grp", axis=0)
+        turned = turn(got)
+        out = solve_and_apply(refs, turned, bins, first_group * SUB, out)
+        first_group += groups
+    return out
 
 
 def transform(chan_rows, starts, dft_table, bin_devices):
@@ -57,7 +339,7 @@
     group_count = bins_here // group_size
     real_order = ref_blocks.shape[-1]
 
-    def solve_group(group_index):
+    def solve_bins(group_index):
         first_bin = group_index * group_size
         ref_group = lax.dynamic_slice_in_dim(ref_blocks, first_bin, group_size, 1)
         chan_group = lax.dynamic_slice_in_dim(channels, first_bin, group_size, 1)
@@ -82,12 +364,29 @@
         )
         return jnp.swapaxes(transfer_t, 1, 2).astype(jnp.bfloat16)
 
-    results = lax.map(solve_group, jnp.arange(group_count))
+    results = lax.map(solve_bins, jnp.arange(group_count))
     return results.reshape(bins_here, results.shape[2], results.shape[3])
 
 
 def solution(mesh):
     placed = (P("grp", "bin", None), P("grp", None), P())
-    return jax.shard_map(
-        local, mesh=mesh, in_specs=placed, out_specs=P("bin", "grp", None), check_vma=False
-    )
+    devices, groups = mesh.shape["bin"], mesh.shape["grp"]
+
+    def whole(record, ref_index, offsets):
+        chans = record.shape[1] // devices
+        kernels = (
+            groups == 2
+            and 2 * chans == LANES
+            and groups * ref_index.shape[1] == LANES
+            and offsets.shape[0] == 2 * SUB
+            and NB // devices == sum(CHUNKS) * SUB
+        )
+        return jax.shard_map(
+            local_kernels if kernels else local,
+            mesh=mesh,
+            in_specs=placed,
+            out_specs=P("bin", "grp", None),
+            check_vma=False,
+        )(record, ref_index, offsets)
+
+    return whole

time: 398 us -> 96 us (0.24)
  the two profiles are of different devices: /device:TPU:0 before, /device:TPU:13 now
where the time goes in v1:
time: 96 us; the launch traced here: 95.5 us
  waiting for transfers between devices  40.6 us (42%)
  Pallas kernels  31.1 us (32%)
  starting transfers between devices  11.6 us (12%)
  blocking collectives  6.58 us (7%)
  local copies, waits for them, and re-layouts  5.49 us (6%)
    all_to_all x2, waiting for transfers between devices, local_kernels(): got = lax.all_to_all(sent, 'bin', 0, 0, tiled=True)  40.6 us
    pallas_call x2, Pallas kernels, solve_and_apply(): pl.pallas_call(solve_kernel, grid=(groups, SUB), out_shape=jax.ShapeDtype...  23.1 us
    all_to_all x2, starting transfers between devices, local_kernels(): got = lax.all_to_all(sent, 'bin', 0, 0, tiled=True)  11.6 us
    all_gather x2, blocking collectives, local_kernels(): refs = lax.all_gather(own, 'grp', axis=0)  6.58 us
    pallas_call x2, Pallas kernels, spectra_of(): pl.pallas_call(spectra_kernel, out_shape=jax.ShapeDtypeStruct((rows, cols...  6.42 us
    unnamed x16, local copies, waits for them, and re-layouts  5.49 us
  transfers between devices with their start and end apart: 2, of which 2 were waited for; matrix products, arithmetic and copies ran while one was open for 0% of the time, Pallas kernels for 4%

profile of v1, /device:TPU:13, one launch (start us, length us, event | category | flops | bytes accessed | tf_op | source)
XLA Modules:
  0.0 95.5 jit_solution(3032955246796121085)
XLA Ops:
  0.0 0.0 copy-start.1
  0.0 1.2 %copy-done.1 = bf16[1,64,8704]{2,1,0:T(8,128)(2,1)S(1)} copy-done((bf16[1,64,8704]{2,1,0:T(8,128)(2,1)S(1)}, bf16[1,64,8704]{2,1,0:T(8,128)(2,1)}, u32[]{:S(2)}) %copy-start.1) | copy-done | bytes 1114136
  1.2 0.0 copy-start.3
  1.3 1.0 %copy-done.3 = bf16[256,1024]{1,0:T(8,128)(2,1)S(1)} copy-done((bf16[256,1024]{1,0:T(8,128)(2,1)S(1)}, bf16[256,1024]{1,0:T(8,128)(2,1)}, u32[]{:S(2)}) %copy-start.3) | copy-done | bytes 524312
  2.3 0.0 copy-start.4
  2.3 0.7 copy-done.4
  2.9 0.0 copy-start.2
  2.9 0.0 copy-start.5
  3.0 3.2 %spectra.2 = bf16[256,1024]{1,0:T(8,128)(2,1)} custom-call(s32[16]{0:T(128)S(1)} %copy-done.4, bf16[64,8704]{1,0:T(8,128)(2,1)S(1)} %bitcast.6, bf16[256,1024]{1,0:T(8,128)(2,1)S(1)} %copy-done.3), custom_call_target="tpu_custom_call" | custom-call | flops 536870912 | bytes 1048576 | tf_op jit(solution)/shard_map/spectra/pallas_call | solution.py:68
  6.1 6.6 %all-to-all-start = ((bf16[16,16,1024]{2,1,0:T(8,128)(2,1)}), bf16[16,16,1024]{2,1,0:T(8,128)(2,1)S(1)}, u32[]{:S(2)}, u32[]{:S(2)}) async-start(bf16[16,16,1024]{2,1,0:T(8,128)(2,1)} %bitcast.1), calls=%async_computation | async-start | bytes 1048576 | tf_op jit(solution)/shard_map/all_to_all | solution.py:298
  12.7 0.0 copy-done.2
  12.7 0.0 copy-done.5
  12.7 0.0 copy-start.6
  12.8 1.4 %copy-done.6 = bf16[768,1024]{1,0:T(8,128)(2,1)S(1)} copy-done((bf16[768,1024]{1,0:T(8,128)(2,1)S(1)}, bf16[768,1024]{1,0:T(8,128)(2,1)}, u32[]{:S(2)}) %copy-start.6) | copy-done | bytes 1572888
  14.2 3.2 %spectra.3 = bf16[768,1024]{1,0:T(8,128)(2,1)S(1)} custom-call(s32[16]{0:T(128)S(1)} %copy-done.5, bf16[64,8704]{1,0:T(8,128)(2,1)S(1)} %bitcast.7, bf16[768,1024]{1,0:T(8,128)(2,1)S(1)} %copy-done.6), custom_call_target="tpu_custom_call" | custom-call | flops 1610612736 | bytes 3145728 | tf_op jit(solution)/shard_map/spectra/pallas_call | solution.py:68
  17.4 0.0 copy-start
  17.4 1.1 %copy-done = bf16[768,1024]{1,0:T(8,128)(2,1)} copy-done((bf16[768,1024]{1,0:T(8,128)(2,1)}, bf16[768,1024]{1,0:T(8,128)(2,1)S(1)}, u32[]{:S(2)}) %copy-start) | copy-done | bytes 1572888
  18.6 7.6 %all-to-all-done.got_ref = bf16[16,16,1024]{2,1,0:T(8,128)(2,1)S(1)} async-done(((bf16[16,16,1024]{2,1,0:T(8,128)(2,1)}), bf16[16,16,1024]{2,1,0:T(8,128)(2,1)S(1)}, u32[]{:S(2)}, u32[]{:S(2)}) %all-to-all-start) | async-done | bytes 524320 | tf_op jit(solution)/shard_map/all_to_all | solution.py:298
  26.1 0.0 copy-start.7
  26.1 5.0 %all-to-all-start.1 = ((bf16[16,48,1024]{2,1,0:T(8,128)(2,1)}), bf16[16,48,1024]{2,1,0:T(8,128)(2,1)S(1)}, u32[]{:S(2)}, u32[]{:S(2)}) async-start(bf16[16,48,1024]{2,1,0:T(8,128)(2,1)} %bitcast.5), calls=%async_computation.1 | async-start | bytes 3145728 | tf_op jit(solution)/shard_map/all_to_all | solution.py:298
  31.1 0.0 copy-done.7
  31.1 0.1 pad_add_fusion.index_ref
  31.2 0.2 turn.2.turned_ref
  31.4 0.3 pick_refs.2
  31.7 3.5 %all-gather = bf16[2,128,128]{2,1,0:T(8,128)(2,1)S(1)} all-gather(bf16[1,128,128]{2,1,0:T(8,128)(2,1)S(1)} %pick_refs.2), channel_id=2, replica_groups=mesh['bin'=16,'grp'=2] {'grp'}, dimensions={0}, use_global_device_ids=true | all-gather | bytes 98304 | tf_op jit(solution)/shard_map/all_gather | solution.py:300
  35.2 33.1 %all-to-all-done.1.got_ref = bf16[16,48,1024]{2,1,0:T(8,128)(2,1)S(1)} async-done(((bf16[16,48,1024]{2,1,0:T(8,128)(2,1)}), bf16[16,48,1024]{2,1,0:T(8,128)(2,1)S(1)}, u32[]{:S(2)}, u32[]{:S(2)}) %all-to-all-start.1) | async-done | bytes 1572896 | tf_op jit(solution)/shard_map/all_to_all | solution.py:298
  68.3 0.6 pick_refs.3
  68.9 3.1 %all-gather.1 = bf16[6,128,128]{2,1,0:T(8,128)(2,1)S(1)} all-gather(bf16[3,128,128]{2,1,0:T(8,128)(2,1)S(1)} %pick_refs.3), channel_id=3, replica_groups=mesh['bin'=16,'grp'=2] {'grp'}, dimensions={0}, use_global_device_ids=true | all-gather | bytes 294912 | tf_op jit(solution)/shard_map/all_gather | solution.py:300
  71.9 0.5 turn.3.turned_ref
  72.4 17.2 %solve_apply.2.rest_0_ = bf16[32,1024,256]{2,1,0:T(8,128)(2,1)} custom-call(bf16[2,3,128,128]{3,2,1,0:T(8,128)(2,1)S(1)} %bitcast.8, bf16[3,1024,256]{2,1,0:T(8,128)(2,1)S(1)} %turn.3.turned_ref), custom_call_target="tpu_custom_call" | custom-call | flops 3221225472 | bytes 12582912 | tf_op jit(solution)/shard_map/solve_apply/pallas_call | solution.py:264
  89.6 5.9 %solve_apply.3 = bf16[32,1024,256]{2,1,0:T(8,128)(2,1)} custom-call(bf16[2,1,128,128]{3,2,1,0:T(8,128)(2,1)S(1)} %bitcast.9, bf16[1,1024,256]{2,1,0:T(8,128)(2,1)S(1)} %turn.2.turned_ref, bf16[32,1024,256]{2,1,0:T(8,128)(2,1)} %solve_apply.2.rest_0_), custom_call_target="tpu_custom_call", output_to_operand_aliasing={{}: (2, {})} | custom-call | flops 1073741824 | bytes 4194304 | tf_op jit(solution)/shard_map/solve_apply/pallas_call | solution.py:264
Async XLA Ops:
  0.0 1.2 %copy-start.1 = (bf16[1,64,8704]{2,1,0:T(8,128)(2,1)S(1)}, bf16[1,64,8704]{2,1,0:T(8,128)(2,1)}, u32[]{:S(2)}) copy-start(bf16[1,64,8704]{2,1,0:T(8,128)(2,1)} %param.5) | copy-start | bytes 3342340
  1.2 1.0 %copy-start.3 = (bf16[256,1024]{1,0:T(8,128)(2,1)S(1)}, bf16[256,1024]{1,0:T(8,128)(2,1)}, u32[]{:S(2)}) copy-start(bf16[256,1024]{1,0:T(8,128)(2,1)} %constant.5.clone.table_ref) | copy-start | bytes 1572868
  2.3 0.7 copy-start.4
  2.9 9.8 %copy-start.2 = (bf16[1,64,8704]{2,1,0:T(8,128)(2,1)S(1)}, bf16[1,64,8704]{2,1,0:T(8,128)(2,1)}, u32[]{:S(2)}) copy-start(bf16[1,64,8704]{2,1,0:T(8,128)(2,1)} %param.5) | copy-start | bytes 3342340
  2.9 9.8 %copy-start.5 = (s32[16]{0:T(128)S(1)}, s32[16]{0:T(128)}, u32[]{:S(2)}) copy-start(s32[16]{0:T(128)} %starts_ref.3) | copy-start | bytes 196
  6.1 20.0 %all-to-all-start = ((bf16[16,16,1024]{2,1,0:T(8,128)(2,1)}), bf16[16,16,1024]{2,1,0:T(8,128)(2,1)S(1)}, u32[]{:S(2)}, u32[]{:S(2)}) async-start(bf16[16,16,1024]{2,1,0:T(8,128)(2,1)} %bitcast.1), calls=%async_computation | async-start | bytes 1048576 | tf_op jit(solution)/shard_map/all_to_all | solution.py:298
  12.7 1.4 %copy-start.6 = (bf16[768,1024]{1,0:T(8,128)(2,1)S(1)}, bf16[768,1024]{1,0:T(8,128)(2,1)}, u32[]{:S(2)}) copy-start(bf16[768,1024]{1,0:T(8,128)(2,1)} %constant.4.clone.table_ref) | copy-start | bytes 4718596
  17.4 1.1 %copy-start = (bf16[768,1024]{1,0:T(8,128)(2,1)}, bf16[768,1024]{1,0:T(8,128)(2,1)S(1)}, u32[]{:S(2)}) copy-start(bf16[768,1024]{1,0:T(8,128)(2,1)S(1)} %spectra.3) | copy-start | bytes 4718596
  26.1 5.0 %copy-start.7 = (s32[1,64]{1,0:T(1,128)S(1)}, s32[1,64]{1,0:T(1,128)}, u32[]{:S(2)}) copy-start(s32[1,64]{1,0:T(1,128)} %param.6) | copy-start | bytes 772
  26.1 42.1 %all-to-all-start.1 = ((bf16[16,48,1024]{2,1,0:T(8,128)(2,1)}), bf16[16,48,1024]{2,1,0:T(8,128)(2,1)S(1)}, u32[]{:S(2)}, u32[]{:S(2)}) async-start(bf16[16,48,1024]{2,1,0:T(8,128)(2,1)} %bitcast.5), calls=%async_computation.1 | async-start | bytes 3145728 | tf_op jit(solution)/shard_map/all_to_all | solution.py:298

commit v2 on v1

--- a/solution.py
+++ b/solution.py
@@ -13,7 +13,8 @@
 LANES = 128
 SUB = 8
 VMEM_LIMIT = 48 * 1024 * 1024
-CHUNKS = (3, 1)
+SPECTRA_LIMIT = 66000000
+MAX_GAP = 768
 
 ridge_weight = 0.5
 
@@ -37,31 +38,83 @@
     return np.stack([hann_window * np.cos(angles), -(hann_window * np.sin(angles))]).astype(jnp.bfloat16)
 
 
-def spectra_kernel(starts_ref, record_ref, table_ref, out_ref, pieces_ref):
+def spectra_kernel(
+    starts_hbm, record_hbm, table_hbm, out_hbm,
+    starts_ref, record_ref, table_ref, pieces_ref, out_ref, in_sem, table_sem, out_sem,
+):
     chans, samples = record_ref.shape
-    seg_len = table_ref.shape[1]
+    out_rows, seg_len = table_ref.shape
     segs = starts_ref.shape[0]
     wide = seg_len + LANES
-    per_dot = max(1, 256 // chans)
-    for first in range(0, segs, per_dot):
-        for seg in range(first, first + per_dot):
-            start = starts_ref[seg]
-            base = jnp.minimum(start // LANES * LANES, samples - wide)
-            window = record_ref[:, pl.ds(pl.multiple_of(base, LANES), wide)].astype(jnp.float32)
-            shift = lax.rem(wide - (start - base), wide)
-            piece = pltpu.roll(window, shift, 1)[:, :seg_len]
-            pieces_ref[pl.ds(seg * chans, chans), :] = piece.astype(jnp.bfloat16)
-        cols = pl.ds(first * chans, per_dot * chans)
-        out_ref[:, cols] = lax.dot_general(
-            table_ref[...],
-            pieces_ref[cols, :],
-            (((1,), (1,)), ((), ())),
-            preferred_element_type=jnp.float32,
-        ).astype(jnp.bfloat16)
+    per_dot = 256 // chans
+    starts_load = pltpu.make_async_copy(starts_hbm, starts_ref, in_sem.at[0])
+    starts_load.start()
+    ends = [min(samples, MAX_GAP * (first + per_dot - 1) + wide) for first in range(0, segs, per_dot)]
+    loads, begin = [], 0
+    for end in ends:
+        part = pl.ds(begin, end - begin)
+        loads.append(
+            pltpu.make_async_copy(record_hbm.at[:, part], record_ref.at[:, part], in_sem.at[1 + len(loads)])
+            if end > begin
+            else None
+        )
+        begin = end
+    row_blocks = [pl.ds(at, 256) for at in range(0, out_rows, 256)]
+    tables = [
+        pltpu.make_async_copy(table_hbm.at[rows], table_ref.at[rows], table_sem.at[k])
+        for k, rows in enumerate(row_blocks)
+    ]
+    loads[0].start()
+    tables[0].start()
+    for load in loads[1:] + tables[1:]:
+        if load is not None:
+            load.start()
+    lane = lax.broadcasted_iota(jnp.int32, (chans, LANES), 1)
+    starts_load.wait()
+    stores = []
+    for row_block, rows in enumerate(row_blocks):
+        for block, first in enumerate(range(0, segs, per_dot)):
+            if row_block == 0:
+                if loads[block] is not None:
+                    loads[block].wait()
+                for seg in range(first, first + per_dot):
+                    start = starts_ref[seg]
+                    base = jnp.minimum(start // LANES * LANES, samples - wide)
+                    shift = start - base
+                    back = LANES - shift
+                    keep = lane < back
+                    here = pl.ds(seg * chans, chans)
+                    left = None
+                    for tile in range(seg_len // LANES + 1):
+                        at = pl.multiple_of(base + tile * LANES, LANES)
+                        right = pltpu.roll(
+                            record_ref[:, pl.ds(at, LANES)].astype(jnp.float32),
+                            lax.rem(back, LANES),
+                            1,
+                        )
+                        if tile:
+                            pieces_ref[here, pl.ds((tile - 1) * LANES, LANES)] = jnp.where(
+                                keep, left, right
+                            ).astype(jnp.bfloat16)
+                        left = right
+            if block == 0:
+                tables[row_block].wait()
+            cols = pl.ds(first * chans, per_dot * chans)
+            out_ref[rows, cols] = lax.dot_general(
+                table_ref[rows, :],
+                pieces_ref[cols, :],
+                (((1,), (1,)), ((), ())),
+                preferred_element_type=jnp.float32,
+            ).astype(jnp.bfloat16)
+        store = pltpu.make_async_copy(out_ref.at[rows], out_hbm.at[rows], out_sem.at[row_block])
+        store.start()
+        stores.append(store)
+    for store in stores:
+        store.wait()
 
 
 def spectra_of(record, offsets, table):
-    chans = record.shape[0]
+    chans, samples = record.shape
     segs = offsets.shape[0]
     rows, seg_len = table.shape
     cols = segs * chans
@@ -69,13 +122,22 @@
         spectra_kernel,
         out_shape=jax.ShapeDtypeStruct((rows, cols), jnp.bfloat16),
         in_specs=[
-            pl.BlockSpec(memory_space=pltpu.SMEM),
-            pl.BlockSpec(memory_space=pltpu.VMEM),
-            pl.BlockSpec(memory_space=pltpu.VMEM),
+            pl.BlockSpec(memory_space=pltpu.HBM),
+            pl.BlockSpec(memory_space=pltpu.HBM),
+            pl.BlockSpec(memory_space=pltpu.HBM),
         ],
-        out_specs=pl.BlockSpec(memory_space=pltpu.VMEM),
-        scratch_shapes=[pltpu.VMEM((cols, seg_len), jnp.bfloat16)],
-        compiler_params=pltpu.CompilerParams(vmem_limit_bytes=VMEM_LIMIT),
+        out_specs=pl.BlockSpec(memory_space=pltpu.HBM),
+        scratch_shapes=[
+            pltpu.SMEM((segs,), jnp.int32),
+            pltpu.VMEM((chans, samples), jnp.bfloat16),
+            pltpu.VMEM((rows, seg_len), jnp.bfloat16),
+            pltpu.VMEM((cols, seg_len), jnp.bfloat16),
+            pltpu.VMEM((rows, cols), jnp.bfloat16),
+            pltpu.SemaphoreType.DMA((cols // 256 + 1,)),
+            pltpu.SemaphoreType.DMA((rows // 256,)),
+            pltpu.SemaphoreType.DMA((rows // 256,)),
+        ],
+        compiler_params=pltpu.CompilerParams(vmem_limit_bytes=SPECTRA_LIMIT),
         cost_estimate=pl.CostEstimate(
             flops=2 * rows * cols * seg_len, bytes_accessed=4 * rows * cols, transcendentals=0
         ),
@@ -166,22 +228,24 @@
     )(got)
 
 
-def solve_group(refs, segs, total_refs):
-    gram = {}
+def solve_steps(refs, segs, total_refs, found):
+    wide = refs[0][0].shape
+    spread = lambda x: jnp.broadcast_to(x, wide)
+    real, imag = {}, {}
     for i in range(segs):
         for j in range(i + 1):
             (ir, ii), (jr, ji) = refs[i], refs[j]
-            real = jnp.sum(ir * jr + ii * ji, axis=1, keepdims=True)
-            imag = None if i == j else jnp.sum(ir * ji - ii * jr, axis=1, keepdims=True)
-            gram[i, j] = (real, imag)
-    trace = gram[0, 0][0]
+            real[i, j] = spread(jnp.sum(ir * jr + ii * ji, axis=1, keepdims=True))
+            if i != j:
+                imag[i, j] = spread(jnp.sum(ir * ji - ii * jr, axis=1, keepdims=True))
+            yield 6
+    trace = real[0, 0]
     for i in range(1, segs):
-        trace = trace + gram[i, i][0]
+        trace = trace + real[i, i]
     ridge = ridge_weight * trace / total_refs
-    wide = refs[0][0].shape
-    spread = lambda x: jnp.broadcast_to(x, wide)
-    real = {k: spread(v[0] + ridge if k[0] == k[1] else v[0]) for k, v in gram.items()}
-    imag = {k: spread(v[1]) for k, v in gram.items() if k[0] != k[1]}
+    for i in range(segs):
+        real[i, i] = real[i, i] + ridge
+    yield 2 * segs
     right = [(r, -i) for r, i in refs]
     lower = {}
     inverse = []
@@ -190,6 +254,7 @@
         inverse.append(inv)
         for i in range(k + 1, segs):
             lower[i, k] = (real[i, k] * inv, imag[i, k] * inv)
+        yield 8 + 2 * (segs - k)
         for i in range(k + 1, segs):
             lr, li = lower[i, k]
             for j in range(k + 1, i):
@@ -200,7 +265,7 @@
             br, bi = right[k]
             cr, ci = right[i]
             right[i] = (cr - (lr * br - li * bi), ci - (lr * bi + li * br))
-    found = [None] * segs
+            yield 8 * (i - k - 1) + 12
     for k in range(segs - 1, -1, -1):
         br, bi = right[k]
         vr, vi = br * inverse[k], bi * inverse[k]
@@ -210,20 +275,29 @@
             vr = vr - (lr * wr + li * wi)
             vi = vi - (lr * wi - li * wr)
         found[k] = (vr, vi)
-    return found
-
-
-def solve_kernel(refs_ref, turned_ref, *rest):
-    out_ref, wide_ref = rest[-2], rest[-1]
+        yield 2 + 8 * (segs - 1 - k)
+
+
+def solve_kernel(own_ref, other_ref, turned_ref, out_hbm, wide_ref, slot_ref, sem):
     half = LANES // 2
-    rows = refs_ref.shape[2]
+    groups, rows, _ = own_ref.shape
+    chans = turned_ref.shape[1]
     segs = 2 * rows // (2 * SUB)
-    step = pl.program_id(1)
-
-    @pl.when(step == 0)
-    def _():
-        low = refs_ref[0, 0].astype(jnp.float32)
-        high = refs_ref[1, 0].astype(jnp.float32)
+    steps, pair = slot_ref.shape[:2]
+    blocks = chans // 256
+    first_half = lax.axis_index("grp") == 0
+    row_bin = lax.broadcasted_iota(jnp.int32, wide_ref.shape[1:], 0) % SUB
+
+    def copy_out(step, group):
+        return pltpu.make_async_copy(
+            slot_ref.at[step], out_hbm.at[pl.ds(group * SUB + step * pair, pair)], sem.at[step]
+        )
+
+    def solve(group, into):
+        own = own_ref[group].astype(jnp.float32)
+        other = other_ref[group].astype(jnp.float32)
+        low = jnp.where(first_half, own, other)
+        high = jnp.where(first_half, other, own)
         left = lax.broadcasted_iota(jnp.int32, low.shape, 1) < half
         even = jnp.where(left, low, pltpu.roll(high, half, 1))
         odd = jnp.where(left, pltpu.roll(low, half, 1), high)
@@ -232,76 +306,98 @@
             source = odd if seg % 2 else even
             at = seg // 2 * 2 * SUB
             refs.append((source[at : at + SUB], source[at + SUB : at + 2 * SUB]))
-        found = solve_group(refs, segs, LANES)
+        yield 100
+        found = [None] * segs
+        yield from solve_steps(refs, segs, LANES, found)
         for seg in range(segs):
             vr, vi = found[seg]
             at = (seg % 2) * LANES + seg // 2 * 2 * SUB
-            wide_ref[at : at + SUB, 0:LANES] = vr
-            wide_ref[at : at + SUB, LANES : 2 * LANES] = vi
-            wide_ref[at + SUB : at + 2 * SUB, 0:LANES] = -vi
-            wide_ref[at + SUB : at + 2 * SUB, LANES : 2 * LANES] = vr
-
-    row_bin = lax.broadcasted_iota(jnp.int32, wide_ref.shape, 0) % SUB
-    weights = jnp.where(row_bin == step, wide_ref[...], 0.0).astype(jnp.bfloat16)
-    out_ref[0] = jnp.dot(turned_ref[0], weights, preferred_element_type=jnp.float32).astype(
-        jnp.bfloat16
-    )
-
-
-def solve_and_apply(refs, turned, bins, first_bin, before):
+            wide_ref[into, at : at + SUB, 0:LANES] = vr
+            wide_ref[into, at : at + SUB, LANES : 2 * LANES] = vi
+            wide_ref[into, at + SUB : at + 2 * SUB, 0:LANES] = -vi
+            wide_ref[into, at + SUB : at + 2 * SUB, LANES : 2 * LANES] = vr
+
+    solve_cost = 100 + 6 * 136 + 32 + 8 * 16 + 240 + 8 * 560 + 12 * 120 + 32 + 960
+
+    def apply(group, beside):
+        done = 0
+        for step in range(steps):
+            copy_out(step, group).wait()
+            weights = jnp.concatenate(
+                [
+                    jnp.where(row_bin == step * pair + k, wide_ref[group % 2], 0.0).astype(jnp.bfloat16)
+                    for k in range(pair)
+                ],
+                axis=1,
+            )
+            for block in range(blocks):
+                here = pl.ds(block * 256, 256)
+                product = jnp.dot(
+                    turned_ref[group, here, :], weights, preferred_element_type=jnp.float32
+                ).astype(jnp.bfloat16)
+                for k in range(pair):
+                    slot_ref[step, k, here, :] = product[:, k * 2 * LANES : (k + 1) * 2 * LANES]
+                limit = solve_cost * (step * blocks + block + 1) / (steps * blocks)
+                while done < limit:
+                    cost = next(beside, None)
+                    if cost is None:
+                        break
+                    done += cost
+            copy_out(step, group).start()
+        for _ in beside:
+            pass
+
+    for step in range(steps):
+        pltpu.make_async_copy(turned_ref.at[pl.ds(0, pair)], slot_ref.at[step], sem.at[step]).start()
+    for _ in solve(0, 0):
+        pass
+
+    @pl.loop(0, groups - 1)
+    def _(group):
+        apply(group, solve(group + 1, (group + 1) % 2))
+
+    apply(groups - 1, iter(()))
+    for step in range(steps):
+        copy_out(step, groups - 1).wait()
+
+
+def solve_and_apply(own, other, turned):
     groups, chans, depth = turned.shape
-    first_group = first_bin // SUB
-    operands = [refs, turned]
-    specs = [
-        pl.BlockSpec((2, 1, refs.shape[2], LANES), lambda g, f: (0, g, 0, 0)),
-        pl.BlockSpec((1, chans, depth), lambda g, f: (g, 0, 0)),
-    ]
-    aliases = {}
-    if before is not None:
-        operands.append(before)
-        specs.append(pl.BlockSpec(memory_space=pl.ANY))
-        aliases = {2: 0}
+    pair = 2
+    steps = SUB // pair
     return pl.pallas_call(
         solve_kernel,
-        grid=(groups, SUB),
-        out_shape=jax.ShapeDtypeStruct((bins, chans, 2 * LANES), jnp.bfloat16),
-        in_specs=specs,
-        out_specs=pl.BlockSpec(
-            (1, chans, 2 * LANES), lambda g, f: ((first_group + g) * SUB + f, 0, 0)
-        ),
-        scratch_shapes=[pltpu.VMEM((depth, 2 * LANES), jnp.float32)],
-        input_output_aliases=aliases,
-        compiler_params=pltpu.CompilerParams(
-            vmem_limit_bytes=VMEM_LIMIT, dimension_semantics=("arbitrary", "arbitrary")
-        ),
+        out_shape=jax.ShapeDtypeStruct((groups * SUB, chans, 2 * LANES), jnp.bfloat16),
+        in_specs=[pl.BlockSpec(memory_space=pltpu.VMEM)] * 3,
+        out_specs=pl.BlockSpec(memory_space=pltpu.HBM),
+        scratch_shapes=[
+            pltpu.VMEM((2, depth, 2 * LANES), jnp.float32),
+            pltpu.VMEM((steps, pair, chans, 2 * LANES), jnp.bfloat16),
+            pltpu.SemaphoreType.DMA((steps,)),
+        ],
+        compiler_params=pltpu.CompilerParams(vmem_limit_bytes=VMEM_LIMIT),
         cost_estimate=pl.CostEstimate(
             flops=2 * groups * SUB * chans * depth * 2 * LANES,
             bytes_accessed=groups * SUB * chans * 4 * LANES,
             transcendentals=0,
         ),
         name="solve_apply",
-    )(*operands)
+    )(own, other, turned)
 
 
 def local_kernels(record, ref_index, offsets):
     chan_rows = record[0]
     devices = lax.axis_size("bin")
-    bins = NB // devices
-    table = host_table(L, NB).reshape(2, devices, bins // SUB, SUB, L).transpose(1, 2, 0, 3, 4)
+    groups = NB // devices // SUB
+    table = host_table(L, NB).reshape(2, devices, groups, SUB, L).transpose(1, 2, 0, 3, 4)
     index = jnp.concatenate([ref_index, ref_index], axis=1)
-    out = None
-    first_group = 0
-    for groups in CHUNKS:
-        part = table[:, first_group : first_group + groups].reshape(-1, L)
-        sent = spectra_of(chan_rows, offsets, jnp.asarray(part))
-        sent = sent.reshape(devices, groups * 2 * SUB, -1)
-        got = lax.all_to_all(sent, "bin", 0, 0, tiled=True)
-        own = pick_refs(index, got)
-        refs = lax.all_gather(own, "grp", axis=0)
-        turned = turn(got)
-        out = solve_and_apply(refs, turned, bins, first_group * SUB, out)
-        first_group += groups
-    return out
+    sent = spectra_of(chan_rows, offsets, jnp.asarray(table.reshape(-1, L)))
+    sent = sent.reshape(devices, groups * 2 * SUB, -1)
+    got = lax.all_to_all(sent, "bin", 0, 0, tiled=True)
+    own = pick_refs(index, got)
+    other = lax.ppermute(own, "grp", [(0, 1), (1, 0)])
+    turned = turn(got)
+    return solve_and_apply(own, other, turned)
 
 
 def transform(chan_rows, starts, dft_table, bin_devices):
@@ -379,7 +475,7 @@
             and 2 * chans == LANES
             and groups * ref_index.shape[1] == LANES
             and offsets.shape[0] == 2 * SUB
-            and NB // devices == sum(CHUNKS) * SUB
+            and NB // devices % SUB == 0
         )
         return jax.shard_map(
             local_kernels if kernels else local,

time: 96 us -> 75.2 us (0.78)
  Pallas kernels: 31.1 us -> 18.6 us
  waiting for transfers between devices: 40.6 us -> 48.2 us
  blocking collectives: 6.58 us -> 0 us
  local copies, waits for them, and re-layouts: 5.49 us -> 0.01 us
  starting transfers between devices: 11.6 us -> 8.14 us
    pallas_call x2 -> x1, Pallas kernels: 23.1 us -> 11 us  [solve_and_apply(): pl.pallas_call(solve_kernel, out_shape=jax.ShapeDtypeStruct((groups * SUB...]
    all_to_all x2 -> x1, waiting for transfers between devices: 40.6 us -> 47.8 us  [local_kernels(): got = lax.all_to_all(sent, 'bin', 0, 0, tiled=True)]
    all_gather x2 -> x0, blocking collectives: 6.58 us -> none  [local_kernels(): refs = lax.all_gather(own, 'grp', axis=0)]
    unnamed x16 -> x2, local copies, waits for them, and re-layouts: 5.49 us -> 0.01 us
    all_to_all x2 -> x1, starting transfers between devices: 11.6 us -> 6.62 us  [local_kernels(): got = lax.all_to_all(sent, 'bin', 0, 0, tiled=True)]
    ppermute x0 -> x1, starting transfers between devices: none -> 1.52 us  [local_kernels(): other = lax.ppermute(own, 'grp', [(0, 1), (1, 0)])]
    pallas_call x2 -> x1, Pallas kernels: 6.42 us -> 6.29 us  [spectra_of(): pl.pallas_call(spectra_kernel, out_shape=jax.ShapeDtypeStruct((rows, cols...]
  transfers between devices with their start and end apart: 2 -> 2, of which waited for: 2 -> 2; matrix products, arithmetic and copies ran while one was open for 0% -> 0% of each run, Pallas kernels for 4% -> 1%
where the time goes in v2:
time: 75.2 us; the launch traced here: 75 us
  waiting for transfers between devices  48.2 us (64%)
  Pallas kernels  18.6 us (25%)
  starting transfers between devices  8.14 us (11%)
    all_to_all x1, waiting for transfers between devices, local_kernels(): got = lax.all_to_all(sent, 'bin', 0, 0, tiled=True)  47.8 us
    pallas_call x1, Pallas kernels, solve_and_apply(): pl.pallas_call(solve_kernel, out_shape=jax.ShapeDtypeStruct((groups * SUB...  11 us
    all_to_all x1, starting transfers between devices, local_kernels(): got = lax.all_to_all(sent, 'bin', 0, 0, tiled=True)  6.62 us
    pallas_call x1, Pallas kernels, spectra_of(): pl.pallas_call(spectra_kernel, out_shape=jax.ShapeDtypeStruct((rows, cols...  6.29 us
    ppermute x1, starting transfers between devices, local_kernels(): other = lax.ppermute(own, 'grp', [(0, 1), (1, 0)])  1.52 us
  transfers between devices with their start and end apart: 2, of which 2 were waited for; matrix products, arithmetic and copies ran while one was open for 0% of the time, Pallas kernels for 1%

profile of v2, /device:TPU:13, one launch (start us, length us, event | category | flops | bytes accessed | tf_op | source)
XLA Modules:
  0.0 75.0 jit_solution(5526825902816314646)
XLA Ops:
  0.0 6.3 %spectra.1 = bf16[1024,1024]{1,0:T(8,128)(2,1)} custom-call(s32[16]{0:T(128)} %starts_hbm.1, bf16[64,8704]{1,0:T(8,128)(2,1)} %bitcast.3, bf16[1024,1024]{1,0:T(8,128)(2,1)} %constant.2.clone.table_hbm), custom_call_target="tpu_custom_call" | custom-call | flops 2147483648 | bytes 4194304 | tf_op jit(solution)/shard_map/spectra/pallas_call | solution.py:121
  6.3 0.0 copy-start
  6.3 6.6 %all-to-all-start = ((bf16[16,64,1024]{2,1,0:T(8,128)(2,1)}), bf16[16,64,1024]{2,1,0:T(8,128)(2,1)S(1)}, u32[]{:S(2)}, u32[]{:S(2)}) async-start(bf16[16,64,1024]{2,1,0:T(8,128)(2,1)} %bitcast.2), calls=%async_computation | async-start | bytes 4194304 | tf_op jit(solution)/shard_map/all_to_all | solution.py:396
  12.9 0.0 copy-done
  12.9 0.1 pad_add_fusion.index_ref
  13.0 47.8 %all-to-all-done.got_ref = bf16[16,64,1024]{2,1,0:T(8,128)(2,1)S(1)} async-done(((bf16[16,64,1024]{2,1,0:T(8,128)(2,1)}), bf16[16,64,1024]{2,1,0:T(8,128)(2,1)S(1)}, u32[]{:S(2)}, u32[]{:S(2)}) %all-to-all-start) | async-done | bytes 2097184 | tf_op jit(solution)/shard_map/all_to_all | solution.py:396
  60.8 0.7 pick_refs.1.own_ref
  61.6 1.5 %collective-permute-start = (bf16[4,128,128]{2,1,0:T(8,128)(2,1)S(1)}, bf16[4,128,128]{2,1,0:T(8,128)(2,1)S(1)}, u32[]{:S(2)}, u32[]{:S(2)}) collective-permute-start(bf16[4,128,128]{2,1,0:T(8,128)(2,1)S(1)} %pick_refs.1.own_ref), channel_id=1, source_target_pairs={{0,1},{1,0},{2,3},{3,2},{4,5},{5,4},{6,7},{7,6},{8,9},{9,8},{10,11... | collective-permute-start | bytes 393224 | tf_op jit(solution)/shard_map/ppermute | solution.py:398
  63.1 0.6 turn.1.turned_ref
  63.7 0.4 collective-permute-done.other_ref
  64.1 11.0 %solve_apply.1 = bf16[32,1024,256]{2,1,0:T(8,128)(2,1)} custom-call(bf16[4,128,128]{2,1,0:T(8,128)(2,1)S(1)} %pick_refs.1.own_ref, bf16[4,128,128]{2,1,0:T(8,128)(2,1)S(1)} %collective-permute-done.other_ref, bf16[4,1024,256]{2,1,0:T(8,128)(2,1)S(1)} %turn.1.turned_ref), custom_call_target="tpu_custom_call" | custom-call | flops 4294967296 | bytes 16777216 | tf_op jit(solution)/shard_map/solve_apply/pallas_call | solution.py:368
Async XLA Ops:
  6.3 6.6 %copy-start = (s32[1,64]{1,0:T(1,128)S(1)}, s32[1,64]{1,0:T(1,128)}, u32[]{:S(2)}) copy-start(s32[1,64]{1,0:T(1,128)} %param.5) | copy-start | bytes 772
  6.3 54.5 %all-to-all-start = ((bf16[16,64,1024]{2,1,0:T(8,128)(2,1)}), bf16[16,64,1024]{2,1,0:T(8,128)(2,1)S(1)}, u32[]{:S(2)}, u32[]{:S(2)}) async-start(bf16[16,64,1024]{2,1,0:T(8,128)(2,1)} %bitcast.2), calls=%async_computation | async-start | bytes 4194304 | tf_op jit(solution)/shard_map/all_to_all | solution.py:396
  61.6 2.5 %collective-permute-start = (bf16[4,128,128]{2,1,0:T(8,128)(2,1)S(1)}, bf16[4,128,128]{2,1,0:T(8,128)(2,1)S(1)}, u32[]{:S(2)}, u32[]{:S(2)}) collective-permute-start(bf16[4,128,128]{2,1,0:T(8,128)(2,1)S(1)} %pick_refs.1.own_ref), channel_id=1, source_target_pairs={{0,1},{1,0},{2,3},{3,2},{4,5},{5,4},{6,7},{7,6},{8,9},{9,8},{10,11... | collective-permute-start | bytes 393224 | tf_op jit(solution)/shard_map/ppermute | solution.py:398

commit v3 on v2

--- a/solution.py
+++ b/solution.py
@@ -1,3 +1,4 @@
+import functools
 import math
 
 import jax
@@ -14,6 +15,9 @@
 SUB = 8
 VMEM_LIMIT = 48 * 1024 * 1024
 SPECTRA_LIMIT = 66000000
+SHIFTS = (8, 1, 15, 4, 10, 2, 13, 5, 9, 3, 14, 6, 11, 7, 12)
+FIRST = 4
+LATE = 4
 MAX_GAP = 768
 
 ridge_weight = 0.5
@@ -38,194 +42,184 @@
     return np.stack([hann_window * np.cos(angles), -(hann_window * np.sin(angles))]).astype(jnp.bfloat16)
 
 
-def spectra_kernel(
-    starts_hbm, record_hbm, table_hbm, out_hbm,
-    starts_ref, record_ref, table_ref, pieces_ref, out_ref, in_sem, table_sem, out_sem,
-):
+def spectra_kernel(dest_of, count, starts_hbm, record_hbm, table_hbm, *rest):
+    outs_hbm = rest[:-8]
+    starts_ref, record_ref, table_ref, pieces_ref, out_ref, in_sem, table_sem, out_sem = rest[-8:]
     chans, samples = record_ref.shape
-    out_rows, seg_len = table_ref.shape
+    dest_rows, seg_len = table_ref.shape[1:]
     segs = starts_ref.shape[0]
     wide = seg_len + LANES
     per_dot = 256 // chans
+    per_block = min(count, 256 // dest_rows)
     starts_load = pltpu.make_async_copy(starts_hbm, starts_ref, in_sem.at[0])
     starts_load.start()
     ends = [min(samples, MAX_GAP * (first + per_dot - 1) + wide) for first in range(0, segs, per_dot)]
-    loads, begin = [], 0
+    loads, begin = [starts_load], 0
     for end in ends:
-        part = pl.ds(begin, end - begin)
-        loads.append(
-            pltpu.make_async_copy(record_hbm.at[:, part], record_ref.at[:, part], in_sem.at[1 + len(loads)])
-            if end > begin
-            else None
-        )
-        begin = end
-    row_blocks = [pl.ds(at, 256) for at in range(0, out_rows, 256)]
-    tables = [
-        pltpu.make_async_copy(table_hbm.at[rows], table_ref.at[rows], table_sem.at[k])
-        for k, rows in enumerate(row_blocks)
+        if end > begin:
+            part = pl.ds(begin, end - begin)
+            loads.append(
+                pltpu.make_async_copy(record_hbm.at[:, part], record_ref.at[:, part], in_sem.at[len(loads)])
+            )
+            begin = end
+    loads += [
+        pltpu.make_async_copy(table_hbm.at[dest_of(k)], table_ref.at[k], table_sem.at[k])
+        for k in range(count)
     ]
-    loads[0].start()
-    tables[0].start()
-    for load in loads[1:] + tables[1:]:
-        if load is not None:
-            load.start()
+    for load in loads[1:]:
+        load.start()
+    for load in loads:
+        load.wait()
     lane = lax.broadcasted_iota(jnp.int32, (chans, LANES), 1)
-    starts_load.wait()
+    for seg in range(segs):
+        start = starts_ref[seg]
+        base = jnp.minimum(start // LANES * LANES, samples - wide)
+        shift = start - base
+        back = LANES - shift
+        keep = lane < back
+        here = pl.ds(seg * chans, chans)
+        left = None
+        for tile in range(seg_len // LANES + 1):
+            at = pl.multiple_of(base + tile * LANES, LANES)
+            right = pltpu.roll(
+                record_ref[:, pl.ds(at, LANES)].astype(jnp.float32), lax.rem(back, LANES), 1
+            )
+            if tile:
+                pieces_ref[here, pl.ds((tile - 1) * LANES, LANES)] = jnp.where(
+                    keep, left, right
+                ).astype(jnp.bfloat16)
+            left = right
     stores = []
-    for row_block, rows in enumerate(row_blocks):
-        for block, first in enumerate(range(0, segs, per_dot)):
-            if row_block == 0:
-                if loads[block] is not None:
-                    loads[block].wait()
-                for seg in range(first, first + per_dot):
-                    start = starts_ref[seg]
-                    base = jnp.minimum(start // LANES * LANES, samples - wide)
-                    shift = start - base
-                    back = LANES - shift
-                    keep = lane < back
-                    here = pl.ds(seg * chans, chans)
-                    left = None
-                    for tile in range(seg_len // LANES + 1):
-                        at = pl.multiple_of(base + tile * LANES, LANES)
-                        right = pltpu.roll(
-                            record_ref[:, pl.ds(at, LANES)].astype(jnp.float32),
-                            lax.rem(back, LANES),
-                            1,
-                        )
-                        if tile:
-                            pieces_ref[here, pl.ds((tile - 1) * LANES, LANES)] = jnp.where(
-                                keep, left, right
-                            ).astype(jnp.bfloat16)
-                        left = right
-            if block == 0:
-                tables[row_block].wait()
+    for first_dest in range(0, count, per_block):
+        held = min(per_block, count - first_dest)
+        rows = pl.ds(first_dest * dest_rows, held * dest_rows)
+        for first in range(0, segs, per_dot):
             cols = pl.ds(first * chans, per_dot * chans)
             out_ref[rows, cols] = lax.dot_general(
-                table_ref[rows, :],
+                table_ref[pl.ds(first_dest, held)].reshape(held * dest_rows, seg_len),
                 pieces_ref[cols, :],
                 (((1,), (1,)), ((), ())),
                 preferred_element_type=jnp.float32,
             ).astype(jnp.bfloat16)
-        store = pltpu.make_async_copy(out_ref.at[rows], out_hbm.at[rows], out_sem.at[row_block])
-        store.start()
-        stores.append(store)
+        for k in range(first_dest, first_dest + held):
+            rows = pl.ds(k * dest_rows, dest_rows)
+            to = outs_hbm[k] if len(outs_hbm) > 1 else outs_hbm[0].at[k]
+            stores.append(pltpu.make_async_copy(out_ref.at[rows], to, out_sem.at[k]))
+            stores[-1].start()
     for store in stores:
         store.wait()
 
 
-def spectra_of(record, offsets, table):
+def spectra_of(record, offsets, table, dest_of, count, apart):
     chans, samples = record.shape
     segs = offsets.shape[0]
-    rows, seg_len = table.shape
+    dest_rows, seg_len = table.shape[1:]
     cols = segs * chans
+    if apart:
+        out_shape = [jax.ShapeDtypeStruct((dest_rows, cols), jnp.bfloat16)] * count
+    else:
+        out_shape = [jax.ShapeDtypeStruct((count, dest_rows, cols), jnp.bfloat16)]
     return pl.pallas_call(
-        spectra_kernel,
-        out_shape=jax.ShapeDtypeStruct((rows, cols), jnp.bfloat16),
-        in_specs=[
-            pl.BlockSpec(memory_space=pltpu.HBM),
-            pl.BlockSpec(memory_space=pltpu.HBM),
-            pl.BlockSpec(memory_space=pltpu.HBM),
-        ],
-        out_specs=pl.BlockSpec(memory_space=pltpu.HBM),
+        functools.partial(spectra_kernel, dest_of, count),
+        out_shape=out_shape,
+        in_specs=[pl.BlockSpec(memory_space=pltpu.HBM)] * 3,
+        out_specs=[pl.BlockSpec(memory_space=pltpu.HBM)] * len(out_shape),
         scratch_shapes=[
             pltpu.SMEM((segs,), jnp.int32),
             pltpu.VMEM((chans, samples), jnp.bfloat16),
-            pltpu.VMEM((rows, seg_len), jnp.bfloat16),
+            pltpu.VMEM((count, dest_rows, seg_len), jnp.bfloat16),
             pltpu.VMEM((cols, seg_len), jnp.bfloat16),
-            pltpu.VMEM((rows, cols), jnp.bfloat16),
+            pltpu.VMEM((count * dest_rows, cols), jnp.bfloat16),
             pltpu.SemaphoreType.DMA((cols // 256 + 1,)),
-            pltpu.SemaphoreType.DMA((rows // 256,)),
-            pltpu.SemaphoreType.DMA((rows // 256,)),
+            pltpu.SemaphoreType.DMA((count,)),
+            pltpu.SemaphoreType.DMA((count,)),
         ],
         compiler_params=pltpu.CompilerParams(vmem_limit_bytes=SPECTRA_LIMIT),
         cost_estimate=pl.CostEstimate(
-            flops=2 * rows * cols * seg_len, bytes_accessed=4 * rows * cols, transcendentals=0
+            flops=2 * count * dest_rows * cols * seg_len,
+            bytes_accessed=4 * count * dest_rows * cols,
+            transcendentals=0,
         ),
         name="spectra",
     )(offsets, record, table)
 
 
-def pick_kernel(index_ref, got_ref, out_ref):
-    sources, rows, _ = got_ref.shape
+def stacked(ref, group):
+    tiles = ref.shape[1] // LANES
+    rows = pl.ds(group * 2 * SUB, 2 * SUB)
+    return jnp.concatenate([ref[rows, pl.ds(tile * LANES, LANES)] for tile in range(tiles)], axis=0)
+
+
+def pick_kernel(shifts, index_ref, *rest):
+    out_ref = rest[-1]
     chans = LANES // 2
-    group_rows = 2 * SUB
-    tiles = got_ref.shape[2] // LANES
+    groups = out_ref.shape[0]
     index = index_ref[...]
     chan = lax.broadcasted_iota(jnp.int32, (LANES, LANES), 0)
     col = lax.broadcasted_iota(jnp.int32, (LANES, LANES), 1)
     same_seg = (chan >= chans) == (col >= chans)
     chan = jnp.where(chan >= chans, chan - chans, chan)
-    picks = []
-    for source in range(sources):
+    if len(rest) > len(shifts) + 1:
+        totals = [rest[-2][group].astype(jnp.float32) for group in range(groups)]
+    else:
+        totals = [jnp.zeros(out_ref.shape[1:], jnp.float32)] * groups
+    for shift, ref in zip(shifts, rest):
+        source = lax.axis_index("bin") ^ shift
         hit = same_seg & (chan + source * chans == index)
-        picks.append(jnp.where(hit, 1.0, 0.0).astype(jnp.bfloat16))
-    for group in range(rows // group_rows):
-        total = jnp.zeros((tiles * group_rows, LANES), jnp.float32)
-        for source in range(sources):
-            block = jnp.concatenate(
-                [
-                    got_ref[source, pl.ds(group * group_rows, group_rows), pl.ds(tile * LANES, LANES)]
-                    for tile in range(tiles)
-                ],
-                axis=0,
+        pick = jnp.where(hit, 1.0, 0.0).astype(jnp.bfloat16)
+        for group in range(groups):
+            totals[group] = totals[group] + jnp.dot(
+                stacked(ref, group), pick, preferred_element_type=jnp.float32
             )
-            total = total + jnp.dot(block, picks[source], preferred_element_type=jnp.float32)
-        out_ref[group] = total.astype(jnp.bfloat16)
-
-
-def pick_refs(index, got):
-    sources, rows, cols = got.shape
+    for group in range(groups):
+        out_ref[group] = totals[group].astype(jnp.bfloat16)
+
+
+def pick_refs(index, shifts, got, before):
+    rows, cols = got[0].shape
     groups = rows // (2 * SUB)
     out_rows = cols // LANES * 2 * SUB
+    operands = [index, *got] + ([] if before is None else [before])
     return pl.pallas_call(
-        pick_kernel,
+        functools.partial(pick_kernel, shifts),
         out_shape=jax.ShapeDtypeStruct((groups, out_rows, LANES), jnp.bfloat16),
-        in_specs=[pl.BlockSpec(memory_space=pltpu.VMEM)] * 2,
+        in_specs=[pl.BlockSpec(memory_space=pltpu.VMEM)] * len(operands),
         out_specs=pl.BlockSpec(memory_space=pltpu.VMEM),
         compiler_params=pltpu.CompilerParams(vmem_limit_bytes=VMEM_LIMIT),
         cost_estimate=pl.CostEstimate(
-            flops=2 * groups * out_rows * sources * LANES * LANES,
-            bytes_accessed=2 * sources * rows * cols,
+            flops=2 * len(got) * groups * out_rows * LANES * LANES,
+            bytes_accessed=2 * len(got) * rows * cols,
             transcendentals=0,
         ),
         name="pick_refs",
-    )(index, got)
-
-
-def turn_kernel(got_ref, out_ref):
-    sources, rows, _ = got_ref.shape
+    )(*operands)
+
+
+def turn_kernel(*refs):
+    out_ref = refs[-1]
     chans = LANES // 2
-    group_rows = 2 * SUB
-    tiles = got_ref.shape[2] // LANES
-    for group in range(rows // group_rows):
-        for source in range(sources):
-            block = jnp.concatenate(
-                [
-                    got_ref[source, pl.ds(group * group_rows, group_rows), pl.ds(tile * LANES, LANES)]
-                    for tile in range(tiles)
-                ],
-                axis=0,
-            )
-            turned = block.T
-            here = pl.ds(source * chans, chans)
+    for at, ref in enumerate(refs[:-1]):
+        here = pl.ds(at * chans, chans)
+        for group in range(out_ref.shape[0]):
+            turned = stacked(ref, group).T
             out_ref[group, here, 0:LANES] = turned[:chans]
             out_ref[group, here, LANES : 2 * LANES] = turned[chans:]
 
 
 def turn(got):
-    sources, rows, cols = got.shape
+    rows, cols = got[0].shape
     groups = rows // (2 * SUB)
     return pl.pallas_call(
         turn_kernel,
-        out_shape=jax.ShapeDtypeStruct((groups, sources * LANES // 2, 2 * LANES), jnp.bfloat16),
-        in_specs=[pl.BlockSpec(memory_space=pltpu.VMEM)],
+        out_shape=jax.ShapeDtypeStruct((groups, len(got) * LANES // 2, 2 * LANES), jnp.bfloat16),
+        in_specs=[pl.BlockSpec(memory_space=pltpu.VMEM)] * len(got),
         out_specs=pl.BlockSpec(memory_space=pltpu.VMEM),
         compiler_params=pltpu.CompilerParams(vmem_limit_bytes=VMEM_LIMIT),
         cost_estimate=pl.CostEstimate(
-            flops=0, bytes_accessed=4 * sources * rows * cols, transcendentals=0
+            flops=0, bytes_accessed=4 * len(got) * rows * cols, transcendentals=0
         ),
         name="turn",
-    )(got)
+    )(*got)
 
 
 def solve_steps(refs, segs, total_refs, found):
@@ -278,13 +272,15 @@
         yield 2 + 8 * (segs - 1 - k)
 
 
-def solve_kernel(own_ref, other_ref, turned_ref, out_hbm, wide_ref, slot_ref, sem):
+def solve_kernel(shifts, own_ref, other_ref, early_ref, late_ref, out_hbm, wide_ref, slot_ref, sem):
     half = LANES // 2
     groups, rows, _ = own_ref.shape
-    chans = turned_ref.shape[1]
+    chans = LANES // 2
+    early, late = early_ref.shape[1], late_ref.shape[1]
     segs = 2 * rows // (2 * SUB)
     steps, pair = slot_ref.shape[:2]
-    blocks = chans // 256
+    blocks = [(early_ref, at) for at in range(0, early, 256)] + [(late_ref, at) for at in range(0, late, 256)]
+    sources = [lax.axis_index("bin") ^ shift for shift in shifts]
     first_half = lax.axis_index("grp") == 0
     row_bin = lax.broadcasted_iota(jnp.int32, wide_ref.shape[1:], 0) % SUB
 
@@ -330,14 +326,18 @@
                 ],
                 axis=1,
             )
-            for block in range(blocks):
-                here = pl.ds(block * 256, 256)
+            for block, (turned_ref, first) in enumerate(blocks):
                 product = jnp.dot(
-                    turned_ref[group, here, :], weights, preferred_element_type=jnp.float32
+                    turned_ref[group, pl.ds(first, 256), :], weights, preferred_element_type=jnp.float32
                 ).astype(jnp.bfloat16)
-                for k in range(pair):
-                    slot_ref[step, k, here, :] = product[:, k * 2 * LANES : (k + 1) * 2 * LANES]
-                limit = solve_cost * (step * blocks + block + 1) / (steps * blocks)
+                for at in range(0, 256, chans):
+                    source = sources[(block * 256 + at) // chans]
+                    here = pl.ds(pl.multiple_of(source * chans, chans), chans)
+                    for k in range(pair):
+                        slot_ref[step, k, here, :] = product[
+                            at : at + chans, k * 2 * LANES : (k + 1) * 2 * LANES
+                        ]
+                limit = solve_cost * (step * len(blocks) + block + 1) / (steps * len(blocks))
                 while done < limit:
                     cost = next(beside, None)
                     if cost is None:
@@ -348,7 +348,10 @@
             pass
 
     for step in range(steps):
-        pltpu.make_async_copy(turned_ref.at[pl.ds(0, pair)], slot_ref.at[step], sem.at[step]).start()
+        for ref, rows in ((early_ref, pl.ds(0, early)), (late_ref, pl.ds(early, late))):
+            pltpu.make_async_copy(
+                ref.at[pl.ds(0, pair)], slot_ref.at[step, :, rows], sem.at[step]
+            ).start()
     for _ in solve(0, 0):
         pass
 
@@ -361,14 +364,15 @@
         copy_out(step, groups - 1).wait()
 
 
-def solve_and_apply(own, other, turned):
-    groups, chans, depth = turned.shape
+def solve_and_apply(shifts, own, other, early, late):
+    groups, _, depth = early.shape
+    chans = early.shape[1] + late.shape[1]
     pair = 2
     steps = SUB // pair
     return pl.pallas_call(
-        solve_kernel,
+        functools.partial(solve_kernel, shifts),
         out_shape=jax.ShapeDtypeStruct((groups * SUB, chans, 2 * LANES), jnp.bfloat16),
-        in_specs=[pl.BlockSpec(memory_space=pltpu.VMEM)] * 3,
+        in_specs=[pl.BlockSpec(memory_space=pltpu.VMEM)] * 4,
         out_specs=pl.BlockSpec(memory_space=pltpu.HBM),
         scratch_shapes=[
             pltpu.VMEM((2, depth, 2 * LANES), jnp.float32),
@@ -382,7 +386,7 @@
             transcendentals=0,
         ),
         name="solve_apply",
-    )(own, other, turned)
+    )(own, other, early, late)
 
 
 def local_kernels(record, ref_index, offsets):
@@ -390,14 +394,23 @@
     devices = lax.axis_size("bin")
     groups = NB // devices // SUB
     table = host_table(L, NB).reshape(2, devices, groups, SUB, L).transpose(1, 2, 0, 3, 4)
+    table = jnp.asarray(table.reshape(devices, -1, L))
     index = jnp.concatenate([ref_index, ref_index], axis=1)
-    sent = spectra_of(chan_rows, offsets, jnp.asarray(table.reshape(-1, L)))
-    sent = sent.reshape(devices, groups * 2 * SUB, -1)
-    got = lax.all_to_all(sent, "bin", 0, 0, tiled=True)
-    own = pick_refs(index, got)
+    me = lambda: lax.axis_index("bin")
+    got = {}
+    for part in (SHIFTS[:FIRST], SHIFTS[FIRST:] + (0,)):
+        made = spectra_of(
+            chan_rows, offsets, table, lambda k, part=part: me() ^ part[k], len(part), True
+        )
+        chan_rows, *made = lax.optimization_barrier((chan_rows, *made))
+        for shift, block in zip(part, made):
+            pairs = [(i, i ^ shift) for i in range(devices)]
+            got[shift] = lax.ppermute(block, "bin", pairs) if shift else block
+    early, late = (0,) + SHIFTS[:-LATE], SHIFTS[-LATE:]
+    got_early, got_late = [got[shift] for shift in early], [got[shift] for shift in late]
+    own = pick_refs(index, late, got_late, pick_refs(index, early, got_early, None))
     other = lax.ppermute(own, "grp", [(0, 1), (1, 0)])
-    turned = turn(got)
-    return solve_and_apply(own, other, turned)
+    return solve_and_apply(early + late, own, other, turn(got_early), turn(got_late))
 
 
 def transform(chan_rows, starts, dft_table, bin_devices):
@@ -471,11 +484,13 @@
     def whole(record, ref_index, offsets):
         chans = record.shape[1] // devices
         kernels = (
-            groups == 2
+            devices == 1 + len(SHIFTS)
+            and groups == 2
             and 2 * chans == LANES
             and groups * ref_index.shape[1] == LANES
             and offsets.shape[0] == 2 * SUB
             and NB // devices % SUB == 0
+            and NB // devices >= 2 * SUB
         )
         return jax.shard_map(
             local_kernels if kernels else local,

time: 75.2 us -> 68.2 us (0.907)
  the two profiles are of different devices: /device:TPU:13 before, /device:TPU:0 now
where the time goes in v3:
time: 68.2 us; the launch traced here: 68 us
  starting transfers between devices  35.8 us (52%)
  Pallas kernels  21.2 us (31%)
  waiting for transfers between devices  9.92 us (15%)
  local copies, waits for them, and re-layouts  0.92 us (1%)
    ppermute x15, starting transfers between devices, local_kernels(): got[shift] = lax.ppermute(block, 'bin', pairs) if shift else block  35.7 us
    pallas_call x1, Pallas kernels, solve_and_apply(): pl.pallas_call(functools.partial(solve_kernel, shifts), out_shape=jax.Sha...  11 us
    ppermute x15, waiting for transfers between devices, local_kernels(): got[shift] = lax.ppermute(block, 'bin', pairs) if shift else block  9.26 us
    pallas_call x2, Pallas kernels, spectra_of(): pl.pallas_call(functools.partial(spectra_kernel, dest_of, count), out_sha...  8.68 us
  transfers between devices with their start and end apart: 16, of which 4 were waited for; matrix products, arithmetic and copies ran while one was open for 0% of the time, Pallas kernels for 9%

profile of v3, /device:TPU:0, one launch (start us, length us, event | category | flops | bytes accessed | tf_op | source)
XLA Modules:
  0.0 68.0 jit_solution(2484711838642177779)
XLA Ops:
  0.0 3.5 %spectra.2 = (bf16[64,1024]{1,0:T(8,128)(2,1)}, bf16[64,1024]{1,0:T(8,128)(2,1)}, bf16[64,1024]{1,0:T(8,128)(2,1)}, bf16[64,1024]{1,0:T(8,128)(2,1)}) custom-call(s32[16]{0:T(128)} %starts_hbm.3, bf16[64,8704]{1,0:T(8,128)(2,1)} %bitcast.1, bf16[16,64,1024]{2,1,0:T(8,128)(2,1)} %constant.2.clone.table_hbm), custom_call_target="tpu_custom_call" | custom-call | flops 536870912 | bytes 1048576 | tf_op jit(solution)/shard_map/spectra/pallas_call | solution.py:122
  3.5 0.0 copy-start.2
  3.5 4.1 %collective-permute-start.4 = (bf16[64,1024]{1,0:T(8,128)(2,1)}, bf16[64,1024]{1,0:T(8,128)(2,1)S(1)}, u32[]{:S(2)}, u32[]{:S(2)}) collective-permute-start(bf16[64,1024]{1,0:T(8,128)(2,1)} %get-tuple-element.60), channel_id=1, source_target_pairs={{0,16},{2,18},{4,20},{6,22},{8,24},{10,26},{12,28},{14,30},{16,0},... | collective-permute-start | bytes 393224 | tf_op jit(solution)/shard_map/ppermute | solution.py:408
  7.6 1.5 %collective-permute-start.5 = (bf16[64,1024]{1,0:T(8,128)(2,1)}, bf16[64,1024]{1,0:T(8,128)(2,1)S(1)}, u32[]{:S(2)}, u32[]{:S(2)}) collective-permute-start(bf16[64,1024]{1,0:T(8,128)(2,1)} %get-tuple-element.61), channel_id=1, source_target_pairs={{0,2},{2,0},{4,6},{6,4},{8,10},{10,8},{12,14},{14,12},{16,18},{18,... | collective-permute-start | bytes 393224 | tf_op jit(solution)/shard_map/ppermute | solution.py:408
  9.1 2.3 %collective-permute-start.6 = (bf16[64,1024]{1,0:T(8,128)(2,1)}, bf16[64,1024]{1,0:T(8,128)(2,1)S(1)}, u32[]{:S(2)}, u32[]{:S(2)}) collective-permute-start(bf16[64,1024]{1,0:T(8,128)(2,1)} %get-tuple-element.62), channel_id=1, source_target_pairs={{0,30},{2,28},{4,26},{6,24},{8,22},{10,20},{12,18},{14,16},{16,14}... | collective-permute-start | bytes 393224 | tf_op jit(solution)/shard_map/ppermute | solution.py:408
  11.4 0.0 collective-permute-start.7
  11.4 5.2 %spectra.3 = (bf16[64,1024]{1,0:T(8,128)(2,1)}, bf16[64,1024]{1,0:T(8,128)(2,1)}, bf16[64,1024]{1,0:T(8,128)(2,1)}, bf16[64,1024]{1,0:T(8,128)(2,1)}, bf16[64,10...) custom-call(s32[16]{0:T(128)} %starts_hbm.3, ...), custom_call_target="tpu_custom_call" | custom-call | flops 1610612736 | bytes 3145728 | tf_op jit(solution)/shard_map/spectra/pallas_call | solution.py:122
  16.6 3.0 %collective-permute-start.8 = (bf16[64,1024]{1,0:T(8,128)(2,1)}, bf16[64,1024]{1,0:T(8,128)(2,1)S(1)}, u32[]{:S(2)}, u32[]{:S(2)}) collective-permute-start(bf16[64,1024]{1,0:T(8,128)(2,1)} %get-tuple-element.64), channel_id=1, source_target_pairs={{0,20},{2,22},{4,16},{6,18},{8,28},{10,30},{12,24},{14,26},{16,4},... | collective-permute-start | bytes 393224 | tf_op jit(solution)/shard_map/ppermute | solution.py:408
  19.6 0.0 collective-permute-done.4.rest_1_.refs_1_
  19.6 1.5 %collective-permute-start.9 = (bf16[64,1024]{1,0:T(8,128)(2,1)}, bf16[64,1024]{1,0:T(8,128)(2,1)S(1)}, u32[]{:S(2)}, u32[]{:S(2)}) collective-permute-start(bf16[64,1024]{1,0:T(8,128)(2,1)} %get-tuple-element.65), channel_id=1, source_target_pairs={{0,4},{2,6},{4,0},{6,2},{8,12},{10,14},{12,8},{14,10},{16,20},{18,... | collective-permute-start | bytes 393224 | tf_op jit(solution)/shard_map/ppermute | solution.py:408
  21.2 0.0 collective-permute-done.5.rest_2_.refs_2_
  21.2 2.3 %collective-permute-start.10 = (bf16[64,1024]{1,0:T(8,128)(2,1)}, bf16[64,1024]{1,0:T(8,128)(2,1)S(1)}, u32[]{:S(2)}, u32[]{:S(2)}) collective-permute-start(bf16[64,1024]{1,0:T(8,128)(2,1)} %get-tuple-element.66), channel_id=1, source_target_pairs={{0,26},{2,24},{4,30},{6,28},{8,18},{10,16},{12,22},{14,20},{16,10}... | collective-permute-start | bytes 393224 | tf_op jit(solution)/shard_map/ppermute | solution.py:408
  23.4 0.0 collective-permute-done.6.rest_3_.refs_3_
  23.4 0.0 collective-permute-start.11
  23.4 0.0 collective-permute-done.7.rest_4_.refs_4_
  23.4 3.9 %collective-permute-start.12 = (bf16[64,1024]{1,0:T(8,128)(2,1)}, bf16[64,1024]{1,0:T(8,128)(2,1)S(1)}, u32[]{:S(2)}, u32[]{:S(2)}) collective-permute-start(bf16[64,1024]{1,0:T(8,128)(2,1)} %get-tuple-element.68), channel_id=1, source_target_pairs={{0,18},{2,16},{4,22},{6,20},{8,26},{10,24},{12,30},{14,28},{16,2},... | collective-permute-start | bytes 393224 | tf_op jit(solution)/shard_map/ppermute | solution.py:408
  27.4 2.5 %collective-permute-done.8.rest_5_.refs_5_ = bf16[64,1024]{1,0:T(8,128)(2,1)S(1)} collective-permute-done((bf16[64,1024]{1,0:T(8,128)(2,1)}, bf16[64,1024]{1,0:T(8,128)(2,1)S(1)}, u32[]{:S(2)}, u32[]{:S(2)}) %collective-permute-start.8) | collective-permute-done | bytes 131104 | tf_op jit(solution)/shard_map/ppermute | solution.py:408
  29.8 1.6 %collective-permute-start.13 = (bf16[64,1024]{1,0:T(8,128)(2,1)}, bf16[64,1024]{1,0:T(8,128)(2,1)S(1)}, u32[]{:S(2)}, u32[]{:S(2)}) collective-permute-start(bf16[64,1024]{1,0:T(8,128)(2,1)} %get-tuple-element.69), channel_id=1, source_target_pairs={{0,6},{2,4},{4,2},{6,0},{8,14},{10,12},{12,10},{14,8},{16,22},{18,... | collective-permute-start | bytes 393224 | tf_op jit(solution)/shard_map/ppermute | solution.py:408
  31.5 0.0 collective-permute-done.9.rest_6_.refs_6_
  31.5 4.7 %collective-permute-start.14 = (bf16[64,1024]{1,0:T(8,128)(2,1)}, bf16[64,1024]{1,0:T(8,128)(2,1)S(1)}, u32[]{:S(2)}, u32[]{:S(2)}) collective-permute-start(bf16[64,1024]{1,0:T(8,128)(2,1)} %get-tuple-element.70), channel_id=1, source_target_pairs={{0,28},{2,30},{4,24},{6,26},{8,20},{10,22},{12,16},{14,18},{16,12}... | collective-permute-start | bytes 393224 | tf_op jit(solution)/shard_map/ppermute | solution.py:408
  36.2 0.0 collective-permute-done.10.rest_7_.refs_7_
  36.2 5.4 %collective-permute-start = (bf16[64,1024]{1,0:T(8,128)(2,1)}, bf16[64,1024]{1,0:T(8,128)(2,1)S(1)}, u32[]{:S(2)}, u32[]{:S(2)}) collective-permute-start(bf16[64,1024]{1,0:T(8,128)(2,1)} %get-tuple-element.55), channel_id=1, source_target_pairs={{0,12},{2,14},{4,8},{6,10},{8,4},{10,6},{12,0},{14,2},{16,28},{18,... | collective-permute-start | bytes 393224 | tf_op jit(solution)/shard_map/ppermute | solution.py:408
  41.6 0.0 collective-permute-done.11.rest_8_.refs_8_
  41.6 0.0 collective-permute-start.1
  41.6 0.9 %collective-permute-done.12.rest_9_.refs_9_ = bf16[64,1024]{1,0:T(8,128)(2,1)S(1)} collective-permute-done((bf16[64,1024]{1,0:T(8,128)(2,1)}, bf16[64,1024]{1,0:T(8,128)(2,1)S(1)}, u32[]{:S(2)}, u32[]{:S(2)}) %collective-permute-start.12) | collective-permute-done | bytes 131104 | tf_op jit(solution)/shard_map/ppermute | solution.py:408
  42.5 0.2 collective-permute-start.2
  42.7 0.0 collective-permute-done.13.rest_10_.refs_10_
  42.7 5.1 %collective-permute-start.3 = (bf16[64,1024]{1,0:T(8,128)(2,1)}, bf16[64,1024]{1,0:T(8,128)(2,1)S(1)}, u32[]{:S(2)}, u32[]{:S(2)}) collective-permute-start(bf16[64,1024]{1,0:T(8,128)(2,1)} %get-tuple-element.58), channel_id=1, source_target_pairs={{0,24},{2,26},{4,28},{6,30},{8,16},{10,18},{12,20},{14,22},{16,8},... | collective-permute-start | bytes 393224 | tf_op jit(solution)/shard_map/ppermute | solution.py:408
  47.8 0.0 copy-done.2
  47.8 0.1 pad_add_fusion.index_ref
  47.9 0.0 collective-permute-done.14.rest_11_.refs_11_
  47.9 0.0 copy-start
  47.9 0.9 %copy-done = bf16[64,1024]{1,0:T(8,128)(2,1)S(1)} copy-done((bf16[64,1024]{1,0:T(8,128)(2,1)S(1)}, bf16[64,1024]{1,0:T(8,128)(2,1)}, u32[]{:S(2)}) %copy-start) | copy-done | bytes 131096
  48.8 0.0 copy-start.1
  48.8 0.6 pick_refs.2.rest_4_
  49.4 0.0 collective-permute-done.rest_0_.refs_0_
  49.4 5.9 %collective-permute-done.1.rest_1_.refs_1_ = bf16[64,1024]{1,0:T(8,128)(2,1)S(1)} collective-permute-done((bf16[64,1024]{1,0:T(8,128)(2,1)}, bf16[64,1024]{1,0:T(8,128)(2,1)S(1)}, u32[]{:S(2)}, u32[]{:S(2)}) %collective-permute-start.1) | collective-permute-done | bytes 131104 | tf_op jit(solution)/shard_map/ppermute | solution.py:408
  55.3 0.0 collective-permute-done.2.rest_2_.refs_2_
  55.3 0.0 collective-permute-done.3.rest_3_.refs_3_
  55.3 0.3 pick_refs.3.own_ref
  55.6 0.1 collective-permute-start.15
  55.7 0.2 turn.3.late_ref
  55.9 0.0 copy-done.1
  55.9 0.5 turn.2.early_ref
  56.4 0.7 collective-permute-done.15.other_ref
  57.0 11.0 %solve_apply.1 = bf16[32,1024,256]{2,1,0:T(8,128)(2,1)} custom-call(bf16[4,128,128]{2,1,0:T(8,128)(2,1)S(1)} %pick_refs.3.own_ref, bf16[4,128,128]{2,1,0:T(8,128)(2,1)S(1)} %collective-permute-done.15.other_ref, bf16[4,768,256]{2,1,0:T(8,128)(2,1)S(1)} %turn.2.early_ref, bf16[4,256,256]{2,1,0:T(8,128)(2,1)S(1)} %turn.3.late_ref), custom_call_target="tpu_custom_call" | custom-call | flops 4294967296 | bytes 16777216 | tf_op jit(solution)/shard_map/solve_apply/pallas_call | solution.py:372
Async XLA Ops:
  3.5 44.3 %copy-start.2 = (s32[1,64]{1,0:T(1,128)S(1)}, s32[1,64]{1,0:T(1,128)}, u32[]{:S(2)}) copy-start(s32[1,64]{1,0:T(1,128)} %param.5) | copy-start | bytes 772
  3.5 16.1 %collective-permute-start.4 = (bf16[64,1024]{1,0:T(8,128)(2,1)}, bf16[64,1024]{1,0:T(8,128)(2,1)S(1)}, u32[]{:S(2)}, u32[]{:S(2)}) collective-permute-start(bf16[64,1024]{1,0:T(8,128)(2,1)} %get-tuple-element.60), channel_id=1, source_target_pairs={{0,16},{2,18},{4,20},{6,22},{8,24},{10,26},{12,28},{14,30},{16,0},... | collective-permute-start | bytes 393224 | tf_op jit(solution)/shard_map/ppermute | solution.py:408
  7.6 13.5 %collective-permute-start.5 = (bf16[64,1024]{1,0:T(8,128)(2,1)}, bf16[64,1024]{1,0:T(8,128)(2,1)S(1)}, u32[]{:S(2)}, u32[]{:S(2)}) collective-permute-start(bf16[64,1024]{1,0:T(8,128)(2,1)} %get-tuple-element.61), channel_id=1, source_target_pairs={{0,2},{2,0},{4,6},{6,4},{8,10},{10,8},{12,14},{14,12},{16,18},{18,... | collective-permute-start | bytes 393224 | tf_op jit(solution)/shard_map/ppermute | solution.py:408
  9.1 14.3 %collective-permute-start.6 = (bf16[64,1024]{1,0:T(8,128)(2,1)}, bf16[64,1024]{1,0:T(8,128)(2,1)S(1)}, u32[]{:S(2)}, u32[]{:S(2)}) collective-permute-start(bf16[64,1024]{1,0:T(8,128)(2,1)} %get-tuple-element.62), channel_id=1, source_target_pairs={{0,30},{2,28},{4,26},{6,24},{8,22},{10,20},{12,18},{14,16},{16,14}... | collective-permute-start | bytes 393224 | tf_op jit(solution)/shard_map/ppermute | solution.py:408
  11.4 12.0 %collective-permute-start.7 = (bf16[64,1024]{1,0:T(8,128)(2,1)}, bf16[64,1024]{1,0:T(8,128)(2,1)S(1)}, u32[]{:S(2)}, u32[]{:S(2)}) collective-permute-start(bf16[64,1024]{1,0:T(8,128)(2,1)} %get-tuple-element.63), channel_id=1, source_target_pairs={{0,8},{2,10},{4,12},{6,14},{8,0},{10,2},{12,4},{14,6},{16,24},{18,... | collective-permute-start | bytes 393224 | tf_op jit(solution)/shard_map/ppermute | solution.py:408
  16.6 13.3 %collective-permute-start.8 = (bf16[64,1024]{1,0:T(8,128)(2,1)}, bf16[64,1024]{1,0:T(8,128)(2,1)S(1)}, u32[]{:S(2)}, u32[]{:S(2)}) collective-permute-start(bf16[64,1024]{1,0:T(8,128)(2,1)} %get-tuple-element.64), channel_id=1, source_target_pairs={{0,20},{2,22},{4,16},{6,18},{8,28},{10,30},{12,24},{14,26},{16,4},... | collective-permute-start | bytes 393224 | tf_op jit(solution)/shard_map/ppermute | solution.py:408
  19.6 11.8 %collective-permute-start.9 = (bf16[64,1024]{1,0:T(8,128)(2,1)}, bf16[64,1024]{1,0:T(8,128)(2,1)S(1)}, u32[]{:S(2)}, u32[]{:S(2)}) collective-permute-start(bf16[64,1024]{1,0:T(8,128)(2,1)} %get-tuple-element.65), channel_id=1, source_target_pairs={{0,4},{2,6},{4,0},{6,2},{8,12},{10,14},{12,8},{14,10},{16,20},{18,... | collective-permute-start | bytes 393224 | tf_op jit(solution)/shard_map/ppermute | solution.py:408
  21.2 15.0 %collective-permute-start.10 = (bf16[64,1024]{1,0:T(8,128)(2,1)}, bf16[64,1024]{1,0:T(8,128)(2,1)S(1)}, u32[]{:S(2)}, u32[]{:S(2)}) collective-permute-start(bf16[64,1024]{1,0:T(8,128)(2,1)} %get-tuple-element.66), channel_id=1, source_target_pairs={{0,26},{2,24},{4,30},{6,28},{8,18},{10,16},{12,22},{14,20},{16,10}... | collective-permute-start | bytes 393224 | tf_op jit(solution)/shard_map/ppermute | solution.py:408
  23.4 18.2 %collective-permute-start.11 = (bf16[64,1024]{1,0:T(8,128)(2,1)}, bf16[64,1024]{1,0:T(8,128)(2,1)S(1)}, u32[]{:S(2)}, u32[]{:S(2)}) collective-permute-start(bf16[64,1024]{1,0:T(8,128)(2,1)} %get-tuple-element.67), channel_id=1, source_target_pairs={{0,10},{2,8},{4,14},{6,12},{8,2},{10,0},{12,6},{14,4},{16,26},{18,... | collective-permute-start | bytes 393224 | tf_op jit(solution)/shard_map/ppermute | solution.py:408
  23.4 19.0 %collective-permute-start.12 = (bf16[64,1024]{1,0:T(8,128)(2,1)}, bf16[64,1024]{1,0:T(8,128)(2,1)S(1)}, u32[]{:S(2)}, u32[]{:S(2)}) collective-permute-start(bf16[64,1024]{1,0:T(8,128)(2,1)} %get-tuple-element.68), channel_id=1, source_target_pairs={{0,18},{2,16},{4,22},{6,20},{8,26},{10,24},{12,30},{14,28},{16,2},... | collective-permute-start | bytes 393224 | tf_op jit(solution)/shard_map/ppermute | solution.py:408
  29.8 12.8 %collective-permute-start.13 = (bf16[64,1024]{1,0:T(8,128)(2,1)}, bf16[64,1024]{1,0:T(8,128)(2,1)S(1)}, u32[]{:S(2)}, u32[]{:S(2)}) collective-permute-start(bf16[64,1024]{1,0:T(8,128)(2,1)} %get-tuple-element.69), channel_id=1, source_target_pairs={{0,6},{2,4},{4,2},{6,0},{8,14},{10,12},{12,10},{14,8},{16,22},{18,... | collective-permute-start | bytes 393224 | tf_op jit(solution)/shard_map/ppermute | solution.py:408
  31.5 16.4 %collective-permute-start.14 = (bf16[64,1024]{1,0:T(8,128)(2,1)}, bf16[64,1024]{1,0:T(8,128)(2,1)S(1)}, u32[]{:S(2)}, u32[]{:S(2)}) collective-permute-start(bf16[64,1024]{1,0:T(8,128)(2,1)} %get-tuple-element.70), channel_id=1, source_target_pairs={{0,28},{2,30},{4,24},{6,26},{8,20},{10,22},{12,16},{14,18},{16,12}... | collective-permute-start | bytes 393224 | tf_op jit(solution)/shard_map/ppermute | solution.py:408
  36.2 13.2 %collective-permute-start = (bf16[64,1024]{1,0:T(8,128)(2,1)}, bf16[64,1024]{1,0:T(8,128)(2,1)S(1)}, u32[]{:S(2)}, u32[]{:S(2)}) collective-permute-start(bf16[64,1024]{1,0:T(8,128)(2,1)} %get-tuple-element.55), channel_id=1, source_target_pairs={{0,12},{2,14},{4,8},{6,10},{8,4},{10,6},{12,0},{14,2},{16,28},{18,... | collective-permute-start | bytes 393224 | tf_op jit(solution)/shard_map/ppermute | solution.py:408
  41.6 13.7 %collective-permute-start.1 = (bf16[64,1024]{1,0:T(8,128)(2,1)}, bf16[64,1024]{1,0:T(8,128)(2,1)S(1)}, u32[]{:S(2)}, u32[]{:S(2)}) collective-permute-start(bf16[64,1024]{1,0:T(8,128)(2,1)} %get-tuple-element.56), channel_id=1, source_target_pairs={{0,22},{2,20},{4,18},{6,16},{8,30},{10,28},{12,26},{14,24},{16,6},... | collective-permute-start | bytes 393224 | tf_op jit(solution)/shard_map/ppermute | solution.py:408
  42.5 12.8 %collective-permute-start.2 = (bf16[64,1024]{1,0:T(8,128)(2,1)}, bf16[64,1024]{1,0:T(8,128)(2,1)S(1)}, u32[]{:S(2)}, u32[]{:S(2)}) collective-permute-start(bf16[64,1024]{1,0:T(8,128)(2,1)} %get-tuple-element.57), channel_id=1, source_target_pairs={{0,14},{2,12},{4,10},{6,8},{8,6},{10,4},{12,2},{14,0},{16,30},{18,... | collective-permute-start | bytes 393224 | tf_op jit(solution)/shard_map/ppermute | solution.py:408
  42.7 12.6 %collective-permute-start.3 = (bf16[64,1024]{1,0:T(8,128)(2,1)}, bf16[64,1024]{1,0:T(8,128)(2,1)S(1)}, u32[]{:S(2)}, u32[]{:S(2)}) collective-permute-start(bf16[64,1024]{1,0:T(8,128)(2,1)} %get-tuple-element.58), channel_id=1, source_target_pairs={{0,24},{2,26},{4,28},{6,30},{8,16},{10,18},{12,20},{14,22},{16,8},... | collective-permute-start | bytes 393224 | tf_op jit(solution)/shard_map/ppermute | solution.py:408
  47.9 0.9 %copy-start = (bf16[64,1024]{1,0:T(8,128)(2,1)S(1)}, bf16[64,1024]{1,0:T(8,128)(2,1)}, u32[]{:S(2)}) copy-start(bf16[64,1024]{1,0:T(8,128)(2,1)} %get-tuple-element.59.rest_0_.refs_0_) | copy-start | bytes 393220
  48.8 7.1 %copy-start.1 = (bf16[64,1024]{1,0:T(8,128)(2,1)S(1)}, bf16[64,1024]{1,0:T(8,128)(2,1)}, u32[]{:S(2)}) copy-start(bf16[64,1024]{1,0:T(8,128)(2,1)} %get-tuple-element.59.rest_0_.refs_0_) | copy-start | bytes 393220
  55.6 1.4 %collective-permute-start.15 = (bf16[4,128,128]{2,1,0:T(8,128)(2,1)S(1)}, bf16[4,128,128]{2,1,0:T(8,128)(2,1)S(1)}, u32[]{:S(2)}, u32[]{:S(2)}) collective-permute-start(bf16[4,128,128]{2,1,0:T(8,128)(2,1)S(1)} %pick_refs.3.own_ref), channel_id=1, source_target_pairs={{0,1},{1,0},{2,3},{3,2},{4,5},{5,4},{6,7},{7,6},{8,9},{9,8},{10,11... | collective-permute-start | bytes 393224 | tf_op jit(solution)/shard_map/ppermute | solution.py:412

commit v4 on v3

--- a/solution.py
+++ b/solution.py
@@ -15,8 +15,8 @@
 SUB = 8
 VMEM_LIMIT = 48 * 1024 * 1024
 SPECTRA_LIMIT = 66000000
-SHIFTS = (8, 1, 15, 4, 10, 2, 13, 5, 9, 3, 14, 6, 11, 7, 12)
-FIRST = 4
+SHIFTS = (12, 7, 9, 4, 10, 5, 15, 1, 13, 2, 11, 6, 14, 3, 8)
+FIRST = 3
 LATE = 4
 MAX_GAP = 768
 

time: 68.2 us -> 67.6 us (level)
  starting transfers between devices: 35.8 us -> 34.7 us
    ppermute x15, starting transfers between devices: 35.7 us -> 34.6 us  [local_kernels(): got[shift] = lax.ppermute(block, 'bin', pairs) if shift else block]
  transfers between devices with their start and end apart: 16 -> 16, of which waited for: 4 -> 7; matrix products, arithmetic and copies ran while one was open for 0% -> 0% of each run, Pallas kernels for 9% -> 10%
where the time goes in v4:
time: 67.6 us; the launch traced here: 67.5 us
  starting transfers between devices  34.7 us (51%)
  Pallas kernels  21.6 us (32%)
  waiting for transfers between devices  10.1 us (15%)
  local copies, waits for them, and re-layouts  0.91 us (1%)
    ppermute x15, starting transfers between devices, local_kernels(): got[shift] = lax.ppermute(block, 'bin', pairs) if shift else block  34.6 us
    pallas_call x1, Pallas kernels, solve_and_apply(): pl.pallas_call(functools.partial(solve_kernel, shifts), out_shape=jax.Sha...  11 us
    ppermute x15, waiting for transfers between devices, local_kernels(): got[shift] = lax.ppermute(block, 'bin', pairs) if shift else block  9.41 us
    pallas_call x2, Pallas kernels, spectra_of(): pl.pallas_call(functools.partial(spectra_kernel, dest_of, count), out_sha...  9.08 us
  transfers between devices with their start and end apart: 16, of which 7 were waited for; matrix products, arithmetic and copies ran while one was open for 0% of the time, Pallas kernels for 10%

profile of v4, /device:TPU:0, one launch (start us, length us, event | category | flops | bytes accessed | tf_op | source)
XLA Modules:
  0.0 67.5 jit_solution(17125827045657195590)
XLA Ops:
  0.0 3.4 %spectra.2 = (bf16[64,1024]{1,0:T(8,128)(2,1)}, bf16[64,1024]{1,0:T(8,128)(2,1)}, bf16[64,1024]{1,0:T(8,128)(2,1)}) custom-call(s32[16]{0:T(128)} %starts_hbm.3, bf16[64,8704]{1,0:T(8,128)(2,1)} %bitcast.1, bf16[16,64,1024]{2,1,0:T(8,128)(2,1)} %constant.2.clone.table_hbm), custom_call_target="tpu_custom_call" | custom-call | flops 402653184 | bytes 786432 | tf_op jit(solution)/shard_map/spectra/pallas_call | solution.py:122
  3.4 0.0 copy-start.2
  3.4 5.1 %collective-permute-start.4 = (bf16[64,1024]{1,0:T(8,128)(2,1)}, bf16[64,1024]{1,0:T(8,128)(2,1)S(1)}, u32[]{:S(2)}, u32[]{:S(2)}) collective-permute-start(bf16[64,1024]{1,0:T(8,128)(2,1)} %get-tuple-element.60), channel_id=1, source_target_pairs={{0,24},{2,26},{4,28},{6,30},{8,16},{10,18},{12,20},{14,22},{16,8},... | collective-permute-start | bytes 393224 | tf_op jit(solution)/shard_map/ppermute | solution.py:408
  8.6 1.4 %collective-permute-start.5 = (bf16[64,1024]{1,0:T(8,128)(2,1)}, bf16[64,1024]{1,0:T(8,128)(2,1)S(1)}, u32[]{:S(2)}, u32[]{:S(2)}) collective-permute-start(bf16[64,1024]{1,0:T(8,128)(2,1)} %get-tuple-element.61), channel_id=1, source_target_pairs={{0,14},{2,12},{4,10},{6,8},{8,6},{10,4},{12,2},{14,0},{16,30},{18,... | collective-permute-start | bytes 393224 | tf_op jit(solution)/shard_map/ppermute | solution.py:408
  10.0 1.2 %collective-permute-start.6 = (bf16[64,1024]{1,0:T(8,128)(2,1)}, bf16[64,1024]{1,0:T(8,128)(2,1)S(1)}, u32[]{:S(2)}, u32[]{:S(2)}) collective-permute-start(bf16[64,1024]{1,0:T(8,128)(2,1)} %get-tuple-element.62), channel_id=1, source_target_pairs={{0,18},{2,16},{4,22},{6,20},{8,26},{10,24},{12,30},{14,28},{16,2},... | collective-permute-start | bytes 393224 | tf_op jit(solution)/shard_map/ppermute | solution.py:408
  11.2 5.7 %spectra.3 = (bf16[64,1024]{1,0:T(8,128)(2,1)}, bf16[64,1024]{1,0:T(8,128)(2,1)}, bf16[64,1024]{1,0:T(8,128)(2,1)}, bf16[64,1024]{1,0:T(8,128)(2,1)}, bf16[64,10...) custom-call(s32[16]{0:T(128)} %starts_hbm.3, ...), custom_call_target="tpu_custom_call" | custom-call | flops 1744830464 | bytes 3407872 | tf_op jit(solution)/shard_map/spectra/pallas_call | solution.py:122
  16.9 1.3 %collective-permute-start.7 = (bf16[64,1024]{1,0:T(8,128)(2,1)}, bf16[64,1024]{1,0:T(8,128)(2,1)S(1)}, u32[]{:S(2)}, u32[]{:S(2)}) collective-permute-start(bf16[64,1024]{1,0:T(8,128)(2,1)} %get-tuple-element.63), channel_id=1, source_target_pairs={{0,8},{2,10},{4,12},{6,14},{8,0},{10,2},{12,4},{14,6},{16,24},{18,... | collective-permute-start | bytes 393224 | tf_op jit(solution)/shard_map/ppermute | solution.py:408
  18.2 2.8 %collective-permute-start.8 = (bf16[64,1024]{1,0:T(8,128)(2,1)}, bf16[64,1024]{1,0:T(8,128)(2,1)S(1)}, u32[]{:S(2)}, u32[]{:S(2)}) collective-permute-start(bf16[64,1024]{1,0:T(8,128)(2,1)} %get-tuple-element.64), channel_id=1, source_target_pairs={{0,20},{2,22},{4,16},{6,18},{8,28},{10,30},{12,24},{14,26},{16,4},... | collective-permute-start | bytes 393224 | tf_op jit(solution)/shard_map/ppermute | solution.py:408
  21.0 0.0 collective-permute-done.4.rest_1_.refs_1_
  21.0 1.0 %collective-permute-start.9 = (bf16[64,1024]{1,0:T(8,128)(2,1)}, bf16[64,1024]{1,0:T(8,128)(2,1)S(1)}, u32[]{:S(2)}, u32[]{:S(2)}) collective-permute-start(bf16[64,1024]{1,0:T(8,128)(2,1)} %get-tuple-element.65), channel_id=1, source_target_pairs={{0,10},{2,8},{4,14},{6,12},{8,2},{10,0},{12,6},{14,4},{16,26},{18,... | collective-permute-start | bytes 393224 | tf_op jit(solution)/shard_map/ppermute | solution.py:408
  22.0 0.0 collective-permute-done.5.rest_2_.refs_2_
  22.0 2.4 %collective-permute-start.10 = (bf16[64,1024]{1,0:T(8,128)(2,1)}, bf16[64,1024]{1,0:T(8,128)(2,1)S(1)}, u32[]{:S(2)}, u32[]{:S(2)}) collective-permute-start(bf16[64,1024]{1,0:T(8,128)(2,1)} %get-tuple-element.66), channel_id=1, source_target_pairs={{0,30},{2,28},{4,26},{6,24},{8,22},{10,20},{12,18},{14,16},{16,14}... | collective-permute-start | bytes 393224 | tf_op jit(solution)/shard_map/ppermute | solution.py:408
  24.4 0.0 collective-permute-done.6.rest_3_.refs_3_
  24.4 0.9 %collective-permute-start.11 = (bf16[64,1024]{1,0:T(8,128)(2,1)}, bf16[64,1024]{1,0:T(8,128)(2,1)S(1)}, u32[]{:S(2)}, u32[]{:S(2)}) collective-permute-start(bf16[64,1024]{1,0:T(8,128)(2,1)} %get-tuple-element.67), channel_id=1, source_target_pairs={{0,2},{2,0},{4,6},{6,4},{8,10},{10,8},{12,14},{14,12},{16,18},{18,... | collective-permute-start | bytes 393224 | tf_op jit(solution)/shard_map/ppermute | solution.py:408
  25.3 0.9 %collective-permute-done.7.rest_4_.refs_4_ = bf16[64,1024]{1,0:T(8,128)(2,1)S(1)} collective-permute-done((bf16[64,1024]{1,0:T(8,128)(2,1)}, bf16[64,1024]{1,0:T(8,128)(2,1)S(1)}, u32[]{:S(2)}, u32[]{:S(2)}) %collective-permute-start.7) | collective-permute-done | bytes 131104 | tf_op jit(solution)/shard_map/ppermute | solution.py:408
  26.2 3.0 %collective-permute-start.12 = (bf16[64,1024]{1,0:T(8,128)(2,1)}, bf16[64,1024]{1,0:T(8,128)(2,1)S(1)}, u32[]{:S(2)}, u32[]{:S(2)}) collective-permute-start(bf16[64,1024]{1,0:T(8,128)(2,1)} %get-tuple-element.68), channel_id=1, source_target_pairs={{0,26},{2,24},{4,30},{6,28},{8,18},{10,16},{12,22},{14,20},{16,10}... | collective-permute-start | bytes 393224 | tf_op jit(solution)/shard_map/ppermute | solution.py:408
  29.2 0.0 collective-permute-done.8.rest_5_.refs_5_
  29.2 1.4 %collective-permute-start.13 = (bf16[64,1024]{1,0:T(8,128)(2,1)}, bf16[64,1024]{1,0:T(8,128)(2,1)S(1)}, u32[]{:S(2)}, u32[]{:S(2)}) collective-permute-start(bf16[64,1024]{1,0:T(8,128)(2,1)} %get-tuple-element.69), channel_id=1, source_target_pairs={{0,4},{2,6},{4,0},{6,2},{8,12},{10,14},{12,8},{14,10},{16,20},{18,... | collective-permute-start | bytes 393224 | tf_op jit(solution)/shard_map/ppermute | solution.py:408
  30.6 0.0 collective-permute-done.9.rest_6_.refs_6_
  30.6 1.4 %collective-permute-start.14 = (bf16[64,1024]{1,0:T(8,128)(2,1)}, bf16[64,1024]{1,0:T(8,128)(2,1)S(1)}, u32[]{:S(2)}, u32[]{:S(2)}) collective-permute-start(bf16[64,1024]{1,0:T(8,128)(2,1)} %get-tuple-element.70), channel_id=1, source_target_pairs={{0,22},{2,20},{4,18},{6,16},{8,30},{10,28},{12,26},{14,24},{16,6},... | collective-permute-start | bytes 393224 | tf_op jit(solution)/shard_map/ppermute | solution.py:408
  32.0 2.4 %collective-permute-done.10.rest_7_.refs_7_ = bf16[64,1024]{1,0:T(8,128)(2,1)S(1)} collective-permute-done((bf16[64,1024]{1,0:T(8,128)(2,1)}, bf16[64,1024]{1,0:T(8,128)(2,1)S(1)}, u32[]{:S(2)}, u32[]{:S(2)}) %collective-permute-start.10) | collective-permute-done | bytes 131104 | tf_op jit(solution)/shard_map/ppermute | solution.py:408
  34.5 6.8 %collective-permute-start = (bf16[64,1024]{1,0:T(8,128)(2,1)}, bf16[64,1024]{1,0:T(8,128)(2,1)S(1)}, u32[]{:S(2)}, u32[]{:S(2)}) collective-permute-start(bf16[64,1024]{1,0:T(8,128)(2,1)} %get-tuple-element.55), channel_id=1, source_target_pairs={{0,12},{2,14},{4,8},{6,10},{8,4},{10,6},{12,0},{14,2},{16,28},{18,... | collective-permute-start | bytes 393224 | tf_op jit(solution)/shard_map/ppermute | solution.py:408
  41.2 0.0 collective-permute-done.11.rest_8_.refs_8_
  41.2 3.5 %collective-permute-start.1 = (bf16[64,1024]{1,0:T(8,128)(2,1)}, bf16[64,1024]{1,0:T(8,128)(2,1)S(1)}, u32[]{:S(2)}, u32[]{:S(2)}) collective-permute-start(bf16[64,1024]{1,0:T(8,128)(2,1)} %get-tuple-element.56), channel_id=1, source_target_pairs={{0,28},{2,30},{4,24},{6,26},{8,20},{10,22},{12,16},{14,18},{16,12}... | collective-permute-start | bytes 393224 | tf_op jit(solution)/shard_map/ppermute | solution.py:408
  44.7 0.0 collective-permute-done.12.rest_9_.refs_9_
  44.7 0.8 %collective-permute-start.2 = (bf16[64,1024]{1,0:T(8,128)(2,1)}, bf16[64,1024]{1,0:T(8,128)(2,1)S(1)}, u32[]{:S(2)}, u32[]{:S(2)}) collective-permute-start(bf16[64,1024]{1,0:T(8,128)(2,1)} %get-tuple-element.57), channel_id=1, source_target_pairs={{0,6},{2,4},{4,2},{6,0},{8,14},{10,12},{12,10},{14,8},{16,22},{18,... | collective-permute-start | bytes 393224 | tf_op jit(solution)/shard_map/ppermute | solution.py:408
  45.6 0.0 collective-permute-done.13.rest_10_.refs_10_
  45.6 1.5 %collective-permute-start.3 = (bf16[64,1024]{1,0:T(8,128)(2,1)}, bf16[64,1024]{1,0:T(8,128)(2,1)S(1)}, u32[]{:S(2)}, u32[]{:S(2)}) collective-permute-start(bf16[64,1024]{1,0:T(8,128)(2,1)} %get-tuple-element.58), channel_id=1, source_target_pairs={{0,16},{2,18},{4,20},{6,22},{8,24},{10,26},{12,28},{14,30},{16,0},... | collective-permute-start | bytes 393224 | tf_op jit(solution)/shard_map/ppermute | solution.py:408
  47.1 0.0 copy-done.2
  47.1 0.1 pad_add_fusion.index_ref
  47.2 1.2 %collective-permute-done.14.rest_11_.refs_11_ = bf16[64,1024]{1,0:T(8,128)(2,1)S(1)} collective-permute-done((bf16[64,1024]{1,0:T(8,128)(2,1)}, bf16[64,1024]{1,0:T(8,128)(2,1)S(1)}, u32[]{:S(2)}, u32[]{:S(2)}) %collective-permute-start.14) | collective-permute-done | bytes 131104 | tf_op jit(solution)/shard_map/ppermute | solution.py:408
  48.4 0.0 copy-start
  48.4 0.9 %copy-done = bf16[64,1024]{1,0:T(8,128)(2,1)S(1)} copy-done((bf16[64,1024]{1,0:T(8,128)(2,1)S(1)}, bf16[64,1024]{1,0:T(8,128)(2,1)}, u32[]{:S(2)}) %copy-start) | copy-done | bytes 131096
  49.3 0.0 copy-start.1
  49.3 0.6 pick_refs.2.rest_4_
  49.9 0.0 collective-permute-done.rest_0_.refs_0_
  49.9 1.1 %collective-permute-done.1.rest_1_.refs_1_ = bf16[64,1024]{1,0:T(8,128)(2,1)S(1)} collective-permute-done((bf16[64,1024]{1,0:T(8,128)(2,1)}, bf16[64,1024]{1,0:T(8,128)(2,1)S(1)}, u32[]{:S(2)}, u32[]{:S(2)}) %collective-permute-start.1) | collective-permute-done | bytes 131104 | tf_op jit(solution)/shard_map/ppermute | solution.py:408
  50.9 0.7 collective-permute-done.2.rest_2_.refs_2_
  51.6 3.1 %collective-permute-done.3.rest_3_.refs_3_ = bf16[64,1024]{1,0:T(8,128)(2,1)S(1)} collective-permute-done((bf16[64,1024]{1,0:T(8,128)(2,1)}, bf16[64,1024]{1,0:T(8,128)(2,1)S(1)}, u32[]{:S(2)}, u32[]{:S(2)}) %collective-permute-start.3) | collective-permute-done | bytes 131104 | tf_op jit(solution)/shard_map/ppermute | solution.py:408
  54.7 0.3 pick_refs.3.own_ref
  55.0 0.1 collective-permute-start.15
  55.1 0.2 turn.3.late_ref
  55.3 0.0 copy-done.1
  55.3 0.5 turn.2.early_ref
  55.8 0.7 collective-permute-done.15.other_ref
  56.4 11.0 %solve_apply.1 = bf16[32,1024,256]{2,1,0:T(8,128)(2,1)} custom-call(bf16[4,128,128]{2,1,0:T(8,128)(2,1)S(1)} %pick_refs.3.own_ref, bf16[4,128,128]{2,1,0:T(8,128)(2,1)S(1)} %collective-permute-done.15.other_ref, bf16[4,768,256]{2,1,0:T(8,128)(2,1)S(1)} %turn.2.early_ref, bf16[4,256,256]{2,1,0:T(8,128)(2,1)S(1)} %turn.3.late_ref), custom_call_target="tpu_custom_call" | custom-call | flops 4294967296 | bytes 16777216 | tf_op jit(solution)/shard_map/solve_apply/pallas_call | solution.py:372
Async XLA Ops:
  3.4 43.7 %copy-start.2 = (s32[1,64]{1,0:T(1,128)S(1)}, s32[1,64]{1,0:T(1,128)}, u32[]{:S(2)}) copy-start(s32[1,64]{1,0:T(1,128)} %param.5) | copy-start | bytes 772
  3.4 17.6 %collective-permute-start.4 = (bf16[64,1024]{1,0:T(8,128)(2,1)}, bf16[64,1024]{1,0:T(8,128)(2,1)S(1)}, u32[]{:S(2)}, u32[]{:S(2)}) collective-permute-start(bf16[64,1024]{1,0:T(8,128)(2,1)} %get-tuple-element.60), channel_id=1, source_target_pairs={{0,24},{2,26},{4,28},{6,30},{8,16},{10,18},{12,20},{14,22},{16,8},... | collective-permute-start | bytes 393224 | tf_op jit(solution)/shard_map/ppermute | solution.py:408
  8.6 13.5 %collective-permute-start.5 = (bf16[64,1024]{1,0:T(8,128)(2,1)}, bf16[64,1024]{1,0:T(8,128)(2,1)S(1)}, u32[]{:S(2)}, u32[]{:S(2)}) collective-permute-start(bf16[64,1024]{1,0:T(8,128)(2,1)} %get-tuple-element.61), channel_id=1, source_target_pairs={{0,14},{2,12},{4,10},{6,8},{8,6},{10,4},{12,2},{14,0},{16,30},{18,... | collective-permute-start | bytes 393224 | tf_op jit(solution)/shard_map/ppermute | solution.py:408
  10.0 14.4 %collective-permute-start.6 = (bf16[64,1024]{1,0:T(8,128)(2,1)}, bf16[64,1024]{1,0:T(8,128)(2,1)S(1)}, u32[]{:S(2)}, u32[]{:S(2)}) collective-permute-start(bf16[64,1024]{1,0:T(8,128)(2,1)} %get-tuple-element.62), channel_id=1, source_target_pairs={{0,18},{2,16},{4,22},{6,20},{8,26},{10,24},{12,30},{14,28},{16,2},... | collective-permute-start | bytes 393224 | tf_op jit(solution)/shard_map/ppermute | solution.py:408
  16.9 9.3 %collective-permute-start.7 = (bf16[64,1024]{1,0:T(8,128)(2,1)}, bf16[64,1024]{1,0:T(8,128)(2,1)S(1)}, u32[]{:S(2)}, u32[]{:S(2)}) collective-permute-start(bf16[64,1024]{1,0:T(8,128)(2,1)} %get-tuple-element.63), channel_id=1, source_target_pairs={{0,8},{2,10},{4,12},{6,14},{8,0},{10,2},{12,4},{14,6},{16,24},{18,... | collective-permute-start | bytes 393224 | tf_op jit(solution)/shard_map/ppermute | solution.py:408
  18.2 11.0 %collective-permute-start.8 = (bf16[64,1024]{1,0:T(8,128)(2,1)}, bf16[64,1024]{1,0:T(8,128)(2,1)S(1)}, u32[]{:S(2)}, u32[]{:S(2)}) collective-permute-start(bf16[64,1024]{1,0:T(8,128)(2,1)} %get-tuple-element.64), channel_id=1, source_target_pairs={{0,20},{2,22},{4,16},{6,18},{8,28},{10,30},{12,24},{14,26},{16,4},... | collective-permute-start | bytes 393224 | tf_op jit(solution)/shard_map/ppermute | solution.py:408
  21.0 9.6 %collective-permute-start.9 = (bf16[64,1024]{1,0:T(8,128)(2,1)}, bf16[64,1024]{1,0:T(8,128)(2,1)S(1)}, u32[]{:S(2)}, u32[]{:S(2)}) collective-permute-start(bf16[64,1024]{1,0:T(8,128)(2,1)} %get-tuple-element.65), channel_id=1, source_target_pairs={{0,10},{2,8},{4,14},{6,12},{8,2},{10,0},{12,6},{14,4},{16,26},{18,... | collective-permute-start | bytes 393224 | tf_op jit(solution)/shard_map/ppermute | solution.py:408
  22.0 12.4 %collective-permute-start.10 = (bf16[64,1024]{1,0:T(8,128)(2,1)}, bf16[64,1024]{1,0:T(8,128)(2,1)S(1)}, u32[]{:S(2)}, u32[]{:S(2)}) collective-permute-start(bf16[64,1024]{1,0:T(8,128)(2,1)} %get-tuple-element.66), channel_id=1, source_target_pairs={{0,30},{2,28},{4,26},{6,24},{8,22},{10,20},{12,18},{14,16},{16,14}... | collective-permute-start | bytes 393224 | tf_op jit(solution)/shard_map/ppermute | solution.py:408
  24.4 16.8 %collective-permute-start.11 = (bf16[64,1024]{1,0:T(8,128)(2,1)}, bf16[64,1024]{1,0:T(8,128)(2,1)S(1)}, u32[]{:S(2)}, u32[]{:S(2)}) collective-permute-start(bf16[64,1024]{1,0:T(8,128)(2,1)} %get-tuple-element.67), channel_id=1, source_target_pairs={{0,2},{2,0},{4,6},{6,4},{8,10},{10,8},{12,14},{14,12},{16,18},{18,... | collective-permute-start | bytes 393224 | tf_op jit(solution)/shard_map/ppermute | solution.py:408
  26.2 18.5 %collective-permute-start.12 = (bf16[64,1024]{1,0:T(8,128)(2,1)}, bf16[64,1024]{1,0:T(8,128)(2,1)S(1)}, u32[]{:S(2)}, u32[]{:S(2)}) collective-permute-start(bf16[64,1024]{1,0:T(8,128)(2,1)} %get-tuple-element.68), channel_id=1, source_target_pairs={{0,26},{2,24},{4,30},{6,28},{8,18},{10,16},{12,22},{14,20},{16,10}... | collective-permute-start | bytes 393224 | tf_op jit(solution)/shard_map/ppermute | solution.py:408
  29.2 16.3 %collective-permute-start.13 = (bf16[64,1024]{1,0:T(8,128)(2,1)}, bf16[64,1024]{1,0:T(8,128)(2,1)S(1)}, u32[]{:S(2)}, u32[]{:S(2)}) collective-permute-start(bf16[64,1024]{1,0:T(8,128)(2,1)} %get-tuple-element.69), channel_id=1, source_target_pairs={{0,4},{2,6},{4,0},{6,2},{8,12},{10,14},{12,8},{14,10},{16,20},{18,... | collective-permute-start | bytes 393224 | tf_op jit(solution)/shard_map/ppermute | solution.py:408
  30.6 17.8 %collective-permute-start.14 = (bf16[64,1024]{1,0:T(8,128)(2,1)}, bf16[64,1024]{1,0:T(8,128)(2,1)S(1)}, u32[]{:S(2)}, u32[]{:S(2)}) collective-permute-start(bf16[64,1024]{1,0:T(8,128)(2,1)} %get-tuple-element.70), channel_id=1, source_target_pairs={{0,22},{2,20},{4,18},{6,16},{8,30},{10,28},{12,26},{14,24},{16,6},... | collective-permute-start | bytes 393224 | tf_op jit(solution)/shard_map/ppermute | solution.py:408
  34.5 15.4 %collective-permute-start = (bf16[64,1024]{1,0:T(8,128)(2,1)}, bf16[64,1024]{1,0:T(8,128)(2,1)S(1)}, u32[]{:S(2)}, u32[]{:S(2)}) collective-permute-start(bf16[64,1024]{1,0:T(8,128)(2,1)} %get-tuple-element.55), channel_id=1, source_target_pairs={{0,12},{2,14},{4,8},{6,10},{8,4},{10,6},{12,0},{14,2},{16,28},{18,... | collective-permute-start | bytes 393224 | tf_op jit(solution)/shard_map/ppermute | solution.py:408
  41.2 9.7 %collective-permute-start.1 = (bf16[64,1024]{1,0:T(8,128)(2,1)}, bf16[64,1024]{1,0:T(8,128)(2,1)S(1)}, u32[]{:S(2)}, u32[]{:S(2)}) collective-permute-start(bf16[64,1024]{1,0:T(8,128)(2,1)} %get-tuple-element.56), channel_id=1, source_target_pairs={{0,28},{2,30},{4,24},{6,26},{8,20},{10,22},{12,16},{14,18},{16,12}... | collective-permute-start | bytes 393224 | tf_op jit(solution)/shard_map/ppermute | solution.py:408
  44.7 6.8 %collective-permute-start.2 = (bf16[64,1024]{1,0:T(8,128)(2,1)}, bf16[64,1024]{1,0:T(8,128)(2,1)S(1)}, u32[]{:S(2)}, u32[]{:S(2)}) collective-permute-start(bf16[64,1024]{1,0:T(8,128)(2,1)} %get-tuple-element.57), channel_id=1, source_target_pairs={{0,6},{2,4},{4,2},{6,0},{8,14},{10,12},{12,10},{14,8},{16,22},{18,... | collective-permute-start | bytes 393224 | tf_op jit(solution)/shard_map/ppermute | solution.py:408
  45.6 9.1 %collective-permute-start.3 = (bf16[64,1024]{1,0:T(8,128)(2,1)}, bf16[64,1024]{1,0:T(8,128)(2,1)S(1)}, u32[]{:S(2)}, u32[]{:S(2)}) collective-permute-start(bf16[64,1024]{1,0:T(8,128)(2,1)} %get-tuple-element.58), channel_id=1, source_target_pairs={{0,16},{2,18},{4,20},{6,22},{8,24},{10,26},{12,28},{14,30},{16,0},... | collective-permute-start | bytes 393224 | tf_op jit(solution)/shard_map/ppermute | solution.py:408
  48.4 0.9 %copy-start = (bf16[64,1024]{1,0:T(8,128)(2,1)S(1)}, bf16[64,1024]{1,0:T(8,128)(2,1)}, u32[]{:S(2)}) copy-start(bf16[64,1024]{1,0:T(8,128)(2,1)} %get-tuple-element.59.rest_0_.refs_0_) | copy-start | bytes 393220
  49.3 6.0 %copy-start.1 = (bf16[64,1024]{1,0:T(8,128)(2,1)S(1)}, bf16[64,1024]{1,0:T(8,128)(2,1)}, u32[]{:S(2)}) copy-start(bf16[64,1024]{1,0:T(8,128)(2,1)} %get-tuple-element.59.rest_0_.refs_0_) | copy-start | bytes 393220
  55.0 1.4 %collective-permute-start.15 = (bf16[4,128,128]{2,1,0:T(8,128)(2,1)S(1)}, bf16[4,128,128]{2,1,0:T(8,128)(2,1)S(1)}, u32[]{:S(2)}, u32[]{:S(2)}) collective-permute-start(bf16[4,128,128]{2,1,0:T(8,128)(2,1)S(1)} %pick_refs.3.own_ref), channel_id=1, source_target_pairs={{0,1},{1,0},{2,3},{3,2},{4,5},{5,4},{6,7},{7,6},{8,9},{9,8},{10,11... | collective-permute-start | bytes 393224 | tf_op jit(solution)/shard_map/ppermute | solution.py:412

commit v5 on v3

--- a/solution.py
+++ b/solution.py
@@ -15,7 +15,7 @@
 SUB = 8
 VMEM_LIMIT = 48 * 1024 * 1024
 SPECTRA_LIMIT = 66000000
-SHIFTS = (8, 1, 15, 4, 10, 2, 13, 5, 9, 3, 14, 6, 11, 7, 12)
+SHIFTS = (12, 1, 14, 9, 4, 5, 10, 7, 15, 2, 11, 6, 13, 3, 8)
 FIRST = 4
 LATE = 4
 MAX_GAP = 768
@@ -318,7 +318,14 @@
     def apply(group, beside):
         done = 0
         for step in range(steps):
-            copy_out(step, group).wait()
+            if isinstance(group, int):
+                copy_out(step, group).wait()
+            else:
+
+                @pl.when(group > 0)
+                def _():
+                    copy_out(step, group).wait()
+
             weights = jnp.concatenate(
                 [
                     jnp.where(row_bin == step * pair + k, wide_ref[group % 2], 0.0).astype(jnp.bfloat16)
@@ -347,11 +354,6 @@
         for _ in beside:
             pass
 
-    for step in range(steps):
-        for ref, rows in ((early_ref, pl.ds(0, early)), (late_ref, pl.ds(early, late))):
-            pltpu.make_async_copy(
-                ref.at[pl.ds(0, pair)], slot_ref.at[step, :, rows], sem.at[step]
-            ).start()
     for _ in solve(0, 0):
         pass
 

time: 68.2 us -> 66.6 us (0.977)
  starting transfers between devices: 35.8 us -> 26.9 us
  waiting for transfers between devices: 9.92 us -> 17.5 us
    ppermute x15, starting transfers between devices: 35.7 us -> 26.8 us  [local_kernels(): got[shift] = lax.ppermute(block, 'bin', pairs) if shift else block]
    ppermute x15, waiting for transfers between devices: 9.26 us -> 16.8 us  [local_kernels(): got[shift] = lax.ppermute(block, 'bin', pairs) if shift else block]
  transfers between devices with their start and end apart: 16 -> 16, of which waited for: 4 -> 7; matrix products, arithmetic and copies ran while one was open for 0% -> 0% of each run, Pallas kernels for 9% -> 10%
where the time goes in v5:
time: 66.6 us; the launch traced here: 66.4 us
  starting transfers between devices  26.9 us (40%)
  Pallas kernels  20.9 us (31%)
  waiting for transfers between devices  17.5 us (26%)
  local copies, waits for them, and re-layouts  0.91 us (1%)
    ppermute x15, starting transfers between devices, local_kernels(): got[shift] = lax.ppermute(block, 'bin', pairs) if shift else block  26.8 us
    ppermute x15, waiting for transfers between devices, local_kernels(): got[shift] = lax.ppermute(block, 'bin', pairs) if shift else block  16.8 us
    pallas_call x1, Pallas kernels, solve_and_apply(): pl.pallas_call(functools.partial(solve_kernel, shifts), out_shape=jax.Sha...  10.7 us
    pallas_call x2, Pallas kernels, spectra_of(): pl.pallas_call(functools.partial(spectra_kernel, dest_of, count), out_sha...  8.69 us
  transfers between devices with their start and end apart: 16, of which 7 were waited for; matrix products, arithmetic and copies ran while one was open for 0% of the time, Pallas kernels for 10%

profile of v5, /device:TPU:0, one launch (start us, length us, event | category | flops | bytes accessed | tf_op | source)
XLA Modules:
  0.0 66.4 jit_solution(15566541934311235594)
XLA Ops:
  0.0 3.5 %spectra.2 = (bf16[64,1024]{1,0:T(8,128)(2,1)}, bf16[64,1024]{1,0:T(8,128)(2,1)}, bf16[64,1024]{1,0:T(8,128)(2,1)}, bf16[64,1024]{1,0:T(8,128)(2,1)}) custom-call(s32[16]{0:T(128)} %starts_hbm.3, bf16[64,8704]{1,0:T(8,128)(2,1)} %bitcast.1, bf16[16,64,1024]{2,1,0:T(8,128)(2,1)} %constant.2.clone.table_hbm), custom_call_target="tpu_custom_call" | custom-call | flops 536870912 | bytes 1048576 | tf_op jit(solution)/shard_map/spectra/pallas_call | solution.py:122
  3.5 0.0 copy-start.2
  3.5 5.1 %collective-permute-start.4 = (bf16[64,1024]{1,0:T(8,128)(2,1)}, bf16[64,1024]{1,0:T(8,128)(2,1)S(1)}, u32[]{:S(2)}, u32[]{:S(2)}) collective-permute-start(bf16[64,1024]{1,0:T(8,128)(2,1)} %get-tuple-element.60), channel_id=1, source_target_pairs={{0,24},{2,26},{4,28},{6,30},{8,16},{10,18},{12,20},{14,22},{16,8},... | collective-permute-start | bytes 393224 | tf_op jit(solution)/shard_map/ppermute | solution.py:410
  8.7 1.5 %collective-permute-start.5 = (bf16[64,1024]{1,0:T(8,128)(2,1)}, bf16[64,1024]{1,0:T(8,128)(2,1)S(1)}, u32[]{:S(2)}, u32[]{:S(2)}) collective-permute-start(bf16[64,1024]{1,0:T(8,128)(2,1)} %get-tuple-element.61), channel_id=1, source_target_pairs={{0,2},{2,0},{4,6},{6,4},{8,10},{10,8},{12,14},{14,12},{16,18},{18,... | collective-permute-start | bytes 393224 | tf_op jit(solution)/shard_map/ppermute | solution.py:410
  10.2 1.2 %collective-permute-start.6 = (bf16[64,1024]{1,0:T(8,128)(2,1)}, bf16[64,1024]{1,0:T(8,128)(2,1)S(1)}, u32[]{:S(2)}, u32[]{:S(2)}) collective-permute-start(bf16[64,1024]{1,0:T(8,128)(2,1)} %get-tuple-element.62), channel_id=1, source_target_pairs={{0,28},{2,30},{4,24},{6,26},{8,20},{10,22},{12,16},{14,18},{16,12}... | collective-permute-start | bytes 393224 | tf_op jit(solution)/shard_map/ppermute | solution.py:410
  11.3 0.8 %collective-permute-start.7 = (bf16[64,1024]{1,0:T(8,128)(2,1)}, bf16[64,1024]{1,0:T(8,128)(2,1)S(1)}, u32[]{:S(2)}, u32[]{:S(2)}) collective-permute-start(bf16[64,1024]{1,0:T(8,128)(2,1)} %get-tuple-element.63), channel_id=1, source_target_pairs={{0,18},{2,16},{4,22},{6,20},{8,26},{10,24},{12,30},{14,28},{16,2},... | collective-permute-start | bytes 393224 | tf_op jit(solution)/shard_map/ppermute | solution.py:410
  12.1 5.2 %spectra.3 = (bf16[64,1024]{1,0:T(8,128)(2,1)}, bf16[64,1024]{1,0:T(8,128)(2,1)}, bf16[64,1024]{1,0:T(8,128)(2,1)}, bf16[64,1024]{1,0:T(8,128)(2,1)}, bf16[64,10...) custom-call(s32[16]{0:T(128)} %starts_hbm.3, ...), custom_call_target="tpu_custom_call" | custom-call | flops 1610612736 | bytes 3145728 | tf_op jit(solution)/shard_map/spectra/pallas_call | solution.py:122
  17.3 3.4 %collective-permute-start.8 = (bf16[64,1024]{1,0:T(8,128)(2,1)}, bf16[64,1024]{1,0:T(8,128)(2,1)S(1)}, u32[]{:S(2)}, u32[]{:S(2)}) collective-permute-start(bf16[64,1024]{1,0:T(8,128)(2,1)} %get-tuple-element.64), channel_id=1, source_target_pairs={{0,8},{2,10},{4,12},{6,14},{8,0},{10,2},{12,4},{14,6},{16,24},{18,... | collective-permute-start | bytes 393224 | tf_op jit(solution)/shard_map/ppermute | solution.py:410
  20.7 0.0 collective-permute-done.4.rest_1_.refs_1_
  20.7 1.7 %collective-permute-start.9 = (bf16[64,1024]{1,0:T(8,128)(2,1)}, bf16[64,1024]{1,0:T(8,128)(2,1)S(1)}, u32[]{:S(2)}, u32[]{:S(2)}) collective-permute-start(bf16[64,1024]{1,0:T(8,128)(2,1)} %get-tuple-element.65), channel_id=1, source_target_pairs={{0,10},{2,8},{4,14},{6,12},{8,2},{10,0},{12,6},{14,4},{16,26},{18,... | collective-permute-start | bytes 393224 | tf_op jit(solution)/shard_map/ppermute | solution.py:410
  22.4 0.0 collective-permute-done.5.rest_2_.refs_2_
  22.4 1.2 %collective-permute-start.10 = (bf16[64,1024]{1,0:T(8,128)(2,1)}, bf16[64,1024]{1,0:T(8,128)(2,1)S(1)}, u32[]{:S(2)}, u32[]{:S(2)}) collective-permute-start(bf16[64,1024]{1,0:T(8,128)(2,1)} %get-tuple-element.66), channel_id=1, source_target_pairs={{0,20},{2,22},{4,16},{6,18},{8,28},{10,30},{12,24},{14,26},{16,4},... | collective-permute-start | bytes 393224 | tf_op jit(solution)/shard_map/ppermute | solution.py:410
  23.6 0.0 collective-permute-done.6.rest_3_.refs_3_
  23.6 2.5 %collective-permute-start.11 = (bf16[64,1024]{1,0:T(8,128)(2,1)}, bf16[64,1024]{1,0:T(8,128)(2,1)S(1)}, u32[]{:S(2)}, u32[]{:S(2)}) collective-permute-start(bf16[64,1024]{1,0:T(8,128)(2,1)} %get-tuple-element.67), channel_id=1, source_target_pairs={{0,14},{2,12},{4,10},{6,8},{8,6},{10,4},{12,2},{14,0},{16,30},{18,... | collective-permute-start | bytes 393224 | tf_op jit(solution)/shard_map/ppermute | solution.py:410
  26.1 2.7 %collective-permute-done.7.rest_4_.refs_4_ = bf16[64,1024]{1,0:T(8,128)(2,1)S(1)} collective-permute-done((bf16[64,1024]{1,0:T(8,128)(2,1)}, bf16[64,1024]{1,0:T(8,128)(2,1)S(1)}, u32[]{:S(2)}, u32[]{:S(2)}) %collective-permute-start.7) | collective-permute-done | bytes 131104 | tf_op jit(solution)/shard_map/ppermute | solution.py:410
  28.9 3.5 %collective-permute-start.12 = (bf16[64,1024]{1,0:T(8,128)(2,1)}, bf16[64,1024]{1,0:T(8,128)(2,1)S(1)}, u32[]{:S(2)}, u32[]{:S(2)}) collective-permute-start(bf16[64,1024]{1,0:T(8,128)(2,1)} %get-tuple-element.68), channel_id=1, source_target_pairs={{0,30},{2,28},{4,26},{6,24},{8,22},{10,20},{12,18},{14,16},{16,14}... | collective-permute-start | bytes 393224 | tf_op jit(solution)/shard_map/ppermute | solution.py:410
  32.4 0.0 collective-permute-done.8.rest_5_.refs_5_
  32.4 0.2 collective-permute-start.13
  32.6 3.1 %collective-permute-done.9.rest_6_.refs_6_ = bf16[64,1024]{1,0:T(8,128)(2,1)S(1)} collective-permute-done((bf16[64,1024]{1,0:T(8,128)(2,1)}, bf16[64,1024]{1,0:T(8,128)(2,1)S(1)}, u32[]{:S(2)}, u32[]{:S(2)}) %collective-permute-start.9) | collective-permute-done | bytes 131104 | tf_op jit(solution)/shard_map/ppermute | solution.py:410
  35.8 0.0 collective-permute-start.14
  35.8 0.0 collective-permute-done.10.rest_7_.refs_7_
  35.8 1.9 %collective-permute-start = (bf16[64,1024]{1,0:T(8,128)(2,1)}, bf16[64,1024]{1,0:T(8,128)(2,1)S(1)}, u32[]{:S(2)}, u32[]{:S(2)}) collective-permute-start(bf16[64,1024]{1,0:T(8,128)(2,1)} %get-tuple-element.55), channel_id=1, source_target_pairs={{0,12},{2,14},{4,8},{6,10},{8,4},{10,6},{12,0},{14,2},{16,28},{18,... | collective-permute-start | bytes 393224 | tf_op jit(solution)/shard_map/ppermute | solution.py:410
  37.7 1.1 %collective-permute-done.11.rest_8_.refs_8_ = bf16[64,1024]{1,0:T(8,128)(2,1)S(1)} collective-permute-done((bf16[64,1024]{1,0:T(8,128)(2,1)}, bf16[64,1024]{1,0:T(8,128)(2,1)S(1)}, u32[]{:S(2)}, u32[]{:S(2)}) %collective-permute-start.11) | collective-permute-done | bytes 131104 | tf_op jit(solution)/shard_map/ppermute | solution.py:410
  38.7 3.2 %collective-permute-start.1 = (bf16[64,1024]{1,0:T(8,128)(2,1)}, bf16[64,1024]{1,0:T(8,128)(2,1)S(1)}, u32[]{:S(2)}, u32[]{:S(2)}) collective-permute-start(bf16[64,1024]{1,0:T(8,128)(2,1)} %get-tuple-element.56), channel_id=1, source_target_pairs={{0,26},{2,24},{4,30},{6,28},{8,18},{10,16},{12,22},{14,20},{16,10}... | collective-permute-start | bytes 393224 | tf_op jit(solution)/shard_map/ppermute | solution.py:410
  41.9 0.0 collective-permute-done.12.rest_9_.refs_9_
  42.0 0.3 collective-permute-start.2
  42.3 3.9 %collective-permute-done.13.rest_10_.refs_10_ = bf16[64,1024]{1,0:T(8,128)(2,1)S(1)} collective-permute-done((bf16[64,1024]{1,0:T(8,128)(2,1)}, bf16[64,1024]{1,0:T(8,128)(2,1)S(1)}, u32[]{:S(2)}, u32[]{:S(2)}) %collective-permute-start.13) | collective-permute-done | bytes 131104 | tf_op jit(solution)/shard_map/ppermute | solution.py:410
  46.2 0.2 collective-permute-start.3
  46.4 0.0 copy-done.2
  46.4 0.1 pad_add_fusion.index_ref
  46.5 0.3 collective-permute-done.14.rest_11_.refs_11_
  46.9 0.0 copy-start
  46.9 0.9 %copy-done = bf16[64,1024]{1,0:T(8,128)(2,1)S(1)} copy-done((bf16[64,1024]{1,0:T(8,128)(2,1)S(1)}, bf16[64,1024]{1,0:T(8,128)(2,1)}, u32[]{:S(2)}) %copy-start) | copy-done | bytes 131096
  47.8 0.0 copy-start.1
  47.8 0.6 pick_refs.2.rest_4_
  48.4 0.0 collective-permute-done.rest_0_.refs_0_
  48.4 0.0 collective-permute-done.1.rest_1_.refs_1_
  48.4 0.0 collective-permute-done.2.rest_2_.refs_2_
  48.4 5.6 %collective-permute-done.3.rest_3_.refs_3_ = bf16[64,1024]{1,0:T(8,128)(2,1)S(1)} collective-permute-done((bf16[64,1024]{1,0:T(8,128)(2,1)}, bf16[64,1024]{1,0:T(8,128)(2,1)S(1)}, u32[]{:S(2)}, u32[]{:S(2)}) %collective-permute-start.3) | collective-permute-done | bytes 131104 | tf_op jit(solution)/shard_map/ppermute | solution.py:410
  53.9 0.3 pick_refs.3.own_ref
  54.2 0.1 collective-permute-start.15
  54.3 0.2 turn.3.late_ref
  54.5 0.0 copy-done.1
  54.5 0.5 turn.2.early_ref
  55.0 0.7 collective-permute-done.15.other_ref
  55.7 10.7 %solve_apply.1 = bf16[32,1024,256]{2,1,0:T(8,128)(2,1)} custom-call(bf16[4,128,128]{2,1,0:T(8,128)(2,1)S(1)} %pick_refs.3.own_ref, bf16[4,128,128]{2,1,0:T(8,128)(2,1)S(1)} %collective-permute-done.15.other_ref, bf16[4,768,256]{2,1,0:T(8,128)(2,1)S(1)} %turn.2.early_ref, bf16[4,256,256]{2,1,0:T(8,128)(2,1)S(1)} %turn.3.late_ref), custom_call_target="tpu_custom_call" | custom-call | flops 4294967296 | bytes 16777216 | tf_op jit(solution)/shard_map/solve_apply/pallas_call | solution.py:374
Async XLA Ops:
  3.5 42.9 %copy-start.2 = (s32[1,64]{1,0:T(1,128)S(1)}, s32[1,64]{1,0:T(1,128)}, u32[]{:S(2)}) copy-start(s32[1,64]{1,0:T(1,128)} %param.5) | copy-start | bytes 772
  3.5 17.2 %collective-permute-start.4 = (bf16[64,1024]{1,0:T(8,128)(2,1)}, bf16[64,1024]{1,0:T(8,128)(2,1)S(1)}, u32[]{:S(2)}, u32[]{:S(2)}) collective-permute-start(bf16[64,1024]{1,0:T(8,128)(2,1)} %get-tuple-element.60), channel_id=1, source_target_pairs={{0,24},{2,26},{4,28},{6,30},{8,16},{10,18},{12,20},{14,22},{16,8},... | collective-permute-start | bytes 393224 | tf_op jit(solution)/shard_map/ppermute | solution.py:410
  8.7 13.7 %collective-permute-start.5 = (bf16[64,1024]{1,0:T(8,128)(2,1)}, bf16[64,1024]{1,0:T(8,128)(2,1)S(1)}, u32[]{:S(2)}, u32[]{:S(2)}) collective-permute-start(bf16[64,1024]{1,0:T(8,128)(2,1)} %get-tuple-element.61), channel_id=1, source_target_pairs={{0,2},{2,0},{4,6},{6,4},{8,10},{10,8},{12,14},{14,12},{16,18},{18,... | collective-permute-start | bytes 393224 | tf_op jit(solution)/shard_map/ppermute | solution.py:410
  10.2 13.5 %collective-permute-start.6 = (bf16[64,1024]{1,0:T(8,128)(2,1)}, bf16[64,1024]{1,0:T(8,128)(2,1)S(1)}, u32[]{:S(2)}, u32[]{:S(2)}) collective-permute-start(bf16[64,1024]{1,0:T(8,128)(2,1)} %get-tuple-element.62), channel_id=1, source_target_pairs={{0,28},{2,30},{4,24},{6,26},{8,20},{10,22},{12,16},{14,18},{16,12}... | collective-permute-start | bytes 393224 | tf_op jit(solution)/shard_map/ppermute | solution.py:410
  11.3 17.5 %collective-permute-start.7 = (bf16[64,1024]{1,0:T(8,128)(2,1)}, bf16[64,1024]{1,0:T(8,128)(2,1)S(1)}, u32[]{:S(2)}, u32[]{:S(2)}) collective-permute-start(bf16[64,1024]{1,0:T(8,128)(2,1)} %get-tuple-element.63), channel_id=1, source_target_pairs={{0,18},{2,16},{4,22},{6,20},{8,26},{10,24},{12,30},{14,28},{16,2},... | collective-permute-start | bytes 393224 | tf_op jit(solution)/shard_map/ppermute | solution.py:410
  17.3 15.1 %collective-permute-start.8 = (bf16[64,1024]{1,0:T(8,128)(2,1)}, bf16[64,1024]{1,0:T(8,128)(2,1)S(1)}, u32[]{:S(2)}, u32[]{:S(2)}) collective-permute-start(bf16[64,1024]{1,0:T(8,128)(2,1)} %get-tuple-element.64), channel_id=1, source_target_pairs={{0,8},{2,10},{4,12},{6,14},{8,0},{10,2},{12,4},{14,6},{16,24},{18,... | collective-permute-start | bytes 393224 | tf_op jit(solution)/shard_map/ppermute | solution.py:410
  20.7 15.1 %collective-permute-start.9 = (bf16[64,1024]{1,0:T(8,128)(2,1)}, bf16[64,1024]{1,0:T(8,128)(2,1)S(1)}, u32[]{:S(2)}, u32[]{:S(2)}) collective-permute-start(bf16[64,1024]{1,0:T(8,128)(2,1)} %get-tuple-element.65), channel_id=1, source_target_pairs={{0,10},{2,8},{4,14},{6,12},{8,2},{10,0},{12,6},{14,4},{16,26},{18,... | collective-permute-start | bytes 393224 | tf_op jit(solution)/shard_map/ppermute | solution.py:410
  22.4 13.4 %collective-permute-start.10 = (bf16[64,1024]{1,0:T(8,128)(2,1)}, bf16[64,1024]{1,0:T(8,128)(2,1)S(1)}, u32[]{:S(2)}, u32[]{:S(2)}) collective-permute-start(bf16[64,1024]{1,0:T(8,128)(2,1)} %get-tuple-element.66), channel_id=1, source_target_pairs={{0,20},{2,22},{4,16},{6,18},{8,28},{10,30},{12,24},{14,26},{16,4},... | collective-permute-start | bytes 393224 | tf_op jit(solution)/shard_map/ppermute | solution.py:410
  23.6 15.1 %collective-permute-start.11 = (bf16[64,1024]{1,0:T(8,128)(2,1)}, bf16[64,1024]{1,0:T(8,128)(2,1)S(1)}, u32[]{:S(2)}, u32[]{:S(2)}) collective-permute-start(bf16[64,1024]{1,0:T(8,128)(2,1)} %get-tuple-element.67), channel_id=1, source_target_pairs={{0,14},{2,12},{4,10},{6,8},{8,6},{10,4},{12,2},{14,0},{16,30},{18,... | collective-permute-start | bytes 393224 | tf_op jit(solution)/shard_map/ppermute | solution.py:410
  28.9 13.1 %collective-permute-start.12 = (bf16[64,1024]{1,0:T(8,128)(2,1)}, bf16[64,1024]{1,0:T(8,128)(2,1)S(1)}, u32[]{:S(2)}, u32[]{:S(2)}) collective-permute-start(bf16[64,1024]{1,0:T(8,128)(2,1)} %get-tuple-element.68), channel_id=1, source_target_pairs={{0,30},{2,28},{4,26},{6,24},{8,22},{10,20},{12,18},{14,16},{16,14}... | collective-permute-start | bytes 393224 | tf_op jit(solution)/shard_map/ppermute | solution.py:410
  32.4 13.8 %collective-permute-start.13 = (bf16[64,1024]{1,0:T(8,128)(2,1)}, bf16[64,1024]{1,0:T(8,128)(2,1)S(1)}, u32[]{:S(2)}, u32[]{:S(2)}) collective-permute-start(bf16[64,1024]{1,0:T(8,128)(2,1)} %get-tuple-element.69), channel_id=1, source_target_pairs={{0,4},{2,6},{4,0},{6,2},{8,12},{10,14},{12,8},{14,10},{16,20},{18,... | collective-permute-start | bytes 393224 | tf_op jit(solution)/shard_map/ppermute | solution.py:410
  35.8 11.1 %collective-permute-start.14 = (bf16[64,1024]{1,0:T(8,128)(2,1)}, bf16[64,1024]{1,0:T(8,128)(2,1)S(1)}, u32[]{:S(2)}, u32[]{:S(2)}) collective-permute-start(bf16[64,1024]{1,0:T(8,128)(2,1)} %get-tuple-element.70), channel_id=1, source_target_pairs={{0,22},{2,20},{4,18},{6,16},{8,30},{10,28},{12,26},{14,24},{16,6},... | collective-permute-start | bytes 393224 | tf_op jit(solution)/shard_map/ppermute | solution.py:410
  35.8 12.6 %collective-permute-start = (bf16[64,1024]{1,0:T(8,128)(2,1)}, bf16[64,1024]{1,0:T(8,128)(2,1)S(1)}, u32[]{:S(2)}, u32[]{:S(2)}) collective-permute-start(bf16[64,1024]{1,0:T(8,128)(2,1)} %get-tuple-element.55), channel_id=1, source_target_pairs={{0,12},{2,14},{4,8},{6,10},{8,4},{10,6},{12,0},{14,2},{16,28},{18,... | collective-permute-start | bytes 393224 | tf_op jit(solution)/shard_map/ppermute | solution.py:410
  38.7 9.6 %collective-permute-start.1 = (bf16[64,1024]{1,0:T(8,128)(2,1)}, bf16[64,1024]{1,0:T(8,128)(2,1)S(1)}, u32[]{:S(2)}, u32[]{:S(2)}) collective-permute-start(bf16[64,1024]{1,0:T(8,128)(2,1)} %get-tuple-element.56), channel_id=1, source_target_pairs={{0,26},{2,24},{4,30},{6,28},{8,18},{10,16},{12,22},{14,20},{16,10}... | collective-permute-start | bytes 393224 | tf_op jit(solution)/shard_map/ppermute | solution.py:410
  42.0 6.4 %collective-permute-start.2 = (bf16[64,1024]{1,0:T(8,128)(2,1)}, bf16[64,1024]{1,0:T(8,128)(2,1)S(1)}, u32[]{:S(2)}, u32[]{:S(2)}) collective-permute-start(bf16[64,1024]{1,0:T(8,128)(2,1)} %get-tuple-element.57), channel_id=1, source_target_pairs={{0,6},{2,4},{4,2},{6,0},{8,14},{10,12},{12,10},{14,8},{16,22},{18,... | collective-permute-start | bytes 393224 | tf_op jit(solution)/shard_map/ppermute | solution.py:410
  46.2 7.7 %collective-permute-start.3 = (bf16[64,1024]{1,0:T(8,128)(2,1)}, bf16[64,1024]{1,0:T(8,128)(2,1)S(1)}, u32[]{:S(2)}, u32[]{:S(2)}) collective-permute-start(bf16[64,1024]{1,0:T(8,128)(2,1)} %get-tuple-element.58), channel_id=1, source_target_pairs={{0,16},{2,18},{4,20},{6,22},{8,24},{10,26},{12,28},{14,30},{16,0},... | collective-permute-start | bytes 393224 | tf_op jit(solution)/shard_map/ppermute | solution.py:410
  46.9 0.9 %copy-start = (bf16[64,1024]{1,0:T(8,128)(2,1)S(1)}, bf16[64,1024]{1,0:T(8,128)(2,1)}, u32[]{:S(2)}) copy-start(bf16[64,1024]{1,0:T(8,128)(2,1)} %get-tuple-element.59.rest_0_.refs_0_) | copy-start | bytes 393220
  47.8 6.8 %copy-start.1 = (bf16[64,1024]{1,0:T(8,128)(2,1)S(1)}, bf16[64,1024]{1,0:T(8,128)(2,1)}, u32[]{:S(2)}) copy-start(bf16[64,1024]{1,0:T(8,128)(2,1)} %get-tuple-element.59.rest_0_.refs_0_) | copy-start | bytes 393220
  54.2 1.4 %collective-permute-start.15 = (bf16[4,128,128]{2,1,0:T(8,128)(2,1)S(1)}, bf16[4,128,128]{2,1,0:T(8,128)(2,1)S(1)}, u32[]{:S(2)}, u32[]{:S(2)}) collective-permute-start(bf16[4,128,128]{2,1,0:T(8,128)(2,1)S(1)} %pick_refs.3.own_ref), channel_id=1, source_target_pairs={{0,1},{1,0},{2,3},{3,2},{4,5},{5,4},{6,7},{7,6},{8,9},{9,8},{10,11... | collective-permute-start | bytes 393224 | tf_op jit(solution)/shard_map/ppermute | solution.py:414

commit v6 on v5

--- a/solution.py
+++ b/solution.py
@@ -17,6 +17,7 @@
 SPECTRA_LIMIT = 66000000
 SHIFTS = (12, 1, 14, 9, 4, 5, 10, 7, 15, 2, 11, 6, 13, 3, 8)
 FIRST = 4
+SECOND = 8
 LATE = 4
 MAX_GAP = 768
 
@@ -282,7 +283,7 @@
     blocks = [(early_ref, at) for at in range(0, early, 256)] + [(late_ref, at) for at in range(0, late, 256)]
     sources = [lax.axis_index("bin") ^ shift for shift in shifts]
     first_half = lax.axis_index("grp") == 0
-    row_bin = lax.broadcasted_iota(jnp.int32, wide_ref.shape[1:], 0) % SUB
+    row_bin = lax.broadcasted_iota(jnp.int32, (2 * SUB, 2 * LANES), 0) % SUB
 
     def copy_out(step, group):
         return pltpu.make_async_copy(
@@ -308,10 +309,11 @@
         for seg in range(segs):
             vr, vi = found[seg]
             at = (seg % 2) * LANES + seg // 2 * 2 * SUB
-            wide_ref[into, at : at + SUB, 0:LANES] = vr
-            wide_ref[into, at : at + SUB, LANES : 2 * LANES] = vi
-            wide_ref[into, at + SUB : at + 2 * SUB, 0:LANES] = -vi
-            wide_ref[into, at + SUB : at + 2 * SUB, LANES : 2 * LANES] = vr
+            here = pl.ds(at, 2 * SUB)
+            wide_ref[into, here, 0:LANES] = jnp.concatenate([vr, -vi], axis=0).astype(jnp.bfloat16)
+            wide_ref[into, here, LANES : 2 * LANES] = jnp.concatenate([vi, vr], axis=0).astype(
+                jnp.bfloat16
+            )
 
     solve_cost = 100 + 6 * 136 + 32 + 8 * 16 + 240 + 8 * 560 + 12 * 120 + 32 + 960
 
@@ -326,9 +328,12 @@
                 def _():
                     copy_out(step, group).wait()
 
+            tiles = wide_ref[group % 2].reshape(-1, 2 * SUB, 2 * LANES)
             weights = jnp.concatenate(
                 [
-                    jnp.where(row_bin == step * pair + k, wide_ref[group % 2], 0.0).astype(jnp.bfloat16)
+                    jnp.where(
+                        (row_bin == step * pair + k)[None], tiles, jnp.zeros_like(tiles)
+                    ).reshape(wide_ref.shape[1:])
                     for k in range(pair)
                 ],
                 axis=1,
@@ -377,7 +382,7 @@
         in_specs=[pl.BlockSpec(memory_space=pltpu.VMEM)] * 4,
         out_specs=pl.BlockSpec(memory_space=pltpu.HBM),
         scratch_shapes=[
-            pltpu.VMEM((2, depth, 2 * LANES), jnp.float32),
+            pltpu.VMEM((2, depth, 2 * LANES), jnp.bfloat16),
             pltpu.VMEM((steps, pair, chans, 2 * LANES), jnp.bfloat16),
             pltpu.SemaphoreType.DMA((steps,)),
         ],
@@ -400,7 +405,7 @@
     index = jnp.concatenate([ref_index, ref_index], axis=1)
     me = lambda: lax.axis_index("bin")
     got = {}
-    for part in (SHIFTS[:FIRST], SHIFTS[FIRST:] + (0,)):
+    for part in (SHIFTS[:FIRST], SHIFTS[FIRST:SECOND], SHIFTS[SECOND:] + (0,)):
         made = spectra_of(
             chan_rows, offsets, table, lambda k, part=part: me() ^ part[k], len(part), True
         )

time: 66.6 us -> 70.5 us (1.059)
  Pallas kernels: 20.9 us -> 23.7 us
  starting transfers between devices: 26.9 us -> 28.6 us
    pallas_call x2 -> x3, Pallas kernels: 8.69 us -> 11.4 us  [spectra_of(): pl.pallas_call(functools.partial(spectra_kernel, dest_of, count), out_sha...]
    ppermute x15, starting transfers between devices: 26.8 us -> 28.5 us  [local_kernels(): got[shift] = lax.ppermute(block, 'bin', pairs) if shift else block]
  transfers between devices with their start and end apart: 16 -> 16, of which waited for: 7 -> 4; matrix products, arithmetic and copies ran while one was open for 0% -> 0% of each run, Pallas kernels for 10% -> 13%
where the time goes in v6:
time: 70.5 us; the launch traced here: 70.3 us
  starting transfers between devices  28.6 us (41%)
  Pallas kernels  23.7 us (34%)
  waiting for transfers between devices  16.9 us (24%)
  local copies, waits for them, and re-layouts  0.92 us (1%)
    ppermute x15, starting transfers between devices, local_kernels(): got[shift] = lax.ppermute(block, 'bin', pairs) if shift else block  28.5 us
    ppermute x15, waiting for transfers between devices, local_kernels(): got[shift] = lax.ppermute(block, 'bin', pairs) if shift else block  16.2 us
    pallas_call x3, Pallas kernels, spectra_of(): pl.pallas_call(functools.partial(spectra_kernel, dest_of, count), out_sha...  11.4 us
    pallas_call x1, Pallas kernels, solve_and_apply(): pl.pallas_call(functools.partial(solve_kernel, shifts), out_shape=jax.Sha...  10.8 us
  transfers between devices with their start and end apart: 16, of which 4 were waited for; matrix products, arithmetic and copies ran while one was open for 0% of the time, Pallas kernels for 13%

profile of v6, /device:TPU:0, one launch (start us, length us, event | category | flops | bytes accessed | tf_op | source)
XLA Modules:
  0.0 70.3 jit_solution(9886838121282911808)
XLA Ops:
  0.0 3.5 %spectra.3 = (bf16[64,1024]{1,0:T(8,128)(2,1)}, bf16[64,1024]{1,0:T(8,128)(2,1)}, bf16[64,1024]{1,0:T(8,128)(2,1)}, bf16[64,1024]{1,0:T(8,128)(2,1)}) custom-call(s32[16]{0:T(128)} %starts_hbm.5, bf16[64,8704]{1,0:T(8,128)(2,1)} %bitcast.1, bf16[16,64,1024]{2,1,0:T(8,128)(2,1)} %constant.2.clone.table_hbm), custom_call_target="tpu_custom_call" | custom-call | flops 536870912 | bytes 1048576 | tf_op jit(solution)/shard_map/spectra/pallas_call | solution.py:123
  3.5 5.1 %collective-permute-start.4 = (bf16[64,1024]{1,0:T(8,128)(2,1)}, bf16[64,1024]{1,0:T(8,128)(2,1)S(1)}, u32[]{:S(2)}, u32[]{:S(2)}) collective-permute-start(bf16[64,1024]{1,0:T(8,128)(2,1)} %get-tuple-element.62), channel_id=1, source_target_pairs={{0,24},{2,26},{4,28},{6,30},{8,16},{10,18},{12,20},{14,22},{16,8},... | collective-permute-start | bytes 393224 | tf_op jit(solution)/shard_map/ppermute | solution.py:415
  8.6 1.5 %collective-permute-start.5 = (bf16[64,1024]{1,0:T(8,128)(2,1)}, bf16[64,1024]{1,0:T(8,128)(2,1)S(1)}, u32[]{:S(2)}, u32[]{:S(2)}) collective-permute-start(bf16[64,1024]{1,0:T(8,128)(2,1)} %get-tuple-element.63), channel_id=1, source_target_pairs={{0,2},{2,0},{4,6},{6,4},{8,10},{10,8},{12,14},{14,12},{16,18},{18,... | collective-permute-start | bytes 393224 | tf_op jit(solution)/shard_map/ppermute | solution.py:415
  10.1 1.2 %collective-permute-start.6 = (bf16[64,1024]{1,0:T(8,128)(2,1)}, bf16[64,1024]{1,0:T(8,128)(2,1)S(1)}, u32[]{:S(2)}, u32[]{:S(2)}) collective-permute-start(bf16[64,1024]{1,0:T(8,128)(2,1)} %get-tuple-element.64), channel_id=1, source_target_pairs={{0,28},{2,30},{4,24},{6,26},{8,20},{10,22},{12,16},{14,18},{16,12}... | collective-permute-start | bytes 393224 | tf_op jit(solution)/shard_map/ppermute | solution.py:415
  11.3 0.8 %collective-permute-start.7 = (bf16[64,1024]{1,0:T(8,128)(2,1)}, bf16[64,1024]{1,0:T(8,128)(2,1)S(1)}, u32[]{:S(2)}, u32[]{:S(2)}) collective-permute-start(bf16[64,1024]{1,0:T(8,128)(2,1)} %get-tuple-element.65), channel_id=1, source_target_pairs={{0,18},{2,16},{4,22},{6,20},{8,26},{10,24},{12,30},{14,28},{16,2},... | collective-permute-start | bytes 393224 | tf_op jit(solution)/shard_map/ppermute | solution.py:415
  12.0 3.5 %spectra.4 = (bf16[64,1024]{1,0:T(8,128)(2,1)}, bf16[64,1024]{1,0:T(8,128)(2,1)}, bf16[64,1024]{1,0:T(8,128)(2,1)}, bf16[64,1024]{1,0:T(8,128)(2,1)}) custom-call(s32[16]{0:T(128)} %starts_hbm.5, bf16[64,8704]{1,0:T(8,128)(2,1)} %bitcast.2, bf16[16,64,1024]{2,1,0:T(8,128)(2,1)} %constant.2.clone.table_hbm), custom_call_target="tpu_custom_call" | custom-call | flops 536870912 | bytes 1048576 | tf_op jit(solution)/shard_map/spectra/pallas_call | solution.py:123
  15.6 0.0 copy-start.2
  15.6 0.0 copy-start.3
  15.6 3.4 %collective-permute-start.8 = (bf16[64,1024]{1,0:T(8,128)(2,1)}, bf16[64,1024]{1,0:T(8,128)(2,1)S(1)}, u32[]{:S(2)}, u32[]{:S(2)}) collective-permute-start(bf16[64,1024]{1,0:T(8,128)(2,1)} %get-tuple-element.66), channel_id=1, source_target_pairs={{0,8},{2,10},{4,12},{6,14},{8,0},{10,2},{12,4},{14,6},{16,24},{18,... | collective-permute-start | bytes 393224 | tf_op jit(solution)/shard_map/ppermute | solution.py:415
  19.0 0.0 collective-permute-done.4.rest_1_.refs_1_
  19.0 3.3 %collective-permute-start.9 = (bf16[64,1024]{1,0:T(8,128)(2,1)}, bf16[64,1024]{1,0:T(8,128)(2,1)S(1)}, u32[]{:S(2)}, u32[]{:S(2)}) collective-permute-start(bf16[64,1024]{1,0:T(8,128)(2,1)} %get-tuple-element.67), channel_id=1, source_target_pairs={{0,10},{2,8},{4,14},{6,12},{8,2},{10,0},{12,6},{14,4},{16,26},{18,... | collective-permute-start | bytes 393224 | tf_op jit(solution)/shard_map/ppermute | solution.py:415
  22.4 4.4 %spectra.5 = (bf16[64,1024]{1,0:T(8,128)(2,1)}, bf16[64,1024]{1,0:T(8,128)(2,1)}, bf16[64,1024]{1,0:T(8,128)(2,1)}, bf16[64,1024]{1,0:T(8,128)(2,1)}, bf16[64,10...) custom-call(s32[16]{0:T(128)} %starts_hbm.5, ...), custom_call_target="tpu_custom_call" | custom-call | flops 1073741824 | bytes 2097152 | tf_op jit(solution)/shard_map/spectra/pallas_call | solution.py:123
  26.7 0.0 collective-permute-done.5.rest_2_.refs_2_
  26.8 1.3 %collective-permute-start.10 = (bf16[64,1024]{1,0:T(8,128)(2,1)}, bf16[64,1024]{1,0:T(8,128)(2,1)S(1)}, u32[]{:S(2)}, u32[]{:S(2)}) collective-permute-start(bf16[64,1024]{1,0:T(8,128)(2,1)} %get-tuple-element.68), channel_id=1, source_target_pairs={{0,20},{2,22},{4,16},{6,18},{8,28},{10,30},{12,24},{14,26},{16,4},... | collective-permute-start | bytes 393224 | tf_op jit(solution)/shard_map/ppermute | solution.py:415
  28.1 0.0 collective-permute-done.6.rest_3_.refs_3_
  28.1 0.0 copy-done.2
  28.1 2.5 %collective-permute-start.11 = (bf16[64,1024]{1,0:T(8,128)(2,1)S(1)}, bf16[64,1024]{1,0:T(8,128)(2,1)S(1)}, u32[]{:S(2)}, u32[]{:S(2)}) collective-permute-start(bf16[64,1024]{1,0:T(8,128)(2,1)S(1)} %copy-done.2), channel_id=1, source_target_pairs={{0,14},{2,12},{4,10},{6,8},{8,6},{10,4},{12,2},{14,0},{16,30},{18,... | collective-permute-start | bytes 393224 | tf_op jit(solution)/shard_map/ppermute | solution.py:415
  30.5 0.0 collective-permute-done.7.rest_4_.refs_4_
  30.6 3.4 %collective-permute-start.12 = (bf16[64,1024]{1,0:T(8,128)(2,1)}, bf16[64,1024]{1,0:T(8,128)(2,1)S(1)}, u32[]{:S(2)}, u32[]{:S(2)}) collective-permute-start(bf16[64,1024]{1,0:T(8,128)(2,1)} %get-tuple-element.70), channel_id=1, source_target_pairs={{0,30},{2,28},{4,26},{6,24},{8,22},{10,20},{12,18},{14,16},{16,14}... | collective-permute-start | bytes 393224 | tf_op jit(solution)/shard_map/ppermute | solution.py:415
  34.0 0.0 collective-permute-done.8.rest_5_.refs_5_
  34.0 0.5 collective-permute-start.13
  34.5 0.0 collective-permute-done.9.rest_6_.refs_6_
  34.5 1.3 %collective-permute-start.14 = (bf16[64,1024]{1,0:T(8,128)(2,1)}, bf16[64,1024]{1,0:T(8,128)(2,1)S(1)}, u32[]{:S(2)}, u32[]{:S(2)}) collective-permute-start(bf16[64,1024]{1,0:T(8,128)(2,1)} %get-tuple-element.72), channel_id=1, source_target_pairs={{0,22},{2,20},{4,18},{6,16},{8,30},{10,28},{12,26},{14,24},{16,6},... | collective-permute-start | bytes 393224 | tf_op jit(solution)/shard_map/ppermute | solution.py:415
  35.8 4.8 %collective-permute-done.10.rest_7_.refs_7_ = bf16[64,1024]{1,0:T(8,128)(2,1)S(1)} collective-permute-done((bf16[64,1024]{1,0:T(8,128)(2,1)}, bf16[64,1024]{1,0:T(8,128)(2,1)S(1)}, u32[]{:S(2)}, u32[]{:S(2)}) %collective-permute-start.10) | collective-permute-done | bytes 131104 | tf_op jit(solution)/shard_map/ppermute | solution.py:415
  40.5 0.0 collective-permute-start
  40.5 0.0 collective-permute-done.11.rest_8_.refs_8_
  40.5 1.5 %collective-permute-start.1 = (bf16[64,1024]{1,0:T(8,128)(2,1)}, bf16[64,1024]{1,0:T(8,128)(2,1)S(1)}, u32[]{:S(2)}, u32[]{:S(2)}) collective-permute-start(bf16[64,1024]{1,0:T(8,128)(2,1)} %get-tuple-element.58), channel_id=1, source_target_pairs={{0,26},{2,24},{4,30},{6,28},{8,18},{10,16},{12,22},{14,20},{16,10}... | collective-permute-start | bytes 393224 | tf_op jit(solution)/shard_map/ppermute | solution.py:415
  42.1 0.0 collective-permute-done.12.rest_9_.refs_9_
  42.1 2.7 %collective-permute-start.2 = (bf16[64,1024]{1,0:T(8,128)(2,1)}, bf16[64,1024]{1,0:T(8,128)(2,1)S(1)}, u32[]{:S(2)}, u32[]{:S(2)}) collective-permute-start(bf16[64,1024]{1,0:T(8,128)(2,1)} %get-tuple-element.59), channel_id=1, source_target_pairs={{0,6},{2,4},{4,2},{6,0},{8,14},{10,12},{12,10},{14,8},{16,22},{18,... | collective-permute-start | bytes 393224 | tf_op jit(solution)/shard_map/ppermute | solution.py:415
  44.7 5.6 %collective-permute-done.13.rest_10_.refs_10_ = bf16[64,1024]{1,0:T(8,128)(2,1)S(1)} collective-permute-done((bf16[64,1024]{1,0:T(8,128)(2,1)}, bf16[64,1024]{1,0:T(8,128)(2,1)S(1)}, u32[]{:S(2)}, u32[]{:S(2)}) %collective-permute-start.13) | collective-permute-done | bytes 131104 | tf_op jit(solution)/shard_map/ppermute | solution.py:415
  50.3 0.1 collective-permute-start.3
  50.4 0.0 copy-done.3
  50.4 0.1 pad_add_fusion.index_ref
  50.4 0.0 collective-permute-done.14.rest_11_.refs_11_
  50.4 0.0 copy-start
  50.4 0.9 %copy-done = bf16[64,1024]{1,0:T(8,128)(2,1)S(1)} copy-done((bf16[64,1024]{1,0:T(8,128)(2,1)S(1)}, bf16[64,1024]{1,0:T(8,128)(2,1)}, u32[]{:S(2)}) %copy-start) | copy-done | bytes 131096
  51.3 0.6 pick_refs.2.rest_4_
  51.9 0.0 collective-permute-done.rest_0_.refs_0_
  51.9 0.0 collective-permute-done.1.rest_1_.refs_1_
  51.9 0.0 collective-permute-done.2.rest_2_.refs_2_
  52.0 5.8 %collective-permute-done.3.rest_3_.refs_3_ = bf16[64,1024]{1,0:T(8,128)(2,1)S(1)} collective-permute-done((bf16[64,1024]{1,0:T(8,128)(2,1)}, bf16[64,1024]{1,0:T(8,128)(2,1)S(1)}, u32[]{:S(2)}, u32[]{:S(2)}) %collective-permute-start.3) | collective-permute-done | bytes 131104 | tf_op jit(solution)/shard_map/ppermute | solution.py:415
  57.8 0.3 pick_refs.3.own_ref
  58.1 0.1 collective-permute-start.15
  58.2 0.2 turn.3.late_ref
  58.4 0.0 copy-done.1
  58.4 0.5 turn.2.early_ref
  58.8 0.7 collective-permute-done.15.other_ref
  59.5 10.8 %solve_apply.1 = bf16[32,1024,256]{2,1,0:T(8,128)(2,1)} custom-call(bf16[4,128,128]{2,1,0:T(8,128)(2,1)S(1)} %pick_refs.3.own_ref, bf16[4,128,128]{2,1,0:T(8,128)(2,1)S(1)} %collective-permute-done.15.other_ref, bf16[4,768,256]{2,1,0:T(8,128)(2,1)S(1)} %turn.2.early_ref, bf16[4,256,256]{2,1,0:T(8,128)(2,1)S(1)} %turn.3.late_ref), custom_call_target="tpu_custom_call" | custom-call | flops 4294967296 | bytes 16777216 | tf_op jit(solution)/shard_map/solve_apply/pallas_call | solution.py:379
  (1 shorter events, 0.0 us)
Async XLA Ops:
  3.5 15.5 %collective-permute-start.4 = (bf16[64,1024]{1,0:T(8,128)(2,1)}, bf16[64,1024]{1,0:T(8,128)(2,1)S(1)}, u32[]{:S(2)}, u32[]{:S(2)}) collective-permute-start(bf16[64,1024]{1,0:T(8,128)(2,1)} %get-tuple-element.62), channel_id=1, source_target_pairs={{0,24},{2,26},{4,28},{6,30},{8,16},{10,18},{12,20},{14,22},{16,8},... | collective-permute-start | bytes 393224 | tf_op jit(solution)/shard_map/ppermute | solution.py:415
  8.6 18.1 %collective-permute-start.5 = (bf16[64,1024]{1,0:T(8,128)(2,1)}, bf16[64,1024]{1,0:T(8,128)(2,1)S(1)}, u32[]{:S(2)}, u32[]{:S(2)}) collective-permute-start(bf16[64,1024]{1,0:T(8,128)(2,1)} %get-tuple-element.63), channel_id=1, source_target_pairs={{0,2},{2,0},{4,6},{6,4},{8,10},{10,8},{12,14},{14,12},{16,18},{18,... | collective-permute-start | bytes 393224 | tf_op jit(solution)/shard_map/ppermute | solution.py:415
  10.1 18.0 %collective-permute-start.6 = (bf16[64,1024]{1,0:T(8,128)(2,1)}, bf16[64,1024]{1,0:T(8,128)(2,1)S(1)}, u32[]{:S(2)}, u32[]{:S(2)}) collective-permute-start(bf16[64,1024]{1,0:T(8,128)(2,1)} %get-tuple-element.64), channel_id=1, source_target_pairs={{0,28},{2,30},{4,24},{6,26},{8,20},{10,22},{12,16},{14,18},{16,12}... | collective-permute-start | bytes 393224 | tf_op jit(solution)/shard_map/ppermute | solution.py:415
  11.3 19.3 %collective-permute-start.7 = (bf16[64,1024]{1,0:T(8,128)(2,1)}, bf16[64,1024]{1,0:T(8,128)(2,1)S(1)}, u32[]{:S(2)}, u32[]{:S(2)}) collective-permute-start(bf16[64,1024]{1,0:T(8,128)(2,1)} %get-tuple-element.65), channel_id=1, source_target_pairs={{0,18},{2,16},{4,22},{6,20},{8,26},{10,24},{12,30},{14,28},{16,2},... | collective-permute-start | bytes 393224 | tf_op jit(solution)/shard_map/ppermute | solution.py:415
  15.6 12.5 %copy-start.2 = (bf16[64,1024]{1,0:T(8,128)(2,1)S(1)}, bf16[64,1024]{1,0:T(8,128)(2,1)}, u32[]{:S(2)}) copy-start(bf16[64,1024]{1,0:T(8,128)(2,1)} %get-tuple-element.69) | copy-start | bytes 393220
  15.6 34.8 %copy-start.3 = (s32[1,64]{1,0:T(1,128)S(1)}, s32[1,64]{1,0:T(1,128)}, u32[]{:S(2)}) copy-start(s32[1,64]{1,0:T(1,128)} %param.5) | copy-start | bytes 772
  15.6 18.4 %collective-permute-start.8 = (bf16[64,1024]{1,0:T(8,128)(2,1)}, bf16[64,1024]{1,0:T(8,128)(2,1)S(1)}, u32[]{:S(2)}, u32[]{:S(2)}) collective-permute-start(bf16[64,1024]{1,0:T(8,128)(2,1)} %get-tuple-element.66), channel_id=1, source_target_pairs={{0,8},{2,10},{4,12},{6,14},{8,0},{10,2},{12,4},{14,6},{16,24},{18,... | collective-permute-start | bytes 393224 | tf_op jit(solution)/shard_map/ppermute | solution.py:415
  19.0 15.5 %collective-permute-start.9 = (bf16[64,1024]{1,0:T(8,128)(2,1)}, bf16[64,1024]{1,0:T(8,128)(2,1)S(1)}, u32[]{:S(2)}, u32[]{:S(2)}) collective-permute-start(bf16[64,1024]{1,0:T(8,128)(2,1)} %get-tuple-element.67), channel_id=1, source_target_pairs={{0,10},{2,8},{4,14},{6,12},{8,2},{10,0},{12,6},{14,4},{16,26},{18,... | collective-permute-start | bytes 393224 | tf_op jit(solution)/shard_map/ppermute | solution.py:415
  26.8 13.8 %collective-permute-start.10 = (bf16[64,1024]{1,0:T(8,128)(2,1)}, bf16[64,1024]{1,0:T(8,128)(2,1)S(1)}, u32[]{:S(2)}, u32[]{:S(2)}) collective-permute-start(bf16[64,1024]{1,0:T(8,128)(2,1)} %get-tuple-element.68), channel_id=1, source_target_pairs={{0,20},{2,22},{4,16},{6,18},{8,28},{10,30},{12,24},{14,26},{16,4},... | collective-permute-start | bytes 393224 | tf_op jit(solution)/shard_map/ppermute | solution.py:415
  28.1 12.5 %collective-permute-start.11 = (bf16[64,1024]{1,0:T(8,128)(2,1)S(1)}, bf16[64,1024]{1,0:T(8,128)(2,1)S(1)}, u32[]{:S(2)}, u32[]{:S(2)}) collective-permute-start(bf16[64,1024]{1,0:T(8,128)(2,1)S(1)} %copy-done.2), channel_id=1, source_target_pairs={{0,14},{2,12},{4,10},{6,8},{8,6},{10,4},{12,2},{14,0},{16,30},{18,... | collective-permute-start | bytes 393224 | tf_op jit(solution)/shard_map/ppermute | solution.py:415
  30.6 11.5 %collective-permute-start.12 = (bf16[64,1024]{1,0:T(8,128)(2,1)}, bf16[64,1024]{1,0:T(8,128)(2,1)S(1)}, u32[]{:S(2)}, u32[]{:S(2)}) collective-permute-start(bf16[64,1024]{1,0:T(8,128)(2,1)} %get-tuple-element.70), channel_id=1, source_target_pairs={{0,30},{2,28},{4,26},{6,24},{8,22},{10,20},{12,18},{14,16},{16,14}... | collective-permute-start | bytes 393224 | tf_op jit(solution)/shard_map/ppermute | solution.py:415
  34.0 16.3 %collective-permute-start.13 = (bf16[64,1024]{1,0:T(8,128)(2,1)}, bf16[64,1024]{1,0:T(8,128)(2,1)S(1)}, u32[]{:S(2)}, u32[]{:S(2)}) collective-permute-start(bf16[64,1024]{1,0:T(8,128)(2,1)} %get-tuple-element.71), channel_id=1, source_target_pairs={{0,4},{2,6},{4,0},{6,2},{8,12},{10,14},{12,8},{14,10},{16,20},{18,... | collective-permute-start | bytes 393224 | tf_op jit(solution)/shard_map/ppermute | solution.py:415
  34.5 15.9 %collective-permute-start.14 = (bf16[64,1024]{1,0:T(8,128)(2,1)}, bf16[64,1024]{1,0:T(8,128)(2,1)S(1)}, u32[]{:S(2)}, u32[]{:S(2)}) collective-permute-start(bf16[64,1024]{1,0:T(8,128)(2,1)} %get-tuple-element.72), channel_id=1, source_target_pairs={{0,22},{2,20},{4,18},{6,16},{8,30},{10,28},{12,26},{14,24},{16,6},... | collective-permute-start | bytes 393224 | tf_op jit(solution)/shard_map/ppermute | solution.py:415
  40.5 11.4 %collective-permute-start = (bf16[64,1024]{1,0:T(8,128)(2,1)}, bf16[64,1024]{1,0:T(8,128)(2,1)S(1)}, u32[]{:S(2)}, u32[]{:S(2)}) collective-permute-start(bf16[64,1024]{1,0:T(8,128)(2,1)} %get-tuple-element.57), channel_id=1, source_target_pairs={{0,12},{2,14},{4,8},{6,10},{8,4},{10,6},{12,0},{14,2},{16,28},{18,... | collective-permute-start | bytes 393224 | tf_op jit(solution)/shard_map/ppermute | solution.py:415
  40.5 11.4 %collective-permute-start.1 = (bf16[64,1024]{1,0:T(8,128)(2,1)}, bf16[64,1024]{1,0:T(8,128)(2,1)S(1)}, u32[]{:S(2)}, u32[]{:S(2)}) collective-permute-start(bf16[64,1024]{1,0:T(8,128)(2,1)} %get-tuple-element.58), channel_id=1, source_target_pairs={{0,26},{2,24},{4,30},{6,28},{8,18},{10,16},{12,22},{14,20},{16,10}... | collective-permute-start | bytes 393224 | tf_op jit(solution)/shard_map/ppermute | solution.py:415
  42.1 9.9 %collective-permute-start.2 = (bf16[64,1024]{1,0:T(8,128)(2,1)}, bf16[64,1024]{1,0:T(8,128)(2,1)S(1)}, u32[]{:S(2)}, u32[]{:S(2)}) collective-permute-start(bf16[64,1024]{1,0:T(8,128)(2,1)} %get-tuple-element.59), channel_id=1, source_target_pairs={{0,6},{2,4},{4,2},{6,0},{8,14},{10,12},{12,10},{14,8},{16,22},{18,... | collective-permute-start | bytes 393224 | tf_op jit(solution)/shard_map/ppermute | solution.py:415
  50.3 7.5 %collective-permute-start.3 = (bf16[64,1024]{1,0:T(8,128)(2,1)}, bf16[64,1024]{1,0:T(8,128)(2,1)S(1)}, u32[]{:S(2)}, u32[]{:S(2)}) collective-permute-start(bf16[64,1024]{1,0:T(8,128)(2,1)} %get-tuple-element.60), channel_id=1, source_target_pairs={{0,16},{2,18},{4,20},{6,22},{8,24},{10,26},{12,28},{14,30},{16,0},... | collective-permute-start | bytes 393224 | tf_op jit(solution)/shard_map/ppermute | solution.py:415
  50.4 0.9 %copy-start = (bf16[64,1024]{1,0:T(8,128)(2,1)S(1)}, bf16[64,1024]{1,0:T(8,128)(2,1)}, u32[]{:S(2)}) copy-start(bf16[64,1024]{1,0:T(8,128)(2,1)} %get-tuple-element.61.rest_0_.refs_0_) | copy-start | bytes 393220
  51.3 7.0 %copy-start.1 = (bf16[64,1024]{1,0:T(8,128)(2,1)S(1)}, bf16[64,1024]{1,0:T(8,128)(2,1)}, u32[]{:S(2)}) copy-start(bf16[64,1024]{1,0:T(8,128)(2,1)} %get-tuple-element.61.rest_0_.refs_0_) | copy-start | bytes 393220
  58.1 1.4 %collective-permute-start.15 = (bf16[4,128,128]{2,1,0:T(8,128)(2,1)S(1)}, bf16[4,128,128]{2,1,0:T(8,128)(2,1)S(1)}, u32[]{:S(2)}, u32[]{:S(2)}) collective-permute-start(bf16[4,128,128]{2,1,0:T(8,128)(2,1)S(1)} %pick_refs.3.own_ref), channel_id=1, source_target_pairs={{0,1},{1,0},{2,3},{3,2},{4,5},{5,4},{6,7},{7,6},{8,9},{9,8},{10,11... | collective-permute-start | bytes 393224 | tf_op jit(solution)/shard_map/ppermute | solution.py:419

commit v7 on v6

--- a/solution.py
+++ b/solution.py
@@ -17,7 +17,6 @@
 SPECTRA_LIMIT = 66000000
 SHIFTS = (12, 1, 14, 9, 4, 5, 10, 7, 15, 2, 11, 6, 13, 3, 8)
 FIRST = 4
-SECOND = 8
 LATE = 4
 MAX_GAP = 768
 
@@ -405,7 +404,7 @@
     index = jnp.concatenate([ref_index, ref_index], axis=1)
     me = lambda: lax.axis_index("bin")
     got = {}
-    for part in (SHIFTS[:FIRST], SHIFTS[FIRST:SECOND], SHIFTS[SECOND:] + (0,)):
+    for part in (SHIFTS[:FIRST], SHIFTS[FIRST:] + (0,)):
         made = spectra_of(
             chan_rows, offsets, table, lambda k, part=part: me() ^ part[k], len(part), True
         )

time: 70.5 us -> 66.5 us (0.943)
  Pallas kernels: 23.7 us -> 20.9 us
  starting transfers between devices: 28.6 us -> 26.9 us
    pallas_call x3 -> x2, Pallas kernels: 11.4 us -> 8.68 us  [spectra_of(): pl.pallas_call(functools.partial(spectra_kernel, dest_of, count), out_sha...]
    ppermute x15, starting transfers between devices: 28.5 us -> 26.8 us  [local_kernels(): got[shift] = lax.ppermute(block, 'bin', pairs) if shift else block]
  transfers between devices with their start and end apart: 16 -> 16, of which waited for: 4 -> 7; matrix products, arithmetic and copies ran while one was open for 0% -> 0% of each run, Pallas kernels for 13% -> 10%
where the time goes in v7:
time: 66.5 us; the launch traced here: 66.3 us
  starting transfers between devices  26.9 us (40%)
  Pallas kernels  20.9 us (31%)
  waiting for transfers between devices  17.5 us (26%)
  local copies, waits for them, and re-layouts  0.91 us (1%)
    ppermute x15, starting transfers between devices, local_kernels(): got[shift] = lax.ppermute(block, 'bin', pairs) if shift else block  26.8 us
    ppermute x15, waiting for transfers between devices, local_kernels(): got[shift] = lax.ppermute(block, 'bin', pairs) if shift else block  16.8 us
    pallas_call x1, Pallas kernels, solve_and_apply(): pl.pallas_call(functools.partial(solve_kernel, shifts), out_shape=jax.Sha...  10.7 us
    pallas_call x2, Pallas kernels, spectra_of(): pl.pallas_call(functools.partial(spectra_kernel, dest_of, count), out_sha...  8.68 us
  transfers between devices with their start and end apart: 16, of which 7 were waited for; matrix products, arithmetic and copies ran while one was open for 0% of the time, Pallas kernels for 10%

profile of v7, /device:TPU:0, one launch (start us, length us, event | category | flops | bytes accessed | tf_op | source)
XLA Modules:
  0.0 66.3 jit_solution(2477300079333973079)
XLA Ops:
  0.0 3.5 %spectra.2 = (bf16[64,1024]{1,0:T(8,128)(2,1)}, bf16[64,1024]{1,0:T(8,128)(2,1)}, bf16[64,1024]{1,0:T(8,128)(2,1)}, bf16[64,1024]{1,0:T(8,128)(2,1)}) custom-call(s32[16]{0:T(128)} %starts_hbm.3, bf16[64,8704]{1,0:T(8,128)(2,1)} %bitcast.1, bf16[16,64,1024]{2,1,0:T(8,128)(2,1)} %constant.2.clone.table_hbm), custom_call_target="tpu_custom_call" | custom-call | flops 536870912 | bytes 1048576 | tf_op jit(solution)/shard_map/spectra/pallas_call | solution.py:122
  3.5 0.0 copy-start.2
  3.5 5.1 %collective-permute-start.4 = (bf16[64,1024]{1,0:T(8,128)(2,1)}, bf16[64,1024]{1,0:T(8,128)(2,1)S(1)}, u32[]{:S(2)}, u32[]{:S(2)}) collective-permute-start(bf16[64,1024]{1,0:T(8,128)(2,1)} %get-tuple-element.60), channel_id=1, source_target_pairs={{0,24},{2,26},{4,28},{6,30},{8,16},{10,18},{12,20},{14,22},{16,8},... | collective-permute-start | bytes 393224 | tf_op jit(solution)/shard_map/ppermute | solution.py:414
  8.7 1.5 %collective-permute-start.5 = (bf16[64,1024]{1,0:T(8,128)(2,1)}, bf16[64,1024]{1,0:T(8,128)(2,1)S(1)}, u32[]{:S(2)}, u32[]{:S(2)}) collective-permute-start(bf16[64,1024]{1,0:T(8,128)(2,1)} %get-tuple-element.61), channel_id=1, source_target_pairs={{0,2},{2,0},{4,6},{6,4},{8,10},{10,8},{12,14},{14,12},{16,18},{18,... | collective-permute-start | bytes 393224 | tf_op jit(solution)/shard_map/ppermute | solution.py:414
  10.2 1.2 %collective-permute-start.6 = (bf16[64,1024]{1,0:T(8,128)(2,1)}, bf16[64,1024]{1,0:T(8,128)(2,1)S(1)}, u32[]{:S(2)}, u32[]{:S(2)}) collective-permute-start(bf16[64,1024]{1,0:T(8,128)(2,1)} %get-tuple-element.62), channel_id=1, source_target_pairs={{0,28},{2,30},{4,24},{6,26},{8,20},{10,22},{12,16},{14,18},{16,12}... | collective-permute-start | bytes 393224 | tf_op jit(solution)/shard_map/ppermute | solution.py:414
  11.3 0.8 %collective-permute-start.7 = (bf16[64,1024]{1,0:T(8,128)(2,1)}, bf16[64,1024]{1,0:T(8,128)(2,1)S(1)}, u32[]{:S(2)}, u32[]{:S(2)}) collective-permute-start(bf16[64,1024]{1,0:T(8,128)(2,1)} %get-tuple-element.63), channel_id=1, source_target_pairs={{0,18},{2,16},{4,22},{6,20},{8,26},{10,24},{12,30},{14,28},{16,2},... | collective-permute-start | bytes 393224 | tf_op jit(solution)/shard_map/ppermute | solution.py:414
  12.1 5.2 %spectra.3 = (bf16[64,1024]{1,0:T(8,128)(2,1)}, bf16[64,1024]{1,0:T(8,128)(2,1)}, bf16[64,1024]{1,0:T(8,128)(2,1)}, bf16[64,1024]{1,0:T(8,128)(2,1)}, bf16[64,10...) custom-call(s32[16]{0:T(128)} %starts_hbm.3, ...), custom_call_target="tpu_custom_call" | custom-call | flops 1610612736 | bytes 3145728 | tf_op jit(solution)/shard_map/spectra/pallas_call | solution.py:122
  17.3 3.4 %collective-permute-start.8 = (bf16[64,1024]{1,0:T(8,128)(2,1)}, bf16[64,1024]{1,0:T(8,128)(2,1)S(1)}, u32[]{:S(2)}, u32[]{:S(2)}) collective-permute-start(bf16[64,1024]{1,0:T(8,128)(2,1)} %get-tuple-element.64), channel_id=1, source_target_pairs={{0,8},{2,10},{4,12},{6,14},{8,0},{10,2},{12,4},{14,6},{16,24},{18,... | collective-permute-start | bytes 393224 | tf_op jit(solution)/shard_map/ppermute | solution.py:414
  20.7 0.0 collective-permute-done.4.rest_1_.refs_1_
  20.7 1.7 %collective-permute-start.9 = (bf16[64,1024]{1,0:T(8,128)(2,1)}, bf16[64,1024]{1,0:T(8,128)(2,1)S(1)}, u32[]{:S(2)}, u32[]{:S(2)}) collective-permute-start(bf16[64,1024]{1,0:T(8,128)(2,1)} %get-tuple-element.65), channel_id=1, source_target_pairs={{0,10},{2,8},{4,14},{6,12},{8,2},{10,0},{12,6},{14,4},{16,26},{18,... | collective-permute-start | bytes 393224 | tf_op jit(solution)/shard_map/ppermute | solution.py:414
  22.4 0.0 collective-permute-done.5.rest_2_.refs_2_
  22.4 1.2 %collective-permute-start.10 = (bf16[64,1024]{1,0:T(8,128)(2,1)}, bf16[64,1024]{1,0:T(8,128)(2,1)S(1)}, u32[]{:S(2)}, u32[]{:S(2)}) collective-permute-start(bf16[64,1024]{1,0:T(8,128)(2,1)} %get-tuple-element.66), channel_id=1, source_target_pairs={{0,20},{2,22},{4,16},{6,18},{8,28},{10,30},{12,24},{14,26},{16,4},... | collective-permute-start | bytes 393224 | tf_op jit(solution)/shard_map/ppermute | solution.py:414
  23.6 0.0 collective-permute-done.6.rest_3_.refs_3_
  23.6 2.5 %collective-permute-start.11 = (bf16[64,1024]{1,0:T(8,128)(2,1)}, bf16[64,1024]{1,0:T(8,128)(2,1)S(1)}, u32[]{:S(2)}, u32[]{:S(2)}) collective-permute-start(bf16[64,1024]{1,0:T(8,128)(2,1)} %get-tuple-element.67), channel_id=1, source_target_pairs={{0,14},{2,12},{4,10},{6,8},{8,6},{10,4},{12,2},{14,0},{16,30},{18,... | collective-permute-start | bytes 393224 | tf_op jit(solution)/shard_map/ppermute | solution.py:414
  26.1 2.7 %collective-permute-done.7.rest_4_.refs_4_ = bf16[64,1024]{1,0:T(8,128)(2,1)S(1)} collective-permute-done((bf16[64,1024]{1,0:T(8,128)(2,1)}, bf16[64,1024]{1,0:T(8,128)(2,1)S(1)}, u32[]{:S(2)}, u32[]{:S(2)}) %collective-permute-start.7) | collective-permute-done | bytes 131104 | tf_op jit(solution)/shard_map/ppermute | solution.py:414
  28.9 3.5 %collective-permute-start.12 = (bf16[64,1024]{1,0:T(8,128)(2,1)}, bf16[64,1024]{1,0:T(8,128)(2,1)S(1)}, u32[]{:S(2)}, u32[]{:S(2)}) collective-permute-start(bf16[64,1024]{1,0:T(8,128)(2,1)} %get-tuple-element.68), channel_id=1, source_target_pairs={{0,30},{2,28},{4,26},{6,24},{8,22},{10,20},{12,18},{14,16},{16,14}... | collective-permute-start | bytes 393224 | tf_op jit(solution)/shard_map/ppermute | solution.py:414
  32.4 0.0 collective-permute-done.8.rest_5_.refs_5_
  32.4 0.2 collective-permute-start.13
  32.6 3.1 %collective-permute-done.9.rest_6_.refs_6_ = bf16[64,1024]{1,0:T(8,128)(2,1)S(1)} collective-permute-done((bf16[64,1024]{1,0:T(8,128)(2,1)}, bf16[64,1024]{1,0:T(8,128)(2,1)S(1)}, u32[]{:S(2)}, u32[]{:S(2)}) %collective-permute-start.9) | collective-permute-done | bytes 131104 | tf_op jit(solution)/shard_map/ppermute | solution.py:414
  35.8 0.0 collective-permute-start.14
  35.8 0.0 collective-permute-done.10.rest_7_.refs_7_
  35.8 1.9 %collective-permute-start = (bf16[64,1024]{1,0:T(8,128)(2,1)}, bf16[64,1024]{1,0:T(8,128)(2,1)S(1)}, u32[]{:S(2)}, u32[]{:S(2)}) collective-permute-start(bf16[64,1024]{1,0:T(8,128)(2,1)} %get-tuple-element.55), channel_id=1, source_target_pairs={{0,12},{2,14},{4,8},{6,10},{8,4},{10,6},{12,0},{14,2},{16,28},{18,... | collective-permute-start | bytes 393224 | tf_op jit(solution)/shard_map/ppermute | solution.py:414
  37.6 1.1 %collective-permute-done.11.rest_8_.refs_8_ = bf16[64,1024]{1,0:T(8,128)(2,1)S(1)} collective-permute-done((bf16[64,1024]{1,0:T(8,128)(2,1)}, bf16[64,1024]{1,0:T(8,128)(2,1)S(1)}, u32[]{:S(2)}, u32[]{:S(2)}) %collective-permute-start.11) | collective-permute-done | bytes 131104 | tf_op jit(solution)/shard_map/ppermute | solution.py:414
  38.7 3.2 %collective-permute-start.1 = (bf16[64,1024]{1,0:T(8,128)(2,1)}, bf16[64,1024]{1,0:T(8,128)(2,1)S(1)}, u32[]{:S(2)}, u32[]{:S(2)}) collective-permute-start(bf16[64,1024]{1,0:T(8,128)(2,1)} %get-tuple-element.56), channel_id=1, source_target_pairs={{0,26},{2,24},{4,30},{6,28},{8,18},{10,16},{12,22},{14,20},{16,10}... | collective-permute-start | bytes 393224 | tf_op jit(solution)/shard_map/ppermute | solution.py:414
  41.9 0.0 collective-permute-done.12.rest_9_.refs_9_
  41.9 0.3 collective-permute-start.2
  42.2 3.9 %collective-permute-done.13.rest_10_.refs_10_ = bf16[64,1024]{1,0:T(8,128)(2,1)S(1)} collective-permute-done((bf16[64,1024]{1,0:T(8,128)(2,1)}, bf16[64,1024]{1,0:T(8,128)(2,1)S(1)}, u32[]{:S(2)}, u32[]{:S(2)}) %collective-permute-start.13) | collective-permute-done | bytes 131104 | tf_op jit(solution)/shard_map/ppermute | solution.py:414
  46.2 0.3 collective-permute-start.3
  46.5 0.0 copy-done.2
  46.5 0.1 pad_add_fusion.index_ref
  46.5 0.3 collective-permute-done.14.rest_11_.refs_11_
  46.9 0.0 copy-start
  46.9 0.9 %copy-done = bf16[64,1024]{1,0:T(8,128)(2,1)S(1)} copy-done((bf16[64,1024]{1,0:T(8,128)(2,1)S(1)}, bf16[64,1024]{1,0:T(8,128)(2,1)}, u32[]{:S(2)}) %copy-start) | copy-done | bytes 131096
  47.8 0.0 copy-start.1
  47.8 0.6 pick_refs.2.rest_4_
  48.4 0.0 collective-permute-done.rest_0_.refs_0_
  48.4 0.0 collective-permute-done.1.rest_1_.refs_1_
  48.4 0.0 collective-permute-done.2.rest_2_.refs_2_
  48.4 5.6 %collective-permute-done.3.rest_3_.refs_3_ = bf16[64,1024]{1,0:T(8,128)(2,1)S(1)} collective-permute-done((bf16[64,1024]{1,0:T(8,128)(2,1)}, bf16[64,1024]{1,0:T(8,128)(2,1)S(1)}, u32[]{:S(2)}, u32[]{:S(2)}) %collective-permute-start.3) | collective-permute-done | bytes 131104 | tf_op jit(solution)/shard_map/ppermute | solution.py:414
  53.9 0.3 pick_refs.3.own_ref
  54.2 0.1 collective-permute-start.15
  54.3 0.2 turn.3.late_ref
  54.5 0.0 copy-done.1
  54.5 0.5 turn.2.early_ref
  55.0 0.7 collective-permute-done.15.other_ref
  55.7 10.7 %solve_apply.1 = bf16[32,1024,256]{2,1,0:T(8,128)(2,1)} custom-call(bf16[4,128,128]{2,1,0:T(8,128)(2,1)S(1)} %pick_refs.3.own_ref, bf16[4,128,128]{2,1,0:T(8,128)(2,1)S(1)} %collective-permute-done.15.other_ref, bf16[4,768,256]{2,1,0:T(8,128)(2,1)S(1)} %turn.2.early_ref, bf16[4,256,256]{2,1,0:T(8,128)(2,1)S(1)} %turn.3.late_ref), custom_call_target="tpu_custom_call" | custom-call | flops 4294967296 | bytes 16777216 | tf_op jit(solution)/shard_map/solve_apply/pallas_call | solution.py:378
Async XLA Ops:
  3.5 42.9 %copy-start.2 = (s32[1,64]{1,0:T(1,128)S(1)}, s32[1,64]{1,0:T(1,128)}, u32[]{:S(2)}) copy-start(s32[1,64]{1,0:T(1,128)} %param.5) | copy-start | bytes 772
  3.5 17.2 %collective-permute-start.4 = (bf16[64,1024]{1,0:T(8,128)(2,1)}, bf16[64,1024]{1,0:T(8,128)(2,1)S(1)}, u32[]{:S(2)}, u32[]{:S(2)}) collective-permute-start(bf16[64,1024]{1,0:T(8,128)(2,1)} %get-tuple-element.60), channel_id=1, source_target_pairs={{0,24},{2,26},{4,28},{6,30},{8,16},{10,18},{12,20},{14,22},{16,8},... | collective-permute-start | bytes 393224 | tf_op jit(solution)/shard_map/ppermute | solution.py:414
  8.7 13.7 %collective-permute-start.5 = (bf16[64,1024]{1,0:T(8,128)(2,1)}, bf16[64,1024]{1,0:T(8,128)(2,1)S(1)}, u32[]{:S(2)}, u32[]{:S(2)}) collective-permute-start(bf16[64,1024]{1,0:T(8,128)(2,1)} %get-tuple-element.61), channel_id=1, source_target_pairs={{0,2},{2,0},{4,6},{6,4},{8,10},{10,8},{12,14},{14,12},{16,18},{18,... | collective-permute-start | bytes 393224 | tf_op jit(solution)/shard_map/ppermute | solution.py:414
  10.2 13.5 %collective-permute-start.6 = (bf16[64,1024]{1,0:T(8,128)(2,1)}, bf16[64,1024]{1,0:T(8,128)(2,1)S(1)}, u32[]{:S(2)}, u32[]{:S(2)}) collective-permute-start(bf16[64,1024]{1,0:T(8,128)(2,1)} %get-tuple-element.62), channel_id=1, source_target_pairs={{0,28},{2,30},{4,24},{6,26},{8,20},{10,22},{12,16},{14,18},{16,12}... | collective-permute-start | bytes 393224 | tf_op jit(solution)/shard_map/ppermute | solution.py:414
  11.3 17.5 %collective-permute-start.7 = (bf16[64,1024]{1,0:T(8,128)(2,1)}, bf16[64,1024]{1,0:T(8,128)(2,1)S(1)}, u32[]{:S(2)}, u32[]{:S(2)}) collective-permute-start(bf16[64,1024]{1,0:T(8,128)(2,1)} %get-tuple-element.63), channel_id=1, source_target_pairs={{0,18},{2,16},{4,22},{6,20},{8,26},{10,24},{12,30},{14,28},{16,2},... | collective-permute-start | bytes 393224 | tf_op jit(solution)/shard_map/ppermute | solution.py:414
  17.3 15.1 %collective-permute-start.8 = (bf16[64,1024]{1,0:T(8,128)(2,1)}, bf16[64,1024]{1,0:T(8,128)(2,1)S(1)}, u32[]{:S(2)}, u32[]{:S(2)}) collective-permute-start(bf16[64,1024]{1,0:T(8,128)(2,1)} %get-tuple-element.64), channel_id=1, source_target_pairs={{0,8},{2,10},{4,12},{6,14},{8,0},{10,2},{12,4},{14,6},{16,24},{18,... | collective-permute-start | bytes 393224 | tf_op jit(solution)/shard_map/ppermute | solution.py:414
  20.7 15.1 %collective-permute-start.9 = (bf16[64,1024]{1,0:T(8,128)(2,1)}, bf16[64,1024]{1,0:T(8,128)(2,1)S(1)}, u32[]{:S(2)}, u32[]{:S(2)}) collective-permute-start(bf16[64,1024]{1,0:T(8,128)(2,1)} %get-tuple-element.65), channel_id=1, source_target_pairs={{0,10},{2,8},{4,14},{6,12},{8,2},{10,0},{12,6},{14,4},{16,26},{18,... | collective-permute-start | bytes 393224 | tf_op jit(solution)/shard_map/ppermute | solution.py:414
  22.4 13.4 %collective-permute-start.10 = (bf16[64,1024]{1,0:T(8,128)(2,1)}, bf16[64,1024]{1,0:T(8,128)(2,1)S(1)}, u32[]{:S(2)}, u32[]{:S(2)}) collective-permute-start(bf16[64,1024]{1,0:T(8,128)(2,1)} %get-tuple-element.66), channel_id=1, source_target_pairs={{0,20},{2,22},{4,16},{6,18},{8,28},{10,30},{12,24},{14,26},{16,4},... | collective-permute-start | bytes 393224 | tf_op jit(solution)/shard_map/ppermute | solution.py:414
  23.6 15.1 %collective-permute-start.11 = (bf16[64,1024]{1,0:T(8,128)(2,1)}, bf16[64,1024]{1,0:T(8,128)(2,1)S(1)}, u32[]{:S(2)}, u32[]{:S(2)}) collective-permute-start(bf16[64,1024]{1,0:T(8,128)(2,1)} %get-tuple-element.67), channel_id=1, source_target_pairs={{0,14},{2,12},{4,10},{6,8},{8,6},{10,4},{12,2},{14,0},{16,30},{18,... | collective-permute-start | bytes 393224 | tf_op jit(solution)/shard_map/ppermute | solution.py:414
  28.9 13.1 %collective-permute-start.12 = (bf16[64,1024]{1,0:T(8,128)(2,1)}, bf16[64,1024]{1,0:T(8,128)(2,1)S(1)}, u32[]{:S(2)}, u32[]{:S(2)}) collective-permute-start(bf16[64,1024]{1,0:T(8,128)(2,1)} %get-tuple-element.68), channel_id=1, source_target_pairs={{0,30},{2,28},{4,26},{6,24},{8,22},{10,20},{12,18},{14,16},{16,14}... | collective-permute-start | bytes 393224 | tf_op jit(solution)/shard_map/ppermute | solution.py:414
  32.4 13.8 %collective-permute-start.13 = (bf16[64,1024]{1,0:T(8,128)(2,1)}, bf16[64,1024]{1,0:T(8,128)(2,1)S(1)}, u32[]{:S(2)}, u32[]{:S(2)}) collective-permute-start(bf16[64,1024]{1,0:T(8,128)(2,1)} %get-tuple-element.69), channel_id=1, source_target_pairs={{0,4},{2,6},{4,0},{6,2},{8,12},{10,14},{12,8},{14,10},{16,20},{18,... | collective-permute-start | bytes 393224 | tf_op jit(solution)/shard_map/ppermute | solution.py:414
  35.8 11.1 %collective-permute-start.14 = (bf16[64,1024]{1,0:T(8,128)(2,1)}, bf16[64,1024]{1,0:T(8,128)(2,1)S(1)}, u32[]{:S(2)}, u32[]{:S(2)}) collective-permute-start(bf16[64,1024]{1,0:T(8,128)(2,1)} %get-tuple-element.70), channel_id=1, source_target_pairs={{0,22},{2,20},{4,18},{6,16},{8,30},{10,28},{12,26},{14,24},{16,6},... | collective-permute-start | bytes 393224 | tf_op jit(solution)/shard_map/ppermute | solution.py:414
  35.8 12.6 %collective-permute-start = (bf16[64,1024]{1,0:T(8,128)(2,1)}, bf16[64,1024]{1,0:T(8,128)(2,1)S(1)}, u32[]{:S(2)}, u32[]{:S(2)}) collective-permute-start(bf16[64,1024]{1,0:T(8,128)(2,1)} %get-tuple-element.55), channel_id=1, source_target_pairs={{0,12},{2,14},{4,8},{6,10},{8,4},{10,6},{12,0},{14,2},{16,28},{18,... | collective-permute-start | bytes 393224 | tf_op jit(solution)/shard_map/ppermute | solution.py:414
  38.7 9.6 %collective-permute-start.1 = (bf16[64,1024]{1,0:T(8,128)(2,1)}, bf16[64,1024]{1,0:T(8,128)(2,1)S(1)}, u32[]{:S(2)}, u32[]{:S(2)}) collective-permute-start(bf16[64,1024]{1,0:T(8,128)(2,1)} %get-tuple-element.56), channel_id=1, source_target_pairs={{0,26},{2,24},{4,30},{6,28},{8,18},{10,16},{12,22},{14,20},{16,10}... | collective-permute-start | bytes 393224 | tf_op jit(solution)/shard_map/ppermute | solution.py:414
  41.9 6.4 %collective-permute-start.2 = (bf16[64,1024]{1,0:T(8,128)(2,1)}, bf16[64,1024]{1,0:T(8,128)(2,1)S(1)}, u32[]{:S(2)}, u32[]{:S(2)}) collective-permute-start(bf16[64,1024]{1,0:T(8,128)(2,1)} %get-tuple-element.57), channel_id=1, source_target_pairs={{0,6},{2,4},{4,2},{6,0},{8,14},{10,12},{12,10},{14,8},{16,22},{18,... | collective-permute-start | bytes 393224 | tf_op jit(solution)/shard_map/ppermute | solution.py:414
  46.2 7.7 %collective-permute-start.3 = (bf16[64,1024]{1,0:T(8,128)(2,1)}, bf16[64,1024]{1,0:T(8,128)(2,1)S(1)}, u32[]{:S(2)}, u32[]{:S(2)}) collective-permute-start(bf16[64,1024]{1,0:T(8,128)(2,1)} %get-tuple-element.58), channel_id=1, source_target_pairs={{0,16},{2,18},{4,20},{6,22},{8,24},{10,26},{12,28},{14,30},{16,0},... | collective-permute-start | bytes 393224 | tf_op jit(solution)/shard_map/ppermute | solution.py:414
  46.9 0.9 %copy-start = (bf16[64,1024]{1,0:T(8,128)(2,1)S(1)}, bf16[64,1024]{1,0:T(8,128)(2,1)}, u32[]{:S(2)}) copy-start(bf16[64,1024]{1,0:T(8,128)(2,1)} %get-tuple-element.59.rest_0_.refs_0_) | copy-start | bytes 393220
  47.8 6.8 %copy-start.1 = (bf16[64,1024]{1,0:T(8,128)(2,1)S(1)}, bf16[64,1024]{1,0:T(8,128)(2,1)}, u32[]{:S(2)}) copy-start(bf16[64,1024]{1,0:T(8,128)(2,1)} %get-tuple-element.59.rest_0_.refs_0_) | copy-start | bytes 393220
  54.2 1.4 %collective-permute-start.15 = (bf16[4,128,128]{2,1,0:T(8,128)(2,1)S(1)}, bf16[4,128,128]{2,1,0:T(8,128)(2,1)S(1)}, u32[]{:S(2)}, u32[]{:S(2)}) collective-permute-start(bf16[4,128,128]{2,1,0:T(8,128)(2,1)S(1)} %pick_refs.3.own_ref), channel_id=1, source_target_pairs={{0,1},{1,0},{2,3},{3,2},{4,5},{5,4},{6,7},{7,6},{8,9},{9,8},{10,11... | collective-permute-start | bytes 393224 | tf_op jit(solution)/shard_map/ppermute | solution.py:418
